TPU v7x, 32 devices: a whole 2x2x4 slice. The times are simulated.
32 devices in a mesh: pole: 2 (over y), prow: 8 (over z, x), pcol: 2 (over core).
Axes of the slice: x: 2, y: 2, z: 4, core: 2. Of those that a mesh axis runs over, the one named last changes fastest.
Arguments:
- anc_inverse: bfloat16 [4, 8, 2, 48, 768], P('pole', None, 'pcol', None, 'prow'), parts along dimension 0, may hold values from -6 to 6
- panels: bfloat16 [6, 2, 768, 128], P('pole', None, ('prow', 'pcol')), parts along dimension 0, may hold values from -0.3125 to 0.3125
- diag_inverse: bfloat16 [6, 2, 128, 128], P('pole'), parts along dimension 0, may hold values from -3 to 3
- structure: int32 [3, 6], replicated, may hold values 0 or 1
Outputs:
- inverse_columns: bfloat16 [6, 2, 768, 128], P('pole', None, ('prow', 'pcol')), parts along dimension 0
- inverse_diag: float32 [6, 2, 128, 128], P('pole'), parts along dimension 0
There are 2 independent parts, one for each index of `pole`. A program takes and returns all parts, laid end to end along the dimension named above; an argument that names none is the same for every part. Nothing has to cross between parts.
All inputs are finite; a program needn't handle non-finite values.
Results may differ from a plain program's by a relative error of at most 0.0027.
Values may be sent and summed in bfloat16 or wider, within the bound.
No kernel may reach another device: no remote copies, remote signals or barrier semaphores. Data moves between devices by JAX's collectives and lax.ppermute only.
A program may use at most 64 MiB of HBM per device.

v0:
```python
import jax
import jax.numpy as jnp
from jax import lax
from jax.sharding import PartitionSpec as P


def contract_rows(left, right):
    return lax.dot_general(
        left, right, (((0,), (0,)), ((), ())), preferred_element_type=jnp.float32
    )


def complex_product(left, right):
    real_part = contract_rows(left[0], right[0]) - contract_rows(left[1], right[1])
    imag_part = contract_rows(left[0], right[1]) + contract_rows(left[1], right[0])
    return jnp.stack([real_part, imag_part])


def local(anc_inverse, panels, diag_inverse, structure):
    supernodes = panels.shape[0]
    rows_half = panels.shape[2]
    panel_width = panels.shape[3]
    groups = anc_inverse.shape[1]
    rows_dev = anc_inverse.shape[4]
    inverse_loc = anc_inverse.reshape(2, groups * rows_half, rows_dev)
    row_index = lax.axis_index("prow")
    col_index = lax.axis_index("pcol")
    blocks = structure.shape[1]
    block_range = jnp.arange(blocks, dtype=jnp.int32)
    struct_float = structure.astype(jnp.float32)
    local_rows = (
        row_index * rows_dev + col_index * rows_half + jnp.arange(rows_half, dtype=jnp.int32)
    )
    block_hits = (local_rows[:, None] // panel_width == block_range[None, :]).astype(jnp.float32)
    row_mask = jnp.dot(block_hits, struct_float.T, precision=lax.Precision.HIGHEST)
    columns_out = []
    diags = []
    for node in range(supernodes):
        keep = row_mask[:, node]
        masked = panels[node] * keep.astype(jnp.bfloat16)[None, :, None]
        partial_value = complex_product(
            inverse_loc, lax.all_gather(masked, "prow", axis=1, tiled=True)
        )
        summed = lax.psum_scatter(partial_value, "pcol", scatter_dimension=1, tiled=True)
        column = (-(summed * keep[None, :, None])).astype(jnp.bfloat16)
        columns_out.append(column)
        local_diag = complex_product(masked, column)
        diag_total = lax.psum(local_diag, ("prow", "pcol"))
        diags.append(diag_inverse[node].astype(jnp.float32) - diag_total)
    diag_out = jnp.stack(diags)
    return (jnp.stack(columns_out), diag_out)


def solution(mesh):
    in_specs = (
        P("pole", None, "pcol", None, "prow"),
        P("pole", None, ("prow", "pcol"), None),
        P("pole", None, None, None),
        P(),
    )
    out_specs = (P("pole", None, ("prow", "pcol"), None), P("pole", None, None, None))
    return jax.shard_map(local, mesh=mesh, in_specs=in_specs, out_specs=out_specs, check_vma=False)
```

profile of v0, /device:TPU:0, one launch (start us, length us, event | category | flops | bytes accessed | tf_op | source)
XLA Modules:
  0.0 221.3 jit_solution(12243957177769898919)
XLA Ops:
  7.2 0.0 reduce-scatter.8.cloned.1.call-start
  7.2 0.0 copy-start.5
  7.2 1.0 fusion.33
  8.2 0.0 copy-start.4
  8.2 0.0 copy-done.5
  8.2 0.2 fusion.21
  8.4 0.6 copy-done.4
  9.1 0.1 bitcast_multiply_fusion.2
  9.2 32.4 %all_gather.11 = bf16[2,384,128]{2,1,0:T(8,128)(2,1)S(1)} all-gather(bf16[2,48,128]{2,1,0:T(8,128)(2,1)S(1)} %get-tuple-element.11), channel_id=1, replica_groups=mesh['pole'=2,'prow'=8,'pcol'=2] {'prow'}, dimensions={1}, use_global_device_ids=true | all-gather | bytes 221184 | tf_op jit(solution)/shard_map/all_gather | solution.py:42
  41.6 0.2 fusion.20
  41.8 0.2 fusion.19
  42.0 0.2 fusion.6
  42.3 0.2 fusion.7
  42.5 0.7 pad_maximum_fusion.6
  43.1 0.0 reduce-scatter.8.cloned.1.call-update
  43.2 0.0 reduce-scatter.4.cloned.1.call-start
  43.2 30.6 %all_gather.9 = bf16[2,384,128]{2,1,0:T(8,128)(2,1)S(1)} all-gather(bf16[2,48,128]{2,1,0:T(8,128)(2,1)S(1)} %get-tuple-element.10), channel_id=1, replica_groups=mesh['pole'=2,'prow'=8,'pcol'=2] {'prow'}, dimensions={1}, use_global_device_ids=true | all-gather | bytes 221184 | tf_op jit(solution)/shard_map/all_gather | solution.py:42
  73.8 0.2 fusion.16
  74.1 0.2 fusion.15
  74.3 0.2 fusion.10
  74.5 0.2 fusion.11
  74.7 0.6 pad_maximum_fusion.4
  75.4 0.0 reduce-scatter.4.cloned.1.call-update
  75.4 0.0 reduce-scatter.6.cloned.1.call-start
  75.4 30.6 %all_gather.10 = bf16[2,384,128]{2,1,0:T(8,128)(2,1)S(1)} all-gather(bf16[2,48,128]{2,1,0:T(8,128)(2,1)S(1)} %get-tuple-element.12), channel_id=1, replica_groups=mesh['pole'=2,'prow'=8,'pcol'=2] {'prow'}, dimensions={1}, use_global_device_ids=true | all-gather | bytes 221184 | tf_op jit(solution)/shard_map/all_gather | solution.py:42
  106.1 0.2 fusion.18
  106.3 0.2 fusion.17
  106.5 0.2 fusion.8
  106.7 0.2 fusion.9
  107.0 0.7 pad_maximum_fusion.5
  107.6 0.0 reduce-scatter.6.cloned.1.call-update
  107.7 0.0 all-reduce.3.cloned.1.call-start
  107.7 0.0 reduce-scatter.8.cloned.1.call-done
  107.7 0.9 negate_convert_fusion
  108.6 0.2 fusion.27
  108.8 0.2 fusion.28
  109.0 0.0 reduce-scatter.4.cloned.1.call-done
  109.0 0.9 negate_convert_fusion.2
  109.9 0.2 fusion.23
  110.1 0.2 fusion.24
  110.3 6.1 %reduce-scatter.6.cloned.1.call-done = f32[2,48,128]{2,1,0:T(8,128)} async-done(((f32[2,96,128]{2,1,0:T(8,128)}), f32[2,48,128]{2,1,0:T(8,128)}) %reduce-scatter.6.cloned.1.call-update) | async-done | bytes 49168 | tf_op jit(solution)/shard_map/reduce_scatter | solution.py:44
  116.4 0.9 negate_convert_fusion.1
  117.2 0.2 fusion.25
  117.4 0.2 fusion.26
  117.6 0.2 fusion
  117.8 0.2 fusion.1
  118.0 0.2 fusion.4
  118.2 0.2 fusion.5
  118.4 0.2 fusion.2
  118.6 0.2 fusion.3
  118.8 0.7 pad_maximum_fusion.3
  119.4 0.7 pad_maximum_fusion.1
  120.2 0.0 all-reduce.3.cloned.1.call-update
  120.2 0.8 copy-done
  121.0 0.1 fusion.48
  121.0 0.7 copy-done.2
  121.8 0.1 fusion.47
  121.8 0.7 copy-done.1
  122.5 0.1 fusion.46
  122.6 0.6 pad_maximum_fusion.7
  123.3 89.7 %all-reduce.3.cloned.1.call-done = (f32[2,128,128]{2,1,0:T(8,128)}, f32[2,128,128]{2,1,0:T(8,128)}, f32[2,128,128]{2,1,0:T(8,128)}) async-done(((f32[2,128,128]{2,1,0:T(8,128)}, f32[2,128,128]{2,1,0:T(8,128)}, f32[2,128,128]{2,1,0:T(8,128)}), (f32[2,128,128]{2,1,0:T(8,128)}, f32[2,128,128]{2,1,0:T(8,128)}, f32[2,128,128]{2,1,0:T(8,128)})) %all-reduce.3.cloned.1.call-update) | async-done | bytes 393232 | tf_op jit(solution)/shard_map/psum | solution.py:48
  213.0 0.0 copy-done.3
  213.0 1.1 fusion.14
  214.0 0.8 pad_maximum_fusion
  (7 shorter events, 0.0 us)
Async XLA Ops:
  7.2 100.6 %reduce-scatter.8.cloned.1.call-start = ((), (), s32[]{:S(2)}) async-start(), calls=%async_computation.5 | async-start | bytes 147456 | tf_op jit(solution)/shard_map/reduce_scatter | solution.py:44
  7.2 1.0 copy-start.5
  8.2 0.9 copy-start.4
  43.2 65.9 %reduce-scatter.4.cloned.1.call-start = ((), (), s32[]{:S(2)}) async-start(), calls=%async_computation.3 | async-start | bytes 147456 | tf_op jit(solution)/shard_map/reduce_scatter | solution.py:44
  75.4 41.0 %reduce-scatter.6.cloned.1.call-start = ((), (), s32[]{:S(2)}) async-start(), calls=%async_computation.4 | async-start | bytes 147456 | tf_op jit(solution)/shard_map/reduce_scatter | solution.py:44
  107.7 105.3 %all-reduce.3.cloned.1.call-start = ((), (), s32[]{:S(2)}) async-start(), calls=%async_computation.6 | async-start | bytes 786432 | tf_op jit(solution)/shard_map/psum | solution.py:48
  120.2 0.8 copy-start
  121.0 0.8 copy-start.2
  121.8 0.8 copy-start.1
  121.8 91.2 %copy-start.3 = (bf16[3,2,128,128]{3,2,1,0:T(8,128)(2,1)S(1)}, bf16[3,2,128,128]{3,2,1,0:T(8,128)(2,1)}, u32[]{:S(2)}) copy-start(bf16[3,2,128,128]{3,2,1,0:T(8,128)(2,1)} %param.6) | copy-start | bytes 589828
Sparse Core Ops, SparseCore 0:
  43.3 8.4 reduce-scatter.7
  75.5 8.5 reduce-scatter.3
  107.8 8.5 reduce-scatter.5
  120.5 92.4 all-reduce.2
where the time goes:
time: 222 us; the launch traced here: 221 us
  waiting for transfers between devices  95.9 us (43%)
  blocking collectives  93.7 us (42%)
  between operations  13.9 us (6%)
  other arithmetic  8.78 us (4%)
  matrix products  5.08 us (2%)
  local copies, waits for them, and re-layouts  3.85 us (2%)
    all_gather x3, blocking collectives, local(): lax.all_gather(masked, 'prow', axis=1, tiled=True)  93.7 us
    psum x1, waiting for transfers between devices, local(): diag_total = lax.psum(local_diag, ('prow', 'pcol'))  89.7 us
    reduce_scatter x3, waiting for transfers between devices, local(): lax.psum_scatter(partial_value, 'pcol', scatter_dimension=1, tiled=True)  6.15 us
    dot_general x24, matrix products, contract_rows(): lax.dot_general(left, right, (((0,), (0,)), ((), ())), preferred_element_...  4.9 us
  transfers between devices with their start and end apart: 4, of which 2 were waited for; matrix products, arithmetic and copies ran while one was open for 3% of the time, Pallas kernels for 0%

commit v1 on v0

v1 whole, which is shorter than its diff:
```python
import jax
import jax.numpy as jnp
from jax import lax
from jax.sharding import PartitionSpec as P

AXES = ("prow", "pcol")


def swap(value, rows, cols, mask0, mask1):
    pairs = []
    for row in range(rows):
        for col in range(cols):
            mask = mask0 if col == 0 else mask1
            pairs.append((row * cols + col, (row ^ mask) * cols + col))
    return lax.ppermute(value, AXES, pairs)


def swap_core(value):
    return lax.ppermute(value, "pcol", [(0, 1), (1, 0)])


def gather(block, rows, cols, row_index, col_index):
    half = rows // 2
    here = row_index // 2
    held = jnp.zeros((half,) + block.shape, block.dtype)
    masks = [(2, 4), (4, 2), (6, 6)]
    arrived = [swap(block, rows, cols, m0, m1) for m0, m1 in masks]
    held = lax.dynamic_update_index_in_dim(held, block, here, 0)
    for (m0, m1), value in zip(masks, arrived):
        step = jnp.where(col_index == 0, m0, m1) // 2
        held = lax.dynamic_update_index_in_dim(held, value, here ^ step, 0)
    size = 8
    while size < rows:
        count = size // 2
        start = (here // count) * count
        own = lax.dynamic_slice_in_dim(held, start, count, 0)
        other = swap(own, rows, cols, size, size)
        held = lax.dynamic_update_slice_in_dim(held, other, start ^ count, 0)
        size *= 2
    return held, swap(held, rows, cols, 1, 1)


def contract(left, right):
    both = lax.dot_general(
        left, right, (((0, 2), (0, 3)), ((), ())), preferred_element_type=jnp.float32
    )
    real = both[0, :, :, 0] - both[1, :, :, 1]
    imag = both[0, :, :, 1] + both[1, :, :, 0]
    return jnp.stack([real, imag]).transpose(2, 0, 1, 3)


def contract_nodes(left, right):
    both = lax.dot_general(
        left, right, (((0, 3), (0, 3)), ((1,), (1,))), preferred_element_type=jnp.float32
    )
    real = both[:, 0, :, 0] - both[:, 1, :, 1]
    imag = both[:, 0, :, 1] + both[:, 1, :, 0]
    return jnp.stack([real, imag], axis=1)


def solution(mesh):
    rows, cols = mesh.shape["prow"], mesh.shape["pcol"]

    def local(anc_inverse, panels, diag_inverse, structure):
        supernodes, _, rows_half, width = panels.shape
        groups = anc_inverse.shape[1]
        rows_dev = anc_inverse.shape[4]
        row_index = lax.axis_index("prow")
        col_index = lax.axis_index("pcol")
        blocks = structure.shape[1]
        local_rows = (
            row_index * rows_dev + col_index * rows_half + jnp.arange(rows_half, dtype=jnp.int32)
        )
        hits = local_rows[:, None] // width == jnp.arange(blocks, dtype=jnp.int32)[None, :]
        keep = jnp.sum(jnp.where(hits[None], structure[:, None, :], 0), axis=2)
        masked = panels * keep.astype(jnp.bfloat16)[:, None, :, None]

        matrix = anc_inverse.reshape(2, groups // 2, 2, rows_half, rows_dev)
        parity = row_index % 2
        own = lax.dynamic_index_in_dim(matrix, parity, 2, False).swapaxes(0, 1)
        far = lax.dynamic_index_in_dim(matrix, 1 - parity, 2, False).swapaxes(0, 1)

        m_own, m_far = gather(masked, rows, cols, row_index, col_index)
        partial = contract(own, m_own) + contract(far, m_far)
        halves = partial.reshape(supernodes, 2, cols, rows_half, width)
        mine = lax.dynamic_index_in_dim(halves, col_index, 2, False)
        theirs = lax.dynamic_index_in_dim(halves, 1 - col_index, 2, False)
        product = mine + swap_core(theirs)
        column = (-(product * keep.astype(jnp.float32)[:, None, :, None])).astype(jnp.bfloat16)

        c_own, c_far = gather(column, rows, cols, row_index, col_index)
        diag = contract_nodes(m_own, c_own) + contract_nodes(m_far, c_far)
        diag = diag + swap_core(diag)
        return column, diag_inverse.astype(jnp.float32) - diag

    in_specs = (
        P("pole", None, "pcol", None, "prow"),
        P("pole", None, ("prow", "pcol"), None),
        P("pole", None, None, None),
        P(),
    )
    out_specs = (P("pole", None, ("prow", "pcol"), None), P("pole", None, None, None))
    return jax.shard_map(local, mesh=mesh, in_specs=in_specs, out_specs=out_specs, check_vma=False)
```

time: 222 us -> 43.7 us (0.20)
  blocking collectives: 93.7 us -> 0 us
  waiting for transfers between devices: 95.9 us -> 25 us
  starting transfers between devices: 0.16 us -> 13.4 us
  between operations: 13.9 us -> 0.87 us
  other arithmetic: 8.78 us -> 0.65 us
  matrix products: 5.08 us -> 1.15 us
    all_gather x3 -> x0, blocking collectives: 93.7 us -> none  [local(): lax.all_gather(masked, 'prow', axis=1, tiled=True)]
    psum x1 -> x0, waiting for transfers between devices: 89.7 us -> none  [local(): diag_total = lax.psum(local_diag, ('prow', 'pcol'))]
    ppermute x0 -> x10, waiting for transfers between devices: none -> 25 us  [the longest x8 21.9 us: swap(): return lax.ppermute(value, AXES, pairs)]
    ppermute x0 -> x10, starting transfers between devices: none -> 13.4 us  [the longest x8 13.2 us: swap(): return lax.ppermute(value, AXES, pairs)]
    reduce_scatter x3 -> x0, waiting for transfers between devices: 6.15 us -> none  [local(): lax.psum_scatter(partial_value, 'pcol', scatter_dimension=1, tiled=True)]
    another operation x11 -> x0, other arithmetic: 6.06 us -> none  [the longest x5 3.35 us: complex_product(): return jnp.stack([real_part, imag_part])]
    dot_general x25 -> x4, matrix products: 5.08 us -> 1.15 us  [the longest x2 0.62 us: contract_nodes(): lax.dot_general(left, right, (((0, 3), (0, 3)), ((1,), (1,))), preferred_...]
    convert_element_type x3 -> x1, other arithmetic: 2.62 us -> 0.01 us  [local(): masked = panels * keep.astype(jnp.bfloat16)[:, None, :, None]]
  transfers between devices with their start and end apart: 4 -> 10, of which waited for: 2 -> 10; matrix products, arithmetic and copies ran while one was open for 3% -> 2% of each run, Pallas kernels for 0% -> 0%
where the time goes in v1:
time: 43.7 us; the launch traced here: 43.6 us
  waiting for transfers between devices  25 us (57%)
  starting transfers between devices  13.4 us (31%)
  local copies, waits for them, and re-layouts  2.52 us (6%)
  matrix products  1.15 us (3%)
  between operations  0.87 us (2%)
  other arithmetic  0.65 us (1%)
    ppermute x8, waiting for transfers between devices, swap(): return lax.ppermute(value, AXES, pairs)  21.9 us
    ppermute x8, starting transfers between devices, swap(): return lax.ppermute(value, AXES, pairs)  13.2 us
    ppermute x2, waiting for transfers between devices, swap_core(): return lax.ppermute(value, 'pcol', [(0, 1), (1, 0)])  3.07 us
    unnamed x11, local copies, waits for them, and re-layouts  2.31 us
  transfers between devices with their start and end apart: 10, of which 10 were waited for; matrix products, arithmetic and copies ran while one was open for 2% of the time, Pallas kernels for 0%

profile of v1, /device:TPU:0, one launch (start us, length us, event | category | flops | bytes accessed | tf_op | source)
XLA Modules:
  0.0 43.6 jit_solution(14162197671335948381)
XLA Ops:
  0.6 0.0 copy-start
  0.7 0.0 copy-start.4
  0.7 0.7 %copy-done.4 = s32[3,6]{1,0:T(4,128)S(1)} copy-done((s32[3,6]{1,0:T(4,128)S(1)}, s32[3,6]{1,0:T(4,128)}, u32[]{:S(2)}) %copy-start.4) | copy-done | bytes 96
  1.4 0.1 select_reduce_fusion
  1.5 0.0 copy-start.2
  1.5 0.8 %copy-done.2 = bf16[3,2,48,128]{3,2,1,0:T(8,128)(2,1)S(1)} copy-done((bf16[3,2,48,128]{3,2,1,0:T(8,128)(2,1)S(1)}, bf16[3,2,48,128]{3,2,1,0:T(8,128)(2,1)}, u32[]{:S(2)}) %copy-start.2) | copy-done | bytes 73752
  2.4 0.1 bitcast_dynamic-update-slice_fusion.5
  2.5 3.1 %collective-permute-start = (bf16[3,2,48,128]{3,2,1,0:T(8,128)(2,1)S(1)}, bf16[3,2,48,128]{3,2,1,0:T(8,128)(2,1)S(1)}, u32[]{:S(2)}, u32[]{:S(2)}) collective-permute-start(bf16[3,2,48,128]{3,2,1,0:T(8,128)(2,1)S(1)} %get-tuple-element.9), channel_id=1, source_target_pairs={{0,4},{1,9},{2,6},{3,11},{4,0},{5,13},{6,2},{7,15},{8,12},{9,1},{1... | collective-permute-start | bytes 221192 | tf_op jit(solution)/shard_map/ppermute | solution.py:15
  5.6 2.6 %collective-permute-start.1 = (bf16[3,2,48,128]{3,2,1,0:T(8,128)(2,1)S(1)}, bf16[3,2,48,128]{3,2,1,0:T(8,128)(2,1)S(1)}, u32[]{:S(2)}, u32[]{:S(2)}) collective-permute-start(bf16[3,2,48,128]{3,2,1,0:T(8,128)(2,1)S(1)} %get-tuple-element.9), channel_id=1, source_target_pairs={{0,8},{1,5},{2,10},{3,7},{4,12},{5,1},{6,14},{7,3},{8,0},{9,13},{1... | collective-permute-start | bytes 221192 | tf_op jit(solution)/shard_map/ppermute | solution.py:15
  8.2 0.0 collective-permute-start.2
  8.2 0.5 %collective-permute-done = bf16[3,2,48,128]{3,2,1,0:T(8,128)(2,1)S(1)} collective-permute-done((bf16[3,2,48,128]{3,2,1,0:T(8,128)(2,1)S(1)}, bf16[3,2,48,128]{3,2,1,0:T(8,128)(2,1)S(1)}, u32[]{:S(2)}, u32[]{:S(2)}) %collective-permute-start) | collective-permute-done | bytes 73760 | tf_op jit(solution)/shard_map/ppermute | solution.py:15
  8.7 4.4 %collective-permute-done.1 = bf16[3,2,48,128]{3,2,1,0:T(8,128)(2,1)S(1)} collective-permute-done((bf16[3,2,48,128]{3,2,1,0:T(8,128)(2,1)S(1)}, bf16[3,2,48,128]{3,2,1,0:T(8,128)(2,1)S(1)}, u32[]{:S(2)}, u32[]{:S(2)}) %collective-permute-start.1) | collective-permute-done | bytes 73760 | tf_op jit(solution)/shard_map/ppermute | solution.py:15
  13.1 1.3 %collective-permute-done.2 = bf16[3,2,48,128]{3,2,1,0:T(8,128)(2,1)S(1)} collective-permute-done((bf16[3,2,48,128]{3,2,1,0:T(8,128)(2,1)S(1)}, bf16[3,2,48,128]{3,2,1,0:T(8,128)(2,1)S(1)}, u32[]{:S(2)}, u32[]{:S(2)}) %collective-permute-start.2) | collective-permute-done | bytes 73760 | tf_op jit(solution)/shard_map/ppermute | solution.py:15
  14.4 1.6 %collective-permute-start.3 = (bf16[4,3,2,48,128]{4,3,0,2,1:T(8,128)(2,1)S(1)}, bf16[4,3,2,48,128]{4,3,0,2,1:T(8,128)(2,1)S(1)}, u32[]{:S(2)}, u32[]{:S(2)}) collective-permute-start(bf16[4,3,2,48,128]{4,3,0,2,1:T(8,128)(2,1)S(1)} %bitcast_dynamic-update-slice_fusion.7), channel_id=1, source_target_pairs={{0,2},{1,3},{2,0},{3,1},{4,6},{5,7},{6,4},{7,5},{8,10},{9,11},{10,... | collective-permute-start | bytes 884744 | tf_op jit(solution)/shard_map/ppermute | solution.py:15
  16.0 0.0 copy-done
  16.0 0.3 convolution_bitcast_fusion.3
  16.3 5.1 %collective-permute-done.3 = bf16[4,3,2,48,128]{4,3,0,2,1:T(8,128)(2,1)S(1)} collective-permute-done((bf16[4,3,2,48,128]{4,3,0,2,1:T(8,128)(2,1)S(1)}, bf16[4,3,2,48,128]{4,3,0,2,1:T(8,128)(2,1)S(1)}, u32[]{:S(2)}, u32[]{:S(2)}) %collective-permute-start.3) | collective-permute-done | bytes 294944 | tf_op jit(solution)/shard_map/ppermute | solution.py:15
  21.4 0.3 convolution_bitcast_fusion.2
  21.9 0.1 collective-permute-start.4
  21.9 1.4 %collective-permute-done.4 = f32[3,2,48,128]{3,2,1,0:T(8,128)S(1)} collective-permute-done((f32[3,2,48,128]{3,2,1,0:T(8,128)S(1)}, f32[3,2,48,128]{3,2,1,0:T(8,128)S(1)}, u32[]{:S(2)}, u32[]{:S(2)}) %collective-permute-start.4) | collective-permute-done | bytes 147488 | tf_op jit(solution)/shard_map/ppermute | solution.py:19
  23.3 0.1 bitcast_dynamic-update-slice_fusion.2
  23.5 0.0 copy-start.3
  23.5 1.0 %collective-permute-start.5 = (bf16[3,2,48,128]{3,2,1,0:T(8,128)(2,1)S(1)}, bf16[3,2,48,128]{3,2,1,0:T(8,128)(2,1)S(1)}, u32[]{:S(2)}, u32[]{:S(2)}) collective-permute-start(bf16[3,2,48,128]{3,2,1,0:T(8,128)(2,1)S(1)} %get-tuple-element.7), channel_id=1, source_target_pairs={{0,4},{1,9},{2,6},{3,11},{4,0},{5,13},{6,2},{7,15},{8,12},{9,1},{1... | collective-permute-start | bytes 221192 | tf_op jit(solution)/shard_map/ppermute | solution.py:15
  24.4 1.8 %collective-permute-start.6 = (bf16[3,2,48,128]{3,2,1,0:T(8,128)(2,1)S(1)}, bf16[3,2,48,128]{3,2,1,0:T(8,128)(2,1)S(1)}, u32[]{:S(2)}, u32[]{:S(2)}) collective-permute-start(bf16[3,2,48,128]{3,2,1,0:T(8,128)(2,1)S(1)} %get-tuple-element.7), channel_id=1, source_target_pairs={{0,8},{1,5},{2,10},{3,7},{4,12},{5,1},{6,14},{7,3},{8,0},{9,13},{1... | collective-permute-start | bytes 221192 | tf_op jit(solution)/shard_map/ppermute | solution.py:15
  26.2 1.7 %collective-permute-start.7 = (bf16[3,2,48,128]{3,2,1,0:T(8,128)(2,1)S(1)}, bf16[3,2,48,128]{3,2,1,0:T(8,128)(2,1)S(1)}, u32[]{:S(2)}, u32[]{:S(2)}) collective-permute-start(bf16[3,2,48,128]{3,2,1,0:T(8,128)(2,1)S(1)} %get-tuple-element.7), channel_id=1, source_target_pairs={{0,12},{1,13},{2,14},{3,15},{4,8},{5,9},{6,10},{7,11},{8,4},{9,5},... | collective-permute-start | bytes 221192 | tf_op jit(solution)/shard_map/ppermute | solution.py:15
  27.9 0.4 collective-permute-done.5
  28.3 0.0 copy-done.3
  28.3 1.4 %collective-permute-done.6 = bf16[3,2,48,128]{3,2,1,0:T(8,128)(2,1)S(1)} collective-permute-done((bf16[3,2,48,128]{3,2,1,0:T(8,128)(2,1)S(1)}, bf16[3,2,48,128]{3,2,1,0:T(8,128)(2,1)S(1)}, u32[]{:S(2)}, u32[]{:S(2)}) %collective-permute-start.6) | collective-permute-done | bytes 73760 | tf_op jit(solution)/shard_map/ppermute | solution.py:15
  29.8 2.7 %collective-permute-done.7 = bf16[3,2,48,128]{3,2,1,0:T(8,128)(2,1)S(1)} collective-permute-done((bf16[3,2,48,128]{3,2,1,0:T(8,128)(2,1)S(1)}, bf16[3,2,48,128]{3,2,1,0:T(8,128)(2,1)S(1)}, u32[]{:S(2)}, u32[]{:S(2)}) %collective-permute-start.7) | collective-permute-done | bytes 73760 | tf_op jit(solution)/shard_map/ppermute | solution.py:15
  32.5 1.6 %collective-permute-start.8 = (bf16[4,3,2,48,128]{4,3,0,2,1:T(8,128)(2,1)S(1)}, bf16[4,3,2,48,128]{4,3,0,2,1:T(8,128)(2,1)S(1)}, u32[]{:S(2)}, u32[]{:S(2)}) collective-permute-start(bf16[4,3,2,48,128]{4,3,0,2,1:T(8,128)(2,1)S(1)} %bitcast_dynamic-update-slice_fusion.6), channel_id=1, source_target_pairs={{0,2},{1,3},{2,0},{3,1},{4,6},{5,7},{6,4},{7,5},{8,10},{9,11},{10,... | collective-permute-start | bytes 884744 | tf_op jit(solution)/shard_map/ppermute | solution.py:15
  34.1 0.3 convolution_bitcast_fusion.1
  34.4 6.1 %collective-permute-done.8 = bf16[4,3,2,48,128]{4,3,0,2,1:T(8,128)(2,1)S(1)} collective-permute-done((bf16[4,3,2,48,128]{4,3,0,2,1:T(8,128)(2,1)S(1)}, bf16[4,3,2,48,128]{4,3,0,2,1:T(8,128)(2,1)S(1)}, u32[]{:S(2)}, u32[]{:S(2)}) %collective-permute-start.8) | collective-permute-done | bytes 294944 | tf_op jit(solution)/shard_map/ppermute | solution.py:15
  40.5 0.3 convolution_bitcast_fusion
  40.9 0.0 copy-start.1
  40.9 0.1 collective-permute-start.9
  41.0 1.7 %collective-permute-done.9 = f32[3,2,128,128]{3,2,0,1:T(8,128)S(1)} collective-permute-done((f32[3,2,128,128]{3,2,0,1:T(8,128)S(1)}, f32[3,2,128,128]{3,2,0,1:T(8,128)S(1)}, u32[]{:S(2)}, u32[]{:S(2)}) %collective-permute-start.9) | collective-permute-done | bytes 393248 | tf_op jit(solution)/shard_map/ppermute | solution.py:19
  42.7 0.0 copy-done.1
  42.7 0.1 add_subtract_fusion
  42.8 0.8 %copy.53 = f32[3,2,128,128]{3,2,1,0:T(8,128)} copy(f32[3,2,128,128]{3,2,0,1:T(8,128)S(1)} %add_subtract_fusion) | data formatting | bytes 786432
  (21 shorter events, 0.5 us)
Async XLA Ops:
  0.6 15.4 %copy-start = (bf16[2,8,1,48,96]{4,3,2,1,0:T(8,128)(2,1)S(1)}, bf16[2,8,1,48,96]{4,3,2,1,0:T(8,128)(2,1)}, u32[]{:S(2)}) copy-start(bf16[2,8,1,48,96]{4,3,2,1,0:T(8,128)(2,1)} %param.4) | copy-start | bytes 442372
  0.7 0.7 %copy-start.4 = (s32[3,6]{1,0:T(4,128)S(1)}, s32[3,6]{1,0:T(4,128)}, u32[]{:S(2)}) copy-start(s32[3,6]{1,0:T(4,128)} %param.7) | copy-start | bytes 220
  1.5 0.9 %copy-start.2 = (bf16[3,2,48,128]{3,2,1,0:T(8,128)(2,1)S(1)}, bf16[3,2,48,128]{3,2,1,0:T(8,128)(2,1)}, u32[]{:S(2)}) copy-start(bf16[3,2,48,128]{3,2,1,0:T(8,128)(2,1)} %param.5) | copy-start | bytes 221188
  2.5 6.2 %collective-permute-start = (bf16[3,2,48,128]{3,2,1,0:T(8,128)(2,1)S(1)}, bf16[3,2,48,128]{3,2,1,0:T(8,128)(2,1)S(1)}, u32[]{:S(2)}, u32[]{:S(2)}) collective-permute-start(bf16[3,2,48,128]{3,2,1,0:T(8,128)(2,1)S(1)} %get-tuple-element.9), channel_id=1, source_target_pairs={{0,4},{1,9},{2,6},{3,11},{4,0},{5,13},{6,2},{7,15},{8,12},{9,1},{1... | collective-permute-start | bytes 221192 | tf_op jit(solution)/shard_map/ppermute | solution.py:15
  5.6 7.5 %collective-permute-start.1 = (bf16[3,2,48,128]{3,2,1,0:T(8,128)(2,1)S(1)}, bf16[3,2,48,128]{3,2,1,0:T(8,128)(2,1)S(1)}, u32[]{:S(2)}, u32[]{:S(2)}) collective-permute-start(bf16[3,2,48,128]{3,2,1,0:T(8,128)(2,1)S(1)} %get-tuple-element.9), channel_id=1, source_target_pairs={{0,8},{1,5},{2,10},{3,7},{4,12},{5,1},{6,14},{7,3},{8,0},{9,13},{1... | collective-permute-start | bytes 221192 | tf_op jit(solution)/shard_map/ppermute | solution.py:15
  8.2 6.3 %collective-permute-start.2 = (bf16[3,2,48,128]{3,2,1,0:T(8,128)(2,1)S(1)}, bf16[3,2,48,128]{3,2,1,0:T(8,128)(2,1)S(1)}, u32[]{:S(2)}, u32[]{:S(2)}) collective-permute-start(bf16[3,2,48,128]{3,2,1,0:T(8,128)(2,1)S(1)} %get-tuple-element.9), channel_id=1, source_target_pairs={{0,12},{1,13},{2,14},{3,15},{4,8},{5,9},{6,10},{7,11},{8,4},{9,5},... | collective-permute-start | bytes 221192 | tf_op jit(solution)/shard_map/ppermute | solution.py:15
  14.4 7.0 %collective-permute-start.3 = (bf16[4,3,2,48,128]{4,3,0,2,1:T(8,128)(2,1)S(1)}, bf16[4,3,2,48,128]{4,3,0,2,1:T(8,128)(2,1)S(1)}, u32[]{:S(2)}, u32[]{:S(2)}) collective-permute-start(bf16[4,3,2,48,128]{4,3,0,2,1:T(8,128)(2,1)S(1)} %bitcast_dynamic-update-slice_fusion.7), channel_id=1, source_target_pairs={{0,2},{1,3},{2,0},{3,1},{4,6},{5,7},{6,4},{7,5},{8,10},{9,11},{10,... | collective-permute-start | bytes 884744 | tf_op jit(solution)/shard_map/ppermute | solution.py:15
  21.9 1.4 %collective-permute-start.4 = (f32[3,2,48,128]{3,2,1,0:T(8,128)S(1)}, f32[3,2,48,128]{3,2,1,0:T(8,128)S(1)}, u32[]{:S(2)}, u32[]{:S(2)}) collective-permute-start(f32[3,2,48,128]{3,2,1,0:T(8,128)S(1)} %bitcast.146), channel_id=1, source_target_pairs={{0,1},{1,0},{2,3},{3,2},{4,5},{5,4},{6,7},{7,6},{8,9},{9,8},{10,11... | collective-permute-start | bytes 442376 | tf_op jit(solution)/shard_map/ppermute | solution.py:19
  23.5 4.9 %copy-start.3 = (bf16[3,2,48,128]{3,2,1,0:T(8,128)(2,1)}, bf16[3,2,48,128]{3,2,1,0:T(8,128)(2,1)S(1)}, u32[]{:S(2)}) copy-start(bf16[3,2,48,128]{3,2,1,0:T(8,128)(2,1)S(1)} %get-tuple-element.7) | copy-start | bytes 221188
  23.5 4.9 %collective-permute-start.5 = (bf16[3,2,48,128]{3,2,1,0:T(8,128)(2,1)S(1)}, bf16[3,2,48,128]{3,2,1,0:T(8,128)(2,1)S(1)}, u32[]{:S(2)}, u32[]{:S(2)}) collective-permute-start(bf16[3,2,48,128]{3,2,1,0:T(8,128)(2,1)S(1)} %get-tuple-element.7), channel_id=1, source_target_pairs={{0,4},{1,9},{2,6},{3,11},{4,0},{5,13},{6,2},{7,15},{8,12},{9,1},{1... | collective-permute-start | bytes 221192 | tf_op jit(solution)/shard_map/ppermute | solution.py:15
  24.4 5.3 %collective-permute-start.6 = (bf16[3,2,48,128]{3,2,1,0:T(8,128)(2,1)S(1)}, bf16[3,2,48,128]{3,2,1,0:T(8,128)(2,1)S(1)}, u32[]{:S(2)}, u32[]{:S(2)}) collective-permute-start(bf16[3,2,48,128]{3,2,1,0:T(8,128)(2,1)S(1)} %get-tuple-element.7), channel_id=1, source_target_pairs={{0,8},{1,5},{2,10},{3,7},{4,12},{5,1},{6,14},{7,3},{8,0},{9,13},{1... | collective-permute-start | bytes 221192 | tf_op jit(solution)/shard_map/ppermute | solution.py:15
  26.2 6.2 %collective-permute-start.7 = (bf16[3,2,48,128]{3,2,1,0:T(8,128)(2,1)S(1)}, bf16[3,2,48,128]{3,2,1,0:T(8,128)(2,1)S(1)}, u32[]{:S(2)}, u32[]{:S(2)}) collective-permute-start(bf16[3,2,48,128]{3,2,1,0:T(8,128)(2,1)S(1)} %get-tuple-element.7), channel_id=1, source_target_pairs={{0,12},{1,13},{2,14},{3,15},{4,8},{5,9},{6,10},{7,11},{8,4},{9,5},... | collective-permute-start | bytes 221192 | tf_op jit(solution)/shard_map/ppermute | solution.py:15
  32.5 8.0 %collective-permute-start.8 = (bf16[4,3,2,48,128]{4,3,0,2,1:T(8,128)(2,1)S(1)}, bf16[4,3,2,48,128]{4,3,0,2,1:T(8,128)(2,1)S(1)}, u32[]{:S(2)}, u32[]{:S(2)}) collective-permute-start(bf16[4,3,2,48,128]{4,3,0,2,1:T(8,128)(2,1)S(1)} %bitcast_dynamic-update-slice_fusion.6), channel_id=1, source_target_pairs={{0,2},{1,3},{2,0},{3,1},{4,6},{5,7},{6,4},{7,5},{8,10},{9,11},{10,... | collective-permute-start | bytes 884744 | tf_op jit(solution)/shard_map/ppermute | solution.py:15
  40.9 1.9 %copy-start.1 = (bf16[3,2,128,128]{3,2,1,0:T(8,128)(2,1)S(1)}, bf16[3,2,128,128]{3,2,1,0:T(8,128)(2,1)}, u32[]{:S(2)}) copy-start(bf16[3,2,128,128]{3,2,1,0:T(8,128)(2,1)} %param.6) | copy-start | bytes 589828
  40.9 1.8 %collective-permute-start.9 = (f32[3,2,128,128]{3,2,0,1:T(8,128)S(1)}, f32[3,2,128,128]{3,2,0,1:T(8,128)S(1)}, u32[]{:S(2)}, u32[]{:S(2)}) collective-permute-start(f32[3,2,128,128]{3,2,0,1:T(8,128)S(1)} %maximum_add_fusion), channel_id=1, source_target_pairs={{0,1},{1,0},{2,3},{3,2},{4,5},{5,4},{6,7},{7,6},{8,9},{9,8},{10,11... | collective-permute-start | bytes 1179656 | tf_op jit(solution)/shard_map/ppermute | solution.py:19

commit v2 on v1

v2 whole, which is shorter than its diff:
```python
import jax
import jax.numpy as jnp
from jax import lax
from jax.sharding import PartitionSpec as P

AXES = ("prow", "pcol")
MASKS = ((2, 4), (4, 2), (6, 6))


def swap(value, rows, cols, mask0, mask1):
    pairs = []
    for row in range(rows):
        for col in range(cols):
            mask = mask0 if col == 0 else mask1
            pairs.append((row * cols + col, (row ^ mask) * cols + col))
    return lax.ppermute(value, AXES, pairs)


def swap_core(value):
    return lax.ppermute(value, "pcol", [(0, 1), (1, 0)])


def gather(block, rows, cols, here, col_index):
    held = jnp.zeros((rows // 2,) + block.shape, block.dtype)
    held = lax.dynamic_update_index_in_dim(held, block, here, 0)
    for mask0, mask1 in MASKS:
        value = swap(block, rows, cols, mask0, mask1)
        step = jnp.where(col_index == 0, mask0, mask1) // 2
        held = lax.dynamic_update_index_in_dim(held, value, here ^ step, 0)
    size = 8
    while size < rows:
        count = size // 2
        start = (here // count) * count
        own = lax.dynamic_slice_in_dim(held, start, count, 0)
        other = swap(own, rows, cols, size, size)
        held = lax.dynamic_update_slice_in_dim(held, other, start ^ count, 0)
        size *= 2
    return held


def total(block, rows, cols):
    sent = block.astype(jnp.bfloat16)
    first, second, third = [
        swap(sent, rows, cols, mask0, mask1).astype(jnp.float32) for mask0, mask1 in MASKS
    ]
    result = (sent.astype(jnp.float32) + first) + (second + third)
    size = 8
    while size < rows:
        result = result + swap(result, rows, cols, size, size)
        size *= 2
    return result


def pack(value, side, half):
    part = lax.dynamic_slice_in_dim(value, side * half, half, value.ndim - 1)
    return jnp.concatenate([part[..., 0, :, :], part[..., 1, :, :]], axis=-1)


def turned(value, half):
    return jnp.concatenate([-value[..., half:], value[..., :half]], axis=-1)


def solution(mesh):
    rows, cols = mesh.shape["prow"], mesh.shape["pcol"]

    def local(anc_inverse, panels, diag_inverse, structure):
        supernodes, _, rows_half, width = panels.shape
        half = width // 2
        groups = anc_inverse.shape[1]
        rows_dev = anc_inverse.shape[4]
        row_index = lax.axis_index("prow")
        col_index = lax.axis_index("pcol")
        here, parity = row_index // 2, row_index % 2
        blocks = structure.shape[1]

        panels_far = swap(panels, rows, cols, 1, 1)
        matrix_far = swap(anc_inverse, rows, cols, 1, 1)

        def keep_of(row):
            local_rows = row * rows_dev + col_index * rows_half + jnp.arange(rows_half, dtype=jnp.int32)
            hits = local_rows[:, None] // width == jnp.arange(blocks, dtype=jnp.int32)[None, :]
            return jnp.sum(jnp.where(hits[None], structure[:, None, :], 0), axis=2)

        keep = jnp.stack([keep_of(row_index), keep_of(row_index ^ 1)])
        masked = jnp.stack([panels, panels_far]) * keep.astype(jnp.bfloat16)[:, :, None, :, None]

        block = pack(masked, parity, half)
        held = gather(block, rows, cols, here, col_index)

        def ordered(matrix):
            cut = matrix.reshape(2, groups // 2, 2, rows_half, rows_dev).transpose(1, 2, 0, 3, 4)
            return jnp.where(parity == 0, cut, cut[:, ::-1])

        left = jnp.stack([ordered(anc_inverse), ordered(matrix_far)], axis=4)
        right = jnp.stack([held, turned(held, half)], axis=2)
        partial = lax.dot_general(
            left, right, (((0, 1, 2, 3), (0, 1, 2, 4)), ((), ())), preferred_element_type=jnp.float32
        )
        halves = partial.reshape(2, cols, rows_half, supernodes, 2 * half)
        mine = lax.dynamic_index_in_dim(halves, col_index, 1, False)
        theirs = lax.dynamic_index_in_dim(halves, 1 - col_index, 1, False)
        product = mine + swap_core(theirs)
        keep_float = keep.astype(jnp.float32).transpose(0, 2, 1)[..., None]
        column = (-(product * keep_float)).astype(jnp.bfloat16)

        left = masked.transpose(0, 2, 3, 1, 4)
        right = jnp.stack([column, turned(column, half)], axis=1)
        diag = lax.dot_general(
            left, right, (((0, 1, 2), (0, 1, 2)), ((3,), (3,))), preferred_element_type=jnp.float32
        )
        cut = diag.reshape(supernodes, cols, width // cols, 2 * half)
        mine = lax.dynamic_index_in_dim(cut, col_index, 1, False)
        theirs = lax.dynamic_index_in_dim(cut, 1 - col_index, 1, False)
        mine = mine + swap_core(theirs)
        mine = total(mine, rows, cols)

        def whole(near, far, axis):
            low = jnp.where(parity == 0, near, far)
            high = jnp.where(parity == 0, far, near)
            real = jnp.concatenate([low[..., :half], high[..., :half]], axis=-1)
            imag = jnp.concatenate([low[..., half:], high[..., half:]], axis=-1)
            return jnp.stack([real, imag], axis=axis)

        diag_half = whole(mine, swap(mine, rows, cols, 1, 1), 1)
        other = swap_core(diag_half)
        low = jnp.where(col_index == 0, diag_half, other)
        high = jnp.where(col_index == 0, other, diag_half)
        diag = jnp.concatenate([low, high], axis=2)

        column_far = swap(column[1], rows, cols, 1, 1)
        columns = whole(column[0], column_far, 0).transpose(2, 0, 1, 3)
        return columns, diag_inverse.astype(jnp.float32) - diag

    in_specs = (
        P("pole", None, "pcol", None, "prow"),
        P("pole", None, ("prow", "pcol"), None),
        P("pole", None, None, None),
        P(),
    )
    out_specs = (P("pole", None, ("prow", "pcol"), None), P("pole", None, None, None))
    return jax.shard_map(local, mesh=mesh, in_specs=in_specs, out_specs=out_specs, check_vma=False)
```

time: 43.7 us -> 40.9 us (0.936)
  waiting for transfers between devices: 25 us -> 18.1 us
  other arithmetic: 0.65 us -> 3 us
  starting transfers between devices: 13.4 us -> 15.6 us
  matrix products: 1.15 us -> 0.62 us
    ppermute x8 -> x10, waiting for transfers between devices: 21.9 us -> 16 us  [swap(): return lax.ppermute(value, AXES, pairs)]
    ppermute x8 -> x10, starting transfers between devices: 13.2 us -> 15.4 us  [swap(): return lax.ppermute(value, AXES, pairs)]
    ppermute x2 -> x3, waiting for transfers between devices: 3.07 us -> 2.04 us  [swap_core(): return lax.ppermute(value, 'pcol', [(0, 1), (1, 0)])]
    another operation x0 -> x8, other arithmetic: none -> 0.72 us  [the longest x5 0.38 us: whole(): return jnp.stack([real, imag], axis=axis)]
    reduce_sum x1, other arithmetic: 0.09 us -> 0.77 us  [keep_of(): return jnp.sum(jnp.where(hits[None], structure[:, None, :], 0), axis=2)]
    sub x5 -> x1, other arithmetic: 0.19 us -> 0.78 us  [local(): return (columns, diag_inverse.astype(jnp.float32) - diag)]
    unnamed x11 -> x7, local copies, waits for them, and re-layouts: 2.31 us -> 1.76 us
    dot_general x4 -> x2, matrix products: 1.15 us -> 0.62 us  [the longest x1 0.36 us: local(): lax.dot_general(left, right, (((0, 1, 2, 3), (0, 1, 2, 4)), ((), ())), pr...]
  transfers between devices with their start and end apart: 10 -> 13, of which waited for: 10 -> 9; matrix products, arithmetic and copies ran while one was open for 2% -> 6% of each run, Pallas kernels for 0% -> 0%
where the time goes in v2:
time: 40.9 us; the launch traced here: 40.6 us
  waiting for transfers between devices  18.1 us (44%)
  starting transfers between devices  15.6 us (38%)
  other arithmetic  3 us (7%)
  local copies, waits for them, and re-layouts  2.38 us (6%)
  between operations  0.96 us (2%)
  matrix products  0.62 us (2%)
    ppermute x10, waiting for transfers between devices, swap(): return lax.ppermute(value, AXES, pairs)  16 us
    ppermute x10, starting transfers between devices, swap(): return lax.ppermute(value, AXES, pairs)  15.4 us
    ppermute x3, waiting for transfers between devices, swap_core(): return lax.ppermute(value, 'pcol', [(0, 1), (1, 0)])  2.04 us
    unnamed x7, local copies, waits for them, and re-layouts  1.76 us
  transfers between devices with their start and end apart: 13, of which 9 were waited for; matrix products, arithmetic and copies ran while one was open for 6% of the time, Pallas kernels for 0%

profile of v2, /device:TPU:0, one launch (start us, length us, event | category | flops | bytes accessed | tf_op | source)
XLA Modules:
  0.0 40.6 jit_solution(3017622884174144460)
XLA Ops:
  0.6 0.9 %copy.54 = bf16[3,2,48,128]{3,2,0,1:T(8,128)(2,1)S(1)} copy(bf16[3,2,48,128]{3,2,1,0:T(8,128)(2,1)} %param.5) | data formatting | bytes 147456 | tf_op args[1]
  1.5 2.9 %collective-permute-start.1 = (bf16[3,2,48,128]{3,2,0,1:T(8,128)(2,1)S(1)}, bf16[3,2,48,128]{3,2,0,1:T(8,128)(2,1)S(1)}, u32[]{:S(2)}, u32[]{:S(2)}) collective-permute-start(bf16[3,2,48,128]{3,2,0,1:T(8,128)(2,1)S(1)} %copy.54), channel_id=1, source_target_pairs={{0,2},{1,3},{2,0},{3,1},{4,6},{5,7},{6,4},{7,5},{8,10},{9,11},{10,... | collective-permute-start | bytes 221192 | tf_op jit(solution)/shard_map/ppermute | solution.py:16
  4.5 0.8 %select_reduce_fusion.1 = (s32[3,48]{1,0:T(4,128)S(1)}, s32[3,48]{1,0:T(4,128)S(1)}) fusion(s32[3,6]{1,0:T(4,128)} %param.7, pred[48,6]{0,1:T(8,128)(4,1)S(1)} %iota_compare_fusion.1, pred[48,6]{0,1:T(8,128)(4,1)S(1)} %iota_compare_fusion), kind=kLoop, calls=%fused_computation.53 | loop fusion | flops 3168 | bytes 1800 | tf_op jit(solution)/shard_map/reduce_sum | solution.py:82
  5.3 1.5 %collective-permute-done.1 = bf16[3,2,48,128]{3,2,0,1:T(8,128)(2,1)S(1)} collective-permute-done((bf16[3,2,48,128]{3,2,0,1:T(8,128)(2,1)S(1)}, bf16[3,2,48,128]{3,2,0,1:T(8,128)(2,1)S(1)}, u32[]{:S(2)}, u32[]{:S(2)}) %collective-permute-start.1) | collective-permute-done | bytes 73760 | tf_op jit(solution)/shard_map/ppermute | solution.py:16
  6.8 0.1 maximum_multiply_fusion
  6.9 0.0 copy-start
  6.9 0.1 dynamic-slice_bitcast_fusion.3
  7.1 0.1 bitcast_dynamic-update-slice_fusion.3
  7.2 2.2 %collective-permute-start.2 = (bf16[2,3,48,128]{3,2,0,1:T(8,128)(2,1)S(1)}, bf16[2,3,48,128]{3,2,0,1:T(8,128)(2,1)S(1)}, u32[]{:S(2)}, u32[]{:S(2)}) collective-permute-start(bf16[2,3,48,128]{3,2,0,1:T(8,128)(2,1)S(1)} %get-tuple-element.11), channel_id=1, source_target_pairs={{0,4},{1,9},{2,6},{3,11},{4,0},{5,13},{6,2},{7,15},{8,12},{9,1},{1... | collective-permute-start | bytes 221192 | tf_op jit(solution)/shard_map/ppermute | solution.py:16
  9.4 0.0 copy-done
  9.4 1.5 %collective-permute-start = (bf16[2,8,1,48,96]{4,3,2,1,0:T(8,128)(2,1)S(1)}, bf16[2,8,1,48,96]{4,3,2,1,0:T(8,128)(2,1)S(1)}, u32[]{:S(2)}, u32[]{:S(2)}) collective-permute-start(bf16[2,8,1,48,96]{4,3,2,1,0:T(8,128)(2,1)S(1)} %copy-done), channel_id=1, source_target_pairs={{0,2},{1,3},{2,0},{3,1},{4,6},{5,7},{6,4},{7,5},{8,10},{9,11},{10,... | collective-permute-start | bytes 442376 | tf_op jit(solution)/shard_map/ppermute | solution.py:16
  10.9 2.7 %collective-permute-start.3 = (bf16[2,3,48,128]{3,2,0,1:T(8,128)(2,1)S(1)}, bf16[2,3,48,128]{3,2,0,1:T(8,128)(2,1)S(1)}, u32[]{:S(2)}, u32[]{:S(2)}) collective-permute-start(bf16[2,3,48,128]{3,2,0,1:T(8,128)(2,1)S(1)} %get-tuple-element.11), channel_id=1, source_target_pairs={{0,8},{1,5},{2,10},{3,7},{4,12},{5,1},{6,14},{7,3},{8,0},{9,13},{1... | collective-permute-start | bytes 221192 | tf_op jit(solution)/shard_map/ppermute | solution.py:16
  13.6 0.3 collective-permute-start.4
  13.9 0.0 collective-permute-done.2
  13.9 3.9 %collective-permute-done.3 = bf16[2,3,48,128]{3,2,0,1:T(8,128)(2,1)S(1)} collective-permute-done((bf16[2,3,48,128]{3,2,0,1:T(8,128)(2,1)S(1)}, bf16[2,3,48,128]{3,2,0,1:T(8,128)(2,1)S(1)}, u32[]{:S(2)}, u32[]{:S(2)}) %collective-permute-start.3) | collective-permute-done | bytes 73760 | tf_op jit(solution)/shard_map/ppermute | solution.py:16
  17.8 1.9 %collective-permute-done.4 = bf16[2,3,48,128]{3,2,0,1:T(8,128)(2,1)S(1)} collective-permute-done((bf16[2,3,48,128]{3,2,0,1:T(8,128)(2,1)S(1)}, bf16[2,3,48,128]{3,2,0,1:T(8,128)(2,1)S(1)}, u32[]{:S(2)}, u32[]{:S(2)}) %collective-permute-start.4) | collective-permute-done | bytes 73760 | tf_op jit(solution)/shard_map/ppermute | solution.py:16
  19.7 0.1 slice_negate_fusion
  19.9 0.2 maximum_bitcast_fusion.4
  20.1 0.0 collective-permute-done
  20.1 0.1 fusion.5
  20.2 0.4 fusion
  20.6 0.1 collective-permute-start.5
  20.7 1.4 %collective-permute-done.5 = f32[2,48,3,128]{3,1,0,2:T(8,128)S(1)} collective-permute-done((f32[2,48,3,128]{3,1,0,2:T(8,128)S(1)}, f32[2,48,3,128]{3,1,0,2:T(8,128)S(1)}, u32[]{:S(2)}, u32[]{:S(2)}) %collective-permute-start.5) | collective-permute-done | bytes 147488 | tf_op jit(solution)/shard_map/ppermute | solution.py:20
  22.1 0.1 fusion.14
  22.2 0.1 slice_negate_fusion.1
  22.3 0.6 %collective-permute-start.6 = (bf16[48,3,128]{2,0,1:T(8,128)(2,1)S(1)}, bf16[48,3,128]{2,0,1:T(8,128)(2,1)S(1)}, u32[]{:S(2)}, u32[]{:S(2)}) collective-permute-start(bf16[48,3,128]{2,0,1:T(8,128)(2,1)S(1)} %slice_bitcast_fusion), channel_id=1, source_target_pairs={{0,2},{1,3},{2,0},{3,1},{4,6},{5,7},{6,4},{7,5},{8,10},{9,11},{10,... | collective-permute-start | bytes 110600 | tf_op jit(solution)/shard_map/ppermute | solution.py:16
  22.9 0.1 maximum_bitcast_fusion.8
  23.0 0.3 fusion.7
  23.3 0.1 collective-permute-start.7
  23.3 3.0 %collective-permute-done.6 = bf16[48,3,128]{2,0,1:T(8,128)(2,1)S(1)} collective-permute-done((bf16[48,3,128]{2,0,1:T(8,128)(2,1)S(1)}, bf16[48,3,128]{2,0,1:T(8,128)(2,1)S(1)}, u32[]{:S(2)}, u32[]{:S(2)}) %collective-permute-start.6) | collective-permute-done | bytes 36896 | tf_op jit(solution)/shard_map/ppermute | solution.py:16
  26.3 0.1 fusion.21
  26.4 0.0 collective-permute-done.7
  26.4 1.0 %collective-permute-start.10 = (bf16[3,64,128]{2,1,0:T(8,128)(2,1)S(1)}, bf16[3,64,128]{2,1,0:T(8,128)(2,1)S(1)}, u32[]{:S(2)}, u32[]{:S(2)}) collective-permute-start(bf16[3,64,128]{2,1,0:T(8,128)(2,1)S(1)} %fusion.15), channel_id=1, source_target_pairs={{0,12},{1,13},{2,14},{3,15},{4,8},{5,9},{6,10},{7,11},{8,4},{9,5},... | collective-permute-start | bytes 147464 | tf_op jit(solution)/shard_map/ppermute | solution.py:16
  27.4 0.2 collective-permute-start.8
  27.6 3.3 %collective-permute-start.9 = (bf16[3,64,128]{2,1,0:T(8,128)(2,1)S(1)}, bf16[3,64,128]{2,1,0:T(8,128)(2,1)S(1)}, u32[]{:S(2)}, u32[]{:S(2)}) collective-permute-start(bf16[3,64,128]{2,1,0:T(8,128)(2,1)S(1)} %fusion.15), channel_id=1, source_target_pairs={{0,8},{1,5},{2,10},{3,7},{4,12},{5,1},{6,14},{7,3},{8,0},{9,13},{1... | collective-permute-start | bytes 147464 | tf_op jit(solution)/shard_map/ppermute | solution.py:16
  30.9 0.1 fusion.22
  31.0 1.4 %collective-permute-done.10 = bf16[3,64,128]{2,1,0:T(8,128)(2,1)S(1)} collective-permute-done((bf16[3,64,128]{2,1,0:T(8,128)(2,1)S(1)}, bf16[3,64,128]{2,1,0:T(8,128)(2,1)S(1)}, u32[]{:S(2)}, u32[]{:S(2)}) %collective-permute-start.10) | collective-permute-done | bytes 49184 | tf_op jit(solution)/shard_map/ppermute | solution.py:16
  32.4 0.0 collective-permute-done.8
  32.4 0.6 %collective-permute-done.9 = bf16[3,64,128]{2,1,0:T(8,128)(2,1)S(1)} collective-permute-done((bf16[3,64,128]{2,1,0:T(8,128)(2,1)S(1)}, bf16[3,64,128]{2,1,0:T(8,128)(2,1)S(1)}, u32[]{:S(2)}, u32[]{:S(2)}) %collective-permute-start.9) | collective-permute-done | bytes 49184 | tf_op jit(solution)/shard_map/ppermute | solution.py:16
  33.0 0.8 %collective-permute-start.11 = (f32[3,64,128]{2,1,0:T(8,128)S(1)}, f32[3,64,128]{2,1,0:T(8,128)S(1)}, u32[]{:S(2)}, u32[]{:S(2)}) collective-permute-start(f32[3,64,128]{2,1,0:T(8,128)S(1)} %add_add_fusion), channel_id=1, source_target_pairs={{0,2},{1,3},{2,0},{3,1},{4,6},{5,7},{6,4},{7,5},{8,10},{9,11},{10,... | collective-permute-start | bytes 294920 | tf_op jit(solution)/shard_map/ppermute | solution.py:16
  33.7 0.1 maximum_bitcast_fusion.9
  33.8 3.8 %collective-permute-done.11 = f32[3,64,128]{2,1,0:T(8,128)S(1)} collective-permute-done((f32[3,64,128]{2,1,0:T(8,128)S(1)}, f32[3,64,128]{2,1,0:T(8,128)S(1)}, u32[]{:S(2)}, u32[]{:S(2)}) %collective-permute-start.11) | collective-permute-done | bytes 98336 | tf_op jit(solution)/shard_map/ppermute | solution.py:16
  37.7 0.1 fusion.19
  37.8 0.1 fusion.20
  37.9 0.1 maximum_bitcast_fusion.5
  38.0 0.1 maximum_bitcast_fusion.6
  38.1 0.1 collective-permute-start.12
  38.2 0.1 maximum_bitcast_fusion.10
  38.3 0.6 %copy.46 = bf16[3,2,48,128]{3,2,1,0:T(8,128)(2,1)} copy(bf16[3,2,48,128]{3,2,0,1:T(8,128)(2,1)S(1)} %maximum_bitcast_fusion.7) | data formatting | bytes 147456
  38.9 0.0 copy-start.1
  38.9 0.7 %collective-permute-done.12 = f32[3,2,64,128]{3,2,1,0:T(8,128)S(1)} collective-permute-done((f32[3,2,64,128]{3,2,1,0:T(8,128)S(1)}, f32[3,2,64,128]{3,2,1,0:T(8,128)S(1)}, u32[]{:S(2)}, u32[]{:S(2)}) %collective-permute-start.12) | collective-permute-done | bytes 196640 | tf_op jit(solution)/shard_map/ppermute | solution.py:20
  39.6 0.2 copy-done.1
  39.8 0.8 %maximum_subtract_fusion = f32[3,2,128,128]{3,2,1,0:T(8,128)} fusion(f32[3,2,64,128]{3,2,1,0:T(8,128)S(1)} %get-tuple-element.13, f32[3,2,64,128]{3,2,1,0:T(8,128)S(1)} %get-tuple-element.12, bf16[3,2,128,128]{3,2,1,0:T(8,128)(2,1)S(1)} %copy-done.1), kind=kLoop, calls=%fused_computation.7 | loop fusion | flops 294912 | bytes 983040 | tf_op jit(solution)/shard_map/sub | solution.py:132
  (23 shorter events, 0.4 us)
Async XLA Ops:
  1.5 5.3 %collective-permute-start.1 = (bf16[3,2,48,128]{3,2,0,1:T(8,128)(2,1)S(1)}, bf16[3,2,48,128]{3,2,0,1:T(8,128)(2,1)S(1)}, u32[]{:S(2)}, u32[]{:S(2)}) collective-permute-start(bf16[3,2,48,128]{3,2,0,1:T(8,128)(2,1)S(1)} %copy.54), channel_id=1, source_target_pairs={{0,2},{1,3},{2,0},{3,1},{4,6},{5,7},{6,4},{7,5},{8,10},{9,11},{10,... | collective-permute-start | bytes 221192 | tf_op jit(solution)/shard_map/ppermute | solution.py:16
  6.9 2.5 %copy-start = (bf16[2,8,1,48,96]{4,3,2,1,0:T(8,128)(2,1)S(1)}, bf16[2,8,1,48,96]{4,3,2,1,0:T(8,128)(2,1)}, u32[]{:S(2)}) copy-start(bf16[2,8,1,48,96]{4,3,2,1,0:T(8,128)(2,1)} %param.4) | copy-start | bytes 442372
  7.2 6.7 %collective-permute-start.2 = (bf16[2,3,48,128]{3,2,0,1:T(8,128)(2,1)S(1)}, bf16[2,3,48,128]{3,2,0,1:T(8,128)(2,1)S(1)}, u32[]{:S(2)}, u32[]{:S(2)}) collective-permute-start(bf16[2,3,48,128]{3,2,0,1:T(8,128)(2,1)S(1)} %get-tuple-element.11), channel_id=1, source_target_pairs={{0,4},{1,9},{2,6},{3,11},{4,0},{5,13},{6,2},{7,15},{8,12},{9,1},{1... | collective-permute-start | bytes 221192 | tf_op jit(solution)/shard_map/ppermute | solution.py:16
  9.4 10.7 %collective-permute-start = (bf16[2,8,1,48,96]{4,3,2,1,0:T(8,128)(2,1)S(1)}, bf16[2,8,1,48,96]{4,3,2,1,0:T(8,128)(2,1)S(1)}, u32[]{:S(2)}, u32[]{:S(2)}) collective-permute-start(bf16[2,8,1,48,96]{4,3,2,1,0:T(8,128)(2,1)S(1)} %copy-done), channel_id=1, source_target_pairs={{0,2},{1,3},{2,0},{3,1},{4,6},{5,7},{6,4},{7,5},{8,10},{9,11},{10,... | collective-permute-start | bytes 442376 | tf_op jit(solution)/shard_map/ppermute | solution.py:16
  10.9 6.9 %collective-permute-start.3 = (bf16[2,3,48,128]{3,2,0,1:T(8,128)(2,1)S(1)}, bf16[2,3,48,128]{3,2,0,1:T(8,128)(2,1)S(1)}, u32[]{:S(2)}, u32[]{:S(2)}) collective-permute-start(bf16[2,3,48,128]{3,2,0,1:T(8,128)(2,1)S(1)} %get-tuple-element.11), channel_id=1, source_target_pairs={{0,8},{1,5},{2,10},{3,7},{4,12},{5,1},{6,14},{7,3},{8,0},{9,13},{1... | collective-permute-start | bytes 221192 | tf_op jit(solution)/shard_map/ppermute | solution.py:16
  13.6 6.2 %collective-permute-start.4 = (bf16[2,3,48,128]{3,2,0,1:T(8,128)(2,1)S(1)}, bf16[2,3,48,128]{3,2,0,1:T(8,128)(2,1)S(1)}, u32[]{:S(2)}, u32[]{:S(2)}) collective-permute-start(bf16[2,3,48,128]{3,2,0,1:T(8,128)(2,1)S(1)} %get-tuple-element.11), channel_id=1, source_target_pairs={{0,12},{1,13},{2,14},{3,15},{4,8},{5,9},{6,10},{7,11},{8,4},{9,5},... | collective-permute-start | bytes 221192 | tf_op jit(solution)/shard_map/ppermute | solution.py:16
  20.6 1.4 %collective-permute-start.5 = (f32[2,48,3,128]{3,1,0,2:T(8,128)S(1)}, f32[2,48,3,128]{3,1,0,2:T(8,128)S(1)}, u32[]{:S(2)}, u32[]{:S(2)}) collective-permute-start(f32[2,48,3,128]{3,1,0,2:T(8,128)S(1)} %dynamic-slice_bitcast_fusion), channel_id=1, source_target_pairs={{0,1},{1,0},{2,3},{3,2},{4,5},{5,4},{6,7},{7,6},{8,9},{9,8},{10,11... | collective-permute-start | bytes 442376 | tf_op jit(solution)/shard_map/ppermute | solution.py:20
  22.3 4.0 %collective-permute-start.6 = (bf16[48,3,128]{2,0,1:T(8,128)(2,1)S(1)}, bf16[48,3,128]{2,0,1:T(8,128)(2,1)S(1)}, u32[]{:S(2)}, u32[]{:S(2)}) collective-permute-start(bf16[48,3,128]{2,0,1:T(8,128)(2,1)S(1)} %slice_bitcast_fusion), channel_id=1, source_target_pairs={{0,2},{1,3},{2,0},{3,1},{4,6},{5,7},{6,4},{7,5},{8,10},{9,11},{10,... | collective-permute-start | bytes 110600 | tf_op jit(solution)/shard_map/ppermute | solution.py:16
  23.3 3.1 %collective-permute-start.7 = (f32[3,64,128]{2,1,0:T(8,128)S(1)}, f32[3,64,128]{2,1,0:T(8,128)S(1)}, u32[]{:S(2)}, u32[]{:S(2)}) collective-permute-start(f32[3,64,128]{2,1,0:T(8,128)S(1)} %dynamic-slice_bitcast_fusion.1), channel_id=1, source_target_pairs={{0,1},{1,0},{2,3},{3,2},{4,5},{5,4},{6,7},{7,6},{8,9},{9,8},{10,11... | collective-permute-start | bytes 294920 | tf_op jit(solution)/shard_map/ppermute | solution.py:20
  26.4 6.0 %collective-permute-start.10 = (bf16[3,64,128]{2,1,0:T(8,128)(2,1)S(1)}, bf16[3,64,128]{2,1,0:T(8,128)(2,1)S(1)}, u32[]{:S(2)}, u32[]{:S(2)}) collective-permute-start(bf16[3,64,128]{2,1,0:T(8,128)(2,1)S(1)} %fusion.15), channel_id=1, source_target_pairs={{0,12},{1,13},{2,14},{3,15},{4,8},{5,9},{6,10},{7,11},{8,4},{9,5},... | collective-permute-start | bytes 147464 | tf_op jit(solution)/shard_map/ppermute | solution.py:16
  27.4 5.0 %collective-permute-start.8 = (bf16[3,64,128]{2,1,0:T(8,128)(2,1)S(1)}, bf16[3,64,128]{2,1,0:T(8,128)(2,1)S(1)}, u32[]{:S(2)}, u32[]{:S(2)}) collective-permute-start(bf16[3,64,128]{2,1,0:T(8,128)(2,1)S(1)} %fusion.15), channel_id=1, source_target_pairs={{0,4},{1,9},{2,6},{3,11},{4,0},{5,13},{6,2},{7,15},{8,12},{9,1},{1... | collective-permute-start | bytes 147464 | tf_op jit(solution)/shard_map/ppermute | solution.py:16
  27.6 5.3 %collective-permute-start.9 = (bf16[3,64,128]{2,1,0:T(8,128)(2,1)S(1)}, bf16[3,64,128]{2,1,0:T(8,128)(2,1)S(1)}, u32[]{:S(2)}, u32[]{:S(2)}) collective-permute-start(bf16[3,64,128]{2,1,0:T(8,128)(2,1)S(1)} %fusion.15), channel_id=1, source_target_pairs={{0,8},{1,5},{2,10},{3,7},{4,12},{5,1},{6,14},{7,3},{8,0},{9,13},{1... | collective-permute-start | bytes 147464 | tf_op jit(solution)/shard_map/ppermute | solution.py:16
  33.0 4.7 %collective-permute-start.11 = (f32[3,64,128]{2,1,0:T(8,128)S(1)}, f32[3,64,128]{2,1,0:T(8,128)S(1)}, u32[]{:S(2)}, u32[]{:S(2)}) collective-permute-start(f32[3,64,128]{2,1,0:T(8,128)S(1)} %add_add_fusion), channel_id=1, source_target_pairs={{0,2},{1,3},{2,0},{3,1},{4,6},{5,7},{6,4},{7,5},{8,10},{9,11},{10,... | collective-permute-start | bytes 294920 | tf_op jit(solution)/shard_map/ppermute | solution.py:16
  38.1 1.5 %collective-permute-start.12 = (f32[3,2,64,128]{3,2,1,0:T(8,128)S(1)}, f32[3,2,64,128]{3,2,1,0:T(8,128)S(1)}, u32[]{:S(2)}, u32[]{:S(2)}) collective-permute-start(f32[3,2,64,128]{3,2,1,0:T(8,128)S(1)} %pad_maximum_fusion), channel_id=1, source_target_pairs={{0,1},{1,0},{2,3},{3,2},{4,5},{5,4},{6,7},{7,6},{8,9},{9,8},{10,11... | collective-permute-start | bytes 589832 | tf_op jit(solution)/shard_map/ppermute | solution.py:20
  38.9 0.9 %copy-start.1 = (bf16[3,2,128,128]{3,2,1,0:T(8,128)(2,1)S(1)}, bf16[3,2,128,128]{3,2,1,0:T(8,128)(2,1)}, u32[]{:S(2)}) copy-start(bf16[3,2,128,128]{3,2,1,0:T(8,128)(2,1)} %param.6) | copy-start | bytes 589828

commit v3 on v1

v3 whole, which is shorter than its diff:
```python
import functools

import jax
import jax.numpy as jnp
from jax import lax
from jax.experimental import pallas as pl
from jax.experimental.layout import Layout, with_layout_constraint
from jax.experimental.pallas import tpu as pltpu
from jax.sharding import PartitionSpec as P

AXES = ("prow", "pcol")
MASKS = ((2, 4), (4, 2), (6, 6))
MASKS_SUM = ((2, 2), (4, 4), (6, 6))
VMEM = pl.BlockSpec(memory_space=pltpu.VMEM)


def swap(value, rows, cols, mask0, mask1):
    pairs = []
    for row in range(rows):
        for col in range(cols):
            mask = mask0 if col == 0 else mask1
            pairs.append((row * cols + col, (row ^ mask) * cols + col))
    return lax.ppermute(value, AXES, pairs)


def swap_core(value):
    return lax.ppermute(value, "pcol", [(0, 1), (1, 0)])


def after(value, *others):
    return lax.optimization_barrier((value,) + others)[0]


def plain(value):
    return with_layout_constraint(value, Layout(tuple(range(value.ndim))))


def call(kernel, outs, operands, scratch=()):
    shapes = [jax.ShapeDtypeStruct(shape, dtype) for shape, dtype in outs]
    size = sum(v.size * v.dtype.itemsize for v in list(operands) + shapes)
    return pl.pallas_call(
        kernel,
        out_shape=shapes,
        in_specs=[VMEM] * len(operands),
        out_specs=[VMEM] * len(shapes),
        scratch_shapes=list(scratch),
        compiler_params=pltpu.CompilerParams(vmem_limit_bytes=2 * size + (4 << 20)),
    )(*operands)


def keep_rows(structure, node, start, count, width):
    blocks = structure.shape[1]
    row = start + lax.broadcasted_iota(jnp.int32, (count, blocks), 0)
    hit = row // width == lax.broadcasted_iota(jnp.int32, (count, blocks), 1)
    table = structure[node : node + 1, :].astype(jnp.float32)
    return jnp.sum(jnp.where(hit, table, 0.0), axis=1, keepdims=True)


def swap_halves(value):
    half = value.shape[-1] // 2
    return jnp.concatenate([value[:, half:], value[:, :half]], axis=-1)


def turned(value):
    lane = lax.broadcasted_iota(jnp.int32, value.shape, 1)
    other = swap_halves(value)
    return jnp.where(lane < value.shape[-1] // 2, -other, other)


def pick_kernel(structure, panels, panels_far, block):
    supernodes, _, rows_half, width = panels.shape
    row_index, col_index = lax.axis_index("prow"), lax.axis_index("pcol")
    parity = row_index % 2
    lane = lax.broadcasted_iota(jnp.int32, (rows_half, width), 1)
    low = lane < width // 2
    for far, source in ((0, panels), (1, panels_far)):
        start = ((row_index ^ far) * 2 + col_index) * rows_half
        for node in range(supernodes):
            keep = keep_rows(structure, node, start, rows_half, width)
            real = source[node, 0].astype(jnp.float32)
            imag = source[node, 1].astype(jnp.float32)
            left = jnp.where(low, real, swap_halves(imag))
            right = jnp.where(low, swap_halves(real), imag)
            value = jnp.where(parity == 0, left, right) * keep
            block[parity ^ far, :, node * width : (node + 1) * width] = value.astype(jnp.bfloat16)


def product_kernel(width, near, far, held, out, held_turned):
    count, _, rows_half, lanes = held.shape
    supernodes = lanes // width

    def turn(index, _):
        for x in range(2):
            for node in range(supernodes):
                part = slice(node * width, (node + 1) * width)
                value = held[index, x, :, part].astype(jnp.float32)
                held_turned[index, x, :, part] = turned(value).astype(jnp.bfloat16)
        return _

    if count <= 4:
        for index in range(count):
            turn(index, 0)
    else:
        lax.fori_loop(0, count, turn, 0)
    depth = count * 2 * rows_half
    real = held[...].reshape(depth, lanes)
    imag = held_turned[...].reshape(depth, lanes)
    for far_or, left in ((0, near), (1, far)):
        out[far_or] = jnp.dot(
            left[:, :depth], real, preferred_element_type=jnp.float32
        ) + jnp.dot(left[:, depth:], imag, preferred_element_type=jnp.float32)


def diagonal_kernel(structure, mine, theirs, panels, panels_far, panels_core, panels_far_core, own, far, diag, left, right, full):
    supernodes, _, rows_half, width = panels.shape
    row_index, col_index = lax.axis_index("prow"), lax.axis_index("pcol")
    rows_dev = 2 * rows_half
    for far_or, (same, cross) in ((0, (panels, panels_core)), (1, (panels_far, panels_far_core))):
        start = (row_index ^ far_or) * rows_dev
        for node in range(supernodes):
            for part in range(2):
                left[node, far_or, part, col_index] = same[node, part]
                left[node, far_or, part, 1 - col_index] = cross[node, part]
            lanes = slice(node * width, (node + 1) * width)
            keep = keep_rows(structure, node, start, rows_dev, width)
            value = -((mine[far_or, :, lanes] + theirs[far_or, :, lanes]) * keep)
            value = value.astype(jnp.bfloat16).astype(jnp.float32)
            column = value.astype(jnp.bfloat16).reshape(2, rows_half, width)
            right[node, far_or, 0] = column
            right[node, far_or, 1] = turned(value).astype(jnp.bfloat16).reshape(2, rows_half, width)
            out = own if far_or == 0 else far
            out[node] = right[node, far_or, 0, col_index]
    depth = 4 * rows_dev
    for node in range(supernodes):
        full[node] = lax.dot_general(
            left[node].reshape(depth, width),
            right[node].reshape(depth, width),
            (((0,), (0,)), ((), ())),
            preferred_element_type=jnp.float32,
        )
    half = width // 2
    diag[...] = full[:, pl.ds(pl.multiple_of(col_index * half, half), half), :]


def unpack(near, far):
    parity = lax.axis_index("prow") % 2
    low = jnp.where(parity == 0, near, far)
    high = jnp.where(parity == 0, far, near)
    first = lax.broadcasted_iota(jnp.int32, near.shape, 1) < near.shape[1] // 2
    return jnp.where(first, low, swap_halves(high)), jnp.where(first, swap_halves(low), high)


def sum_kernel(terms, columns, packet):
    first, second, third, fourth = [term[...].astype(jnp.float32) for term in terms]
    value = (first + second) + (third + fourth)
    high = value.astype(jnp.bfloat16)
    rows = value.shape[0]
    packet[:rows] = high
    packet[rows : 2 * rows] = (value - high.astype(jnp.float32)).astype(jnp.bfloat16)
    packet[2 * rows :] = columns[...]


def columns_kernel(own, other, out):
    supernodes, _, rows_half, width = out.shape
    for node in range(supernodes):
        rows = slice(node * rows_half, (node + 1) * rows_half)
        real, imag = unpack(
            own[rows].astype(jnp.float32),
            other[rows].astype(jnp.float32),
        )
        out[node, 0] = real.astype(jnp.bfloat16)
        out[node, 1] = imag.astype(jnp.bfloat16)


def final_kernel(diag_inverse, mine, far, mine_core, far_core, out):
    supernodes, _, width, _ = out.shape
    half = width // 2
    col_index = lax.axis_index("pcol")

    def value(ref, node):
        first, second = node * half, (supernodes + node) * half
        return ref[first : first + half].astype(jnp.float32) + ref[second : second + half].astype(jnp.float32)

    for node in range(supernodes):
        for col, near_ref, far_ref in ((col_index, mine, far), (1 - col_index, mine_core, far_core)):
            rows = pl.ds(pl.multiple_of(col * half, half), half)
            real, imag = unpack(value(near_ref, node), value(far_ref, node))
            out[node, 0, rows] = diag_inverse[node, 0, rows].astype(jnp.float32) - real
            out[node, 1, rows] = diag_inverse[node, 1, rows].astype(jnp.float32) - imag


def solution(mesh):
    rows, cols = mesh.shape["prow"], mesh.shape["pcol"]

    def local(anc_inverse, panels, diag_inverse, structure):
        supernodes, _, rows_half, width = panels.shape
        half = width // 2
        groups = anc_inverse.shape[1]
        rows_dev = anc_inverse.shape[4]
        lanes = supernodes * width
        row_index = lax.axis_index("prow")
        col_index = lax.axis_index("pcol")
        here = row_index // 2
        bf16, f32 = jnp.bfloat16, jnp.float32

        panels = plain(panels)
        panels_far = plain(swap(panels, rows, cols, 1, 1))
        near = anc_inverse.reshape(2 * groups * rows_half, rows_dev).T
        far = swap(near, rows, cols, 1, 1)

        (block,) = call(
            pick_kernel, [((2, rows_half, lanes), bf16)], [structure, panels, panels_far]
        )
        held = jnp.zeros((rows // 2,) + block.shape, bf16)
        held = lax.dynamic_update_index_in_dim(held, block, here, 0)
        arrived = [swap(block, rows, cols, mask0, mask1) for mask0, mask1 in MASKS]
        panels_core = swap_core(panels)
        panels_far_core = swap_core(panels_far)
        for (mask0, mask1), value in zip(MASKS, arrived):
            step = jnp.where(col_index == 0, mask0, mask1) // 2
            held = lax.dynamic_update_index_in_dim(held, value, here ^ step, 0)
        size = 8
        while size < rows:
            count = size // 2
            start = (here // count) * count
            own = lax.dynamic_slice_in_dim(held, start, count, 0)
            other = swap(own, rows, cols, size, size)
            held = lax.dynamic_update_slice_in_dim(held, other, start ^ count, 0)
            size *= 2

        held = after(held, panels_core, panels_far_core)
        (partial,) = call(
            functools.partial(product_kernel, width),
            [((2, rows_dev, lanes), f32)],
            [near, far, held],
            [pltpu.VMEM(held.shape, bf16)],
        )
        pieces = (supernodes, 2, 2, cols, rows_half, width)
        own, send, diag = call(
            diagonal_kernel,
            [((supernodes, rows_half, width), bf16)] * 2 + [((supernodes, half, width), f32)],
            [structure, partial, swap_core(partial), panels, panels_far, panels_core, panels_far_core],
            [pltpu.VMEM(pieces, bf16), pltpu.VMEM(pieces, bf16), pltpu.VMEM((supernodes, width, width), f32)],
        )
        count = supernodes * half
        term = diag.astype(bf16).reshape(count, width)
        terms = [term] + [swap(term, rows, cols, mask0, mask1) for mask0, mask1 in MASKS_SUM]
        size = 8
        while size < rows:
            first, second, third, fourth = [t.astype(f32) for t in terms]
            term = (first + second) + (third + fourth)
            other = swap(term, rows, cols, size, size)
            terms = [term, other, jnp.zeros_like(term), jnp.zeros_like(term)]
            size *= 2
        columns_rows = supernodes * rows_half
        (packet,) = call(
            lambda *refs: sum_kernel(refs[:4], refs[4], refs[5]),
            [((2 * count + columns_rows, width), bf16)],
            terms + [send.reshape(columns_rows, width)],
        )
        other = swap(packet, rows, cols, 1, 1)
        mine, far = packet[: 2 * count], other[: 2 * count]
        (columns,) = call(
            columns_kernel,
            [((supernodes, 2, rows_half, width), bf16)],
            [own.reshape(columns_rows, width), other[2 * count :]],
        )
        (diag,) = call(
            final_kernel,
            [((supernodes, 2, width, width), f32)],
            [diag_inverse, mine, far, swap_core(mine), swap_core(far)],
        )
        return columns, diag

    in_specs = (
        P("pole", None, "pcol", None, "prow"),
        P("pole", None, ("prow", "pcol"), None),
        P("pole", None, None, None),
        P(),
    )
    out_specs = (P("pole", None, ("prow", "pcol"), None), P("pole", None, None, None))
    return jax.shard_map(local, mesh=mesh, in_specs=in_specs, out_specs=out_specs, check_vma=False)
```

time: 43.7 us -> 35.4 us (0.81)
  waiting for transfers between devices: 25 us -> 16 us
  Pallas kernels: 0 us -> 3.1 us
  local copies, waits for them, and re-layouts: 2.52 us -> 1.18 us
  matrix products: 1.15 us -> 0 us
  starting transfers between devices: 13.4 us -> 14.1 us
  other arithmetic: 0.65 us -> 0.01 us
    ppermute x8 -> x9, waiting for transfers between devices: 21.9 us -> 13.9 us  [swap(): return lax.ppermute(value, AXES, pairs)]
    pallas_call x0 -> x6, Pallas kernels: none -> 3.1 us  [call(): pl.pallas_call(kernel, out_shape=shapes, in_specs=[VMEM] * len(operands),...]
    unnamed x11 -> x6, local copies, waits for them, and re-layouts: 2.31 us -> 0.01 us
    dot_general x4 -> x0, matrix products: 1.15 us -> none  [the longest x2 0.62 us: contract_nodes(): lax.dot_general(left, right, (((0, 3), (0, 3)), ((1,), (1,))), preferred_...]
    reshape x0 -> x1, local copies, waits for them, and re-layouts: none -> 1.05 us  [local(): near = anc_inverse.reshape(2 * groups * rows_half, rows_dev).T]
    ppermute x2 -> x5, waiting for transfers between devices: 3.07 us -> 2.11 us  [swap_core(): return lax.ppermute(value, 'pcol', [(0, 1), (1, 0)])]
    ppermute x8 -> x9, starting transfers between devices: 13.2 us -> 13.9 us  [swap(): return lax.ppermute(value, AXES, pairs)]
  transfers between devices with their start and end apart: 10 -> 14, of which waited for: 10 -> 10; matrix products, arithmetic and copies ran while one was open for 2% -> 3% of each run, Pallas kernels for 0% -> 3%
where the time goes in v3:
time: 35.4 us; the launch traced here: 35.2 us
  waiting for transfers between devices  16 us (45%)
  starting transfers between devices  14.1 us (40%)
  Pallas kernels  3.1 us (9%)
  local copies, waits for them, and re-layouts  1.18 us (3%)
  between operations  0.77 us (2%)
    ppermute x9, starting transfers between devices, swap(): return lax.ppermute(value, AXES, pairs)  13.9 us
    ppermute x9, waiting for transfers between devices, swap(): return lax.ppermute(value, AXES, pairs)  13.9 us
    pallas_call x6, Pallas kernels, call(): pl.pallas_call(kernel, out_shape=shapes, in_specs=[VMEM] * len(operands),...  3.1 us
    ppermute x5, waiting for transfers between devices, swap_core(): return lax.ppermute(value, 'pcol', [(0, 1), (1, 0)])  2.11 us
    reshape x1, local copies, waits for them, and re-layouts, local(): near = anc_inverse.reshape(2 * groups * rows_half, rows_dev).T  1.05 us
  transfers between devices with their start and end apart: 14, of which 10 were waited for; matrix products, arithmetic and copies ran while one was open for 3% of the time, Pallas kernels for 3%

profile of v3, /device:TPU:0, one launch (start us, length us, event | category | flops | bytes accessed | tf_op | source)
XLA Modules:
  0.0 35.2 jit_solution(3174138567007715520)
XLA Ops:
  0.6 3.0 %collective-permute-start.1 = (bf16[3,2,48,128]{3,2,1,0:T(8,128)(2,1)}, bf16[3,2,48,128]{3,2,1,0:T(8,128)(2,1)S(1)}, u32[]{:S(2)}, u32[]{:S(2)}) collective-permute-start(bf16[3,2,48,128]{3,2,1,0:T(8,128)(2,1)} %panels.1), channel_id=1, source_target_pairs={{0,2},{1,3},{2,0},{3,1},{4,6},{5,7},{6,4},{7,5},{8,10},{9,11},{10,... | collective-permute-start | bytes 221192 | tf_op jit(solution)/shard_map/ppermute | solution.py:23
  3.6 0.0 collective-permute-start.5
  3.6 1.1 %copy.7 = bf16[768,96]{0,1:T(8,128)(2,1)S(1)} copy(bf16[768,96]{1,0:T(8,128)(2,1)} %bitcast.21) | data formatting | bytes 294912 | tf_op jit(solution)/shard_map/reshape | solution.py:208
  4.7 0.0 copy-start
  4.7 0.2 collective-permute-start
  4.9 0.0 copy-start.2
  4.9 1.3 %collective-permute-done.1.panels_far = bf16[3,2,48,128]{3,2,1,0:T(8,128)(2,1)S(1)} collective-permute-done((bf16[3,2,48,128]{3,2,1,0:T(8,128)(2,1)}, bf16[3,2,48,128]{3,2,1,0:T(8,128)(2,1)S(1)}, u32[]{:S(2)}, u32[]{:S(2)}) %collective-permute-start.1) | collective-permute-done | bytes 73760 | tf_op jit(solution)/shard_map/ppermute | solution.py:23
  6.2 0.0 copy-done
  6.2 0.0 copy-done.2
  6.2 0.3 shard_map.59
  6.5 2.2 %collective-permute-start.2 = (bf16[2,48,384]{2,1,0:T(8,128)(2,1)S(1)}, bf16[2,48,384]{2,1,0:T(8,128)(2,1)S(1)}, u32[]{:S(2)}, u32[]{:S(2)}) collective-permute-start(bf16[2,48,384]{2,1,0:T(8,128)(2,1)S(1)} %shard_map.59), channel_id=1, source_target_pairs={{0,4},{1,9},{2,6},{3,11},{4,0},{5,13},{6,2},{7,15},{8,12},{9,1},{1... | collective-permute-start | bytes 221192 | tf_op jit(solution)/shard_map/ppermute | solution.py:23
  8.6 2.6 %collective-permute-start.3 = (bf16[2,48,384]{2,1,0:T(8,128)(2,1)S(1)}, bf16[2,48,384]{2,1,0:T(8,128)(2,1)S(1)}, u32[]{:S(2)}, u32[]{:S(2)}) collective-permute-start(bf16[2,48,384]{2,1,0:T(8,128)(2,1)S(1)} %shard_map.59), channel_id=1, source_target_pairs={{0,8},{1,5},{2,10},{3,7},{4,12},{5,1},{6,14},{7,3},{8,0},{9,13},{1... | collective-permute-start | bytes 221192 | tf_op jit(solution)/shard_map/ppermute | solution.py:23
  11.2 0.0 collective-permute-start.4
  11.3 0.4 %collective-permute-done.2 = bf16[2,48,384]{2,1,0:T(8,128)(2,1)S(1)} collective-permute-done((bf16[2,48,384]{2,1,0:T(8,128)(2,1)S(1)}, bf16[2,48,384]{2,1,0:T(8,128)(2,1)S(1)}, u32[]{:S(2)}, u32[]{:S(2)}) %collective-permute-start.2) | collective-permute-done | bytes 73760 | tf_op jit(solution)/shard_map/ppermute | solution.py:23
  11.7 0.0 collective-permute-start.6
  11.7 4.1 %collective-permute-done.3 = bf16[2,48,384]{2,1,0:T(8,128)(2,1)S(1)} collective-permute-done((bf16[2,48,384]{2,1,0:T(8,128)(2,1)S(1)}, bf16[2,48,384]{2,1,0:T(8,128)(2,1)S(1)}, u32[]{:S(2)}, u32[]{:S(2)}) %collective-permute-start.3) | collective-permute-done | bytes 73760 | tf_op jit(solution)/shard_map/ppermute | solution.py:23
  15.8 1.6 %collective-permute-done.4 = bf16[2,48,384]{2,1,0:T(8,128)(2,1)S(1)} collective-permute-done((bf16[2,48,384]{2,1,0:T(8,128)(2,1)S(1)}, bf16[2,48,384]{2,1,0:T(8,128)(2,1)S(1)}, u32[]{:S(2)}, u32[]{:S(2)}) %collective-permute-start.4) | collective-permute-done | bytes 73760 | tf_op jit(solution)/shard_map/ppermute | solution.py:23
  17.4 0.0 collective-permute-done.5.panels_core
  17.4 0.0 collective-permute-done.6.panels_far_core
  17.4 0.0 collective-permute-done.far
  17.4 0.5 %shard_map.60.mine = f32[2,96,384]{2,1,0:T(8,128)S(1)} custom-call(bf16[96,768]{1,0:T(8,128)(2,1)S(1)} %bitcast.14, bf16[96,768]{1,0:T(8,128)(2,1)S(1)} %collective-permute-done.far, bf16[4,2,48,384]{3,2,1,0:T(8,128)(2,1)S(1)} %bitcast_dynamic-update-slice_fusion.held), custom_call_target="tpu_custom_call" | custom-call | tf_op jit(solution)/shard_map/pallas_call | solution.py:41
  17.9 0.1 collective-permute-start.7
  18.0 1.6 %collective-permute-done.7.theirs = f32[2,96,384]{2,1,0:T(8,128)S(1)} collective-permute-done((f32[2,96,384]{2,1,0:T(8,128)S(1)}, f32[2,96,384]{2,1,0:T(8,128)S(1)}, u32[]{:S(2)}, u32[]{:S(2)}) %collective-permute-start.7) | collective-permute-done | bytes 294944 | tf_op jit(solution)/shard_map/ppermute | solution.py:27
  19.6 0.7 %shard_map.61 = (bf16[3,48,128]{2,1,0:T(8,128)(2,1)S(1)}, bf16[3,48,128]{2,1,0:T(8,128)(2,1)S(1)}, f32[3,64,128]{2,1,0:T(8,128)S(1)}) custom-call(s32[3,6]{1,0:T(4,128)S(1)} %copy-done.2, f32[2,96,384]{2,1,0:T(8,128)S(1)} %shard_map.60.mine, f32[2,96,384]{2,1,0:T(8,128)S(1)} %collective-permute-done.7.theirs, bf16[3,2,48,128]{3,2,1,0:T(8,128)(2,1)S(1)} %copy-done, ...), custom_call_target="tpu_custom_call" | custom-call | tf_op jit(solution)/shard_map/pallas_call | solution.py:41
  20.3 1.8 %collective-permute-start.10 = (bf16[192,128]{1,0:T(8,128)(2,1)S(1)}, bf16[192,128]{1,0:T(8,128)(2,1)S(1)}, u32[]{:S(2)}, u32[]{:S(2)}) collective-permute-start(bf16[192,128]{1,0:T(8,128)(2,1)S(1)} %bitcast.15), channel_id=1, source_target_pairs={{0,12},{1,13},{2,14},{3,15},{4,8},{5,9},{6,10},{7,11},{8,4},{9,5},... | collective-permute-start | bytes 147464 | tf_op jit(solution)/shard_map/ppermute | solution.py:23
  22.0 0.4 %collective-permute-start.8 = (bf16[192,128]{1,0:T(8,128)(2,1)S(1)}, bf16[192,128]{1,0:T(8,128)(2,1)S(1)}, u32[]{:S(2)}, u32[]{:S(2)}) collective-permute-start(bf16[192,128]{1,0:T(8,128)(2,1)S(1)} %bitcast.16), channel_id=1, source_target_pairs={{0,4},{1,5},{2,6},{3,7},{4,0},{5,1},{6,2},{7,3},{8,12},{9,13},{10,... | collective-permute-start | bytes 147464 | tf_op jit(solution)/shard_map/ppermute | solution.py:23
  22.5 2.2 %collective-permute-start.9 = (bf16[192,128]{1,0:T(8,128)(2,1)S(1)}, bf16[192,128]{1,0:T(8,128)(2,1)S(1)}, u32[]{:S(2)}, u32[]{:S(2)}) collective-permute-start(bf16[192,128]{1,0:T(8,128)(2,1)S(1)} %bitcast.17), channel_id=1, source_target_pairs={{0,8},{1,9},{2,10},{3,11},{4,12},{5,13},{6,14},{7,15},{8,0},{9,1},... | collective-permute-start | bytes 147464 | tf_op jit(solution)/shard_map/ppermute | solution.py:23
  24.7 1.8 %collective-permute-done.10.refs_3_ = bf16[192,128]{1,0:T(8,128)(2,1)S(1)} collective-permute-done((bf16[192,128]{1,0:T(8,128)(2,1)S(1)}, bf16[192,128]{1,0:T(8,128)(2,1)S(1)}, u32[]{:S(2)}, u32[]{:S(2)}) %collective-permute-start.10) | collective-permute-done | bytes 49184 | tf_op jit(solution)/shard_map/ppermute | solution.py:23
  26.5 0.8 %collective-permute-done.8.refs_1_ = bf16[192,128]{1,0:T(8,128)(2,1)S(1)} collective-permute-done((bf16[192,128]{1,0:T(8,128)(2,1)S(1)}, bf16[192,128]{1,0:T(8,128)(2,1)S(1)}, u32[]{:S(2)}, u32[]{:S(2)}) %collective-permute-start.8) | collective-permute-done | bytes 49184 | tf_op jit(solution)/shard_map/ppermute | solution.py:23
  27.3 0.5 %collective-permute-done.9.refs_2_ = bf16[192,128]{1,0:T(8,128)(2,1)S(1)} collective-permute-done((bf16[192,128]{1,0:T(8,128)(2,1)S(1)}, bf16[192,128]{1,0:T(8,128)(2,1)S(1)}, u32[]{:S(2)}, u32[]{:S(2)}) %collective-permute-start.9) | collective-permute-done | bytes 49184 | tf_op jit(solution)/shard_map/ppermute | solution.py:23
  27.8 1.5 %collective-permute-start.11 = (bf16[528,128]{1,0:T(8,128)(2,1)S(1)}, bf16[528,128]{1,0:T(8,128)(2,1)S(1)}, u32[]{:S(2)}, u32[]{:S(2)}) collective-permute-start(bf16[528,128]{1,0:T(8,128)(2,1)S(1)} %shard_map.62), channel_id=1, source_target_pairs={{0,2},{1,3},{2,0},{3,1},{4,6},{5,7},{6,4},{7,5},{8,10},{9,11},{10,... | collective-permute-start | bytes 405512 | tf_op jit(solution)/shard_map/ppermute | solution.py:23
  29.4 0.0 copy-start.1
  29.4 0.1 collective-permute-start.12
  29.5 3.4 %collective-permute-done.11 = bf16[528,128]{1,0:T(8,128)(2,1)S(1)} collective-permute-done((bf16[528,128]{1,0:T(8,128)(2,1)S(1)}, bf16[528,128]{1,0:T(8,128)(2,1)S(1)}, u32[]{:S(2)}, u32[]{:S(2)}) %collective-permute-start.11) | collective-permute-done | bytes 135200 | tf_op jit(solution)/shard_map/ppermute | solution.py:23
  32.9 0.1 collective-permute-start.13
  33.0 0.7 %shard_map.63 = bf16[3,2,48,128]{3,2,1,0:T(8,128)(2,1)} custom-call(bf16[144,128]{1,0:T(8,128)(2,1)S(1)} %bitcast.20, bf16[144,128]{1,0:T(8,128)(2,1)S(1)} %slice.12.other), custom_call_target="tpu_custom_call" | custom-call | tf_op jit(solution)/shard_map/pallas_call | solution.py:41
  33.8 0.0 collective-permute-done.12.mine_core
  33.8 0.5 %collective-permute-done.13.far_core = bf16[384,128]{1,0:T(8,128)(2,1)S(1)} collective-permute-done((bf16[384,128]{1,0:T(8,128)(2,1)S(1)}, bf16[384,128]{1,0:T(8,128)(2,1)S(1)}, u32[]{:S(2)}, u32[]{:S(2)}) %collective-permute-start.13) | collective-permute-done | bytes 98336 | tf_op jit(solution)/shard_map/ppermute | solution.py:27
  34.3 0.0 copy-done.1
  34.3 0.9 %shard_map.64 = f32[3,2,128,128]{3,2,1,0:T(8,128)} custom-call(bf16[3,2,128,128]{3,2,1,0:T(8,128)(2,1)S(1)} %copy-done.1, bf16[384,128]{1,0:T(8,128)(2,1)S(1)} %slice.13.mine, bf16[384,128]{1,0:T(8,128)(2,1)S(1)} %slice.14.far, bf16[384,128]{1,0:T(8,128)(2,1)S(1)} %collective-permute-done.12.mine_core, bf16[384,128]{1,0:T(8,128)(2,1)S(1)} %collective-permute-done.13.far_core), custom_call_target="tpu_custom_call" | custom-call | tf_op jit(solution)/shard_map/pallas_call | solution.py:41
  (10 shorter events, 0.2 us)
Async XLA Ops:
  0.6 5.5 %collective-permute-start.1 = (bf16[3,2,48,128]{3,2,1,0:T(8,128)(2,1)}, bf16[3,2,48,128]{3,2,1,0:T(8,128)(2,1)S(1)}, u32[]{:S(2)}, u32[]{:S(2)}) collective-permute-start(bf16[3,2,48,128]{3,2,1,0:T(8,128)(2,1)} %panels.1), channel_id=1, source_target_pairs={{0,2},{1,3},{2,0},{3,1},{4,6},{5,7},{6,4},{7,5},{8,10},{9,11},{10,... | collective-permute-start | bytes 221192 | tf_op jit(solution)/shard_map/ppermute | solution.py:23
  3.6 13.8 %collective-permute-start.5 = (bf16[3,2,48,128]{3,2,1,0:T(8,128)(2,1)}, bf16[3,2,48,128]{3,2,1,0:T(8,128)(2,1)S(1)}, u32[]{:S(2)}, u32[]{:S(2)}) collective-permute-start(bf16[3,2,48,128]{3,2,1,0:T(8,128)(2,1)} %panels.1), channel_id=1, source_target_pairs={{0,1},{1,0},{2,3},{3,2},{4,5},{5,4},{6,7},{7,6},{8,9},{9,8},{10,11... | collective-permute-start | bytes 221192 | tf_op jit(solution)/shard_map/ppermute | solution.py:27
  4.7 1.5 %copy-start = (bf16[3,2,48,128]{3,2,1,0:T(8,128)(2,1)S(1)}, bf16[3,2,48,128]{3,2,1,0:T(8,128)(2,1)}, u32[]{:S(2)}) copy-start(bf16[3,2,48,128]{3,2,1,0:T(8,128)(2,1)} %panels.1) | copy-start | bytes 221188
  4.7 12.7 %collective-permute-start = (bf16[96,768]{1,0:T(8,128)(2,1)S(1)}, bf16[96,768]{1,0:T(8,128)(2,1)S(1)}, u32[]{:S(2)}, u32[]{:S(2)}) collective-permute-start(bf16[96,768]{1,0:T(8,128)(2,1)S(1)} %bitcast.13), channel_id=1, source_target_pairs={{0,2},{1,3},{2,0},{3,1},{4,6},{5,7},{6,4},{7,5},{8,10},{9,11},{10,... | collective-permute-start | bytes 442376 | tf_op jit(solution)/shard_map/ppermute | solution.py:23
  4.9 1.3 %copy-start.2 = (s32[3,6]{1,0:T(4,128)S(1)}, s32[3,6]{1,0:T(4,128)}, u32[]{:S(2)}) copy-start(s32[3,6]{1,0:T(4,128)} %structure.3) | copy-start | bytes 220
  6.5 5.2 %collective-permute-start.2 = (bf16[2,48,384]{2,1,0:T(8,128)(2,1)S(1)}, bf16[2,48,384]{2,1,0:T(8,128)(2,1)S(1)}, u32[]{:S(2)}, u32[]{:S(2)}) collective-permute-start(bf16[2,48,384]{2,1,0:T(8,128)(2,1)S(1)} %shard_map.59), channel_id=1, source_target_pairs={{0,4},{1,9},{2,6},{3,11},{4,0},{5,13},{6,2},{7,15},{8,12},{9,1},{1... | collective-permute-start | bytes 221192 | tf_op jit(solution)/shard_map/ppermute | solution.py:23
  8.6 7.2 %collective-permute-start.3 = (bf16[2,48,384]{2,1,0:T(8,128)(2,1)S(1)}, bf16[2,48,384]{2,1,0:T(8,128)(2,1)S(1)}, u32[]{:S(2)}, u32[]{:S(2)}) collective-permute-start(bf16[2,48,384]{2,1,0:T(8,128)(2,1)S(1)} %shard_map.59), channel_id=1, source_target_pairs={{0,8},{1,5},{2,10},{3,7},{4,12},{5,1},{6,14},{7,3},{8,0},{9,13},{1... | collective-permute-start | bytes 221192 | tf_op jit(solution)/shard_map/ppermute | solution.py:23
  11.2 6.2 %collective-permute-start.4 = (bf16[2,48,384]{2,1,0:T(8,128)(2,1)S(1)}, bf16[2,48,384]{2,1,0:T(8,128)(2,1)S(1)}, u32[]{:S(2)}, u32[]{:S(2)}) collective-permute-start(bf16[2,48,384]{2,1,0:T(8,128)(2,1)S(1)} %shard_map.59), channel_id=1, source_target_pairs={{0,12},{1,13},{2,14},{3,15},{4,8},{5,9},{6,10},{7,11},{8,4},{9,5},... | collective-permute-start | bytes 221192 | tf_op jit(solution)/shard_map/ppermute | solution.py:23
  11.7 5.8 %collective-permute-start.6 = (bf16[3,2,48,128]{3,2,1,0:T(8,128)(2,1)S(1)}, bf16[3,2,48,128]{3,2,1,0:T(8,128)(2,1)S(1)}, u32[]{:S(2)}, u32[]{:S(2)}) collective-permute-start(bf16[3,2,48,128]{3,2,1,0:T(8,128)(2,1)S(1)} %collective-permute-done.1.panels_far), channel_id=1, source_target_pairs={{0,1},{1,0},{2,3},{3,2},{4,5},{5,4},{6,7},{7,6},{8,9},{9,8},{10,11... | collective-permute-start | bytes 221192 | tf_op jit(solution)/shard_map/ppermute | solution.py:27
  17.9 1.6 %collective-permute-start.7 = (f32[2,96,384]{2,1,0:T(8,128)S(1)}, f32[2,96,384]{2,1,0:T(8,128)S(1)}, u32[]{:S(2)}, u32[]{:S(2)}) collective-permute-start(f32[2,96,384]{2,1,0:T(8,128)S(1)} %shard_map.60.mine), channel_id=1, source_target_pairs={{0,1},{1,0},{2,3},{3,2},{4,5},{5,4},{6,7},{7,6},{8,9},{9,8},{10,11... | collective-permute-start | bytes 884744 | tf_op jit(solution)/shard_map/ppermute | solution.py:27
  20.3 6.2 %collective-permute-start.10 = (bf16[192,128]{1,0:T(8,128)(2,1)S(1)}, bf16[192,128]{1,0:T(8,128)(2,1)S(1)}, u32[]{:S(2)}, u32[]{:S(2)}) collective-permute-start(bf16[192,128]{1,0:T(8,128)(2,1)S(1)} %bitcast.15), channel_id=1, source_target_pairs={{0,12},{1,13},{2,14},{3,15},{4,8},{5,9},{6,10},{7,11},{8,4},{9,5},... | collective-permute-start | bytes 147464 | tf_op jit(solution)/shard_map/ppermute | solution.py:23
  22.0 5.3 %collective-permute-start.8 = (bf16[192,128]{1,0:T(8,128)(2,1)S(1)}, bf16[192,128]{1,0:T(8,128)(2,1)S(1)}, u32[]{:S(2)}, u32[]{:S(2)}) collective-permute-start(bf16[192,128]{1,0:T(8,128)(2,1)S(1)} %bitcast.16), channel_id=1, source_target_pairs={{0,4},{1,5},{2,6},{3,7},{4,0},{5,1},{6,2},{7,3},{8,12},{9,13},{10,... | collective-permute-start | bytes 147464 | tf_op jit(solution)/shard_map/ppermute | solution.py:23
  22.5 5.3 %collective-permute-start.9 = (bf16[192,128]{1,0:T(8,128)(2,1)S(1)}, bf16[192,128]{1,0:T(8,128)(2,1)S(1)}, u32[]{:S(2)}, u32[]{:S(2)}) collective-permute-start(bf16[192,128]{1,0:T(8,128)(2,1)S(1)} %bitcast.17), channel_id=1, source_target_pairs={{0,8},{1,9},{2,10},{3,11},{4,12},{5,13},{6,14},{7,15},{8,0},{9,1},... | collective-permute-start | bytes 147464 | tf_op jit(solution)/shard_map/ppermute | solution.py:23
  27.8 5.1 %collective-permute-start.11 = (bf16[528,128]{1,0:T(8,128)(2,1)S(1)}, bf16[528,128]{1,0:T(8,128)(2,1)S(1)}, u32[]{:S(2)}, u32[]{:S(2)}) collective-permute-start(bf16[528,128]{1,0:T(8,128)(2,1)S(1)} %shard_map.62), channel_id=1, source_target_pairs={{0,2},{1,3},{2,0},{3,1},{4,6},{5,7},{6,4},{7,5},{8,10},{9,11},{10,... | collective-permute-start | bytes 405512 | tf_op jit(solution)/shard_map/ppermute | solution.py:23
  29.4 4.9 %copy-start.1 = (bf16[3,2,128,128]{3,2,1,0:T(8,128)(2,1)S(1)}, bf16[3,2,128,128]{3,2,1,0:T(8,128)(2,1)}, u32[]{:S(2)}) copy-start(bf16[3,2,128,128]{3,2,1,0:T(8,128)(2,1)} %diag_inverse.1) | copy-start | bytes 589828
  29.4 4.4 %collective-permute-start.12 = (bf16[384,128]{1,0:T(8,128)(2,1)S(1)}, bf16[384,128]{1,0:T(8,128)(2,1)S(1)}, u32[]{:S(2)}, u32[]{:S(2)}) collective-permute-start(bf16[384,128]{1,0:T(8,128)(2,1)S(1)} %slice.13.mine), channel_id=1, source_target_pairs={{0,1},{1,0},{2,3},{3,2},{4,5},{5,4},{6,7},{7,6},{8,9},{9,8},{10,11... | collective-permute-start | bytes 294920 | tf_op jit(solution)/shard_map/ppermute | solution.py:27
  32.9 1.4 %collective-permute-start.13 = (bf16[384,128]{1,0:T(8,128)(2,1)S(1)}, bf16[384,128]{1,0:T(8,128)(2,1)S(1)}, u32[]{:S(2)}, u32[]{:S(2)}) collective-permute-start(bf16[384,128]{1,0:T(8,128)(2,1)S(1)} %slice.14.far), channel_id=1, source_target_pairs={{0,1},{1,0},{2,3},{3,2},{4,5},{5,4},{6,7},{7,6},{8,9},{9,8},{10,11... | collective-permute-start | bytes 294920 | tf_op jit(solution)/shard_map/ppermute | solution.py:27

commit v4 on v3

--- a/solution.py
+++ b/solution.py
@@ -1,4 +1,5 @@
 import functools
+import math
 
 import jax
 import jax.numpy as jnp
@@ -9,7 +10,7 @@
 from jax.sharding import PartitionSpec as P
 
 AXES = ("prow", "pcol")
-MASKS = ((2, 4), (4, 2), (6, 6))
+MASKS = ((6, 6), (2, 4), (4, 2))
 MASKS_SUM = ((2, 2), (4, 4), (6, 6))
 VMEM = pl.BlockSpec(memory_space=pltpu.VMEM)
 
@@ -111,7 +112,7 @@
         ) + jnp.dot(left[:, depth:], imag, preferred_element_type=jnp.float32)
 
 
-def diagonal_kernel(structure, mine, theirs, panels, panels_far, panels_core, panels_far_core, own, far, diag, left, right, full):
+def diagonal_kernel(scale, structure, mine, theirs, panels, panels_far, panels_core, panels_far_core, own, far, diag, left, right, full):
     supernodes, _, rows_half, width = panels.shape
     row_index, col_index = lax.axis_index("prow"), lax.axis_index("pcol")
     rows_dev = 2 * rows_half
@@ -139,7 +140,7 @@
             preferred_element_type=jnp.float32,
         )
     half = width // 2
-    diag[...] = full[:, pl.ds(pl.multiple_of(col_index * half, half), half), :]
+    diag[...] = full[:, pl.ds(pl.multiple_of(col_index * half, half), half), :] * (1.0 / scale)
 
 
 def unpack(near, far):
@@ -148,16 +149,6 @@
     high = jnp.where(parity == 0, far, near)
     first = lax.broadcasted_iota(jnp.int32, near.shape, 1) < near.shape[1] // 2
     return jnp.where(first, low, swap_halves(high)), jnp.where(first, swap_halves(low), high)
-
-
-def sum_kernel(terms, columns, packet):
-    first, second, third, fourth = [term[...].astype(jnp.float32) for term in terms]
-    value = (first + second) + (third + fourth)
-    high = value.astype(jnp.bfloat16)
-    rows = value.shape[0]
-    packet[:rows] = high
-    packet[rows : 2 * rows] = (value - high.astype(jnp.float32)).astype(jnp.bfloat16)
-    packet[2 * rows :] = columns[...]
 
 
 def columns_kernel(own, other, out):
@@ -172,19 +163,15 @@
         out[node, 1] = imag.astype(jnp.bfloat16)
 
 
-def final_kernel(diag_inverse, mine, far, mine_core, far_core, out):
+def final_kernel(scale, diag_inverse, mine, far, mine_core, far_core, out):
     supernodes, _, width, _ = out.shape
     half = width // 2
     col_index = lax.axis_index("pcol")
-
-    def value(ref, node):
-        first, second = node * half, (supernodes + node) * half
-        return ref[first : first + half].astype(jnp.float32) + ref[second : second + half].astype(jnp.float32)
-
     for node in range(supernodes):
+        part = slice(node * half, (node + 1) * half)
         for col, near_ref, far_ref in ((col_index, mine, far), (1 - col_index, mine_core, far_core)):
             rows = pl.ds(pl.multiple_of(col * half, half), half)
-            real, imag = unpack(value(near_ref, node), value(far_ref, node))
+            real, imag = unpack(near_ref[part] * scale, far_ref[part] * scale)
             out[node, 0, rows] = diag_inverse[node, 0, rows].astype(jnp.float32) - real
             out[node, 1, rows] = diag_inverse[node, 1, rows].astype(jnp.float32) - imag
 
@@ -235,40 +222,40 @@
             [near, far, held],
             [pltpu.VMEM(held.shape, bf16)],
         )
+        scale = 2 ** max(0, math.ceil(math.log2(groups * 2 * rows_half / 24)))
         pieces = (supernodes, 2, 2, cols, rows_half, width)
         own, send, diag = call(
-            diagonal_kernel,
+            functools.partial(diagonal_kernel, float(scale)),
             [((supernodes, rows_half, width), bf16)] * 2 + [((supernodes, half, width), f32)],
             [structure, partial, swap_core(partial), panels, panels_far, panels_core, panels_far_core],
             [pltpu.VMEM(pieces, bf16), pltpu.VMEM(pieces, bf16), pltpu.VMEM((supernodes, width, width), f32)],
         )
+        f16 = jnp.float16
         count = supernodes * half
-        term = diag.astype(bf16).reshape(count, width)
+        columns_rows = supernodes * rows_half
+        term = diag.reshape(count, width).astype(f16)
         terms = [term] + [swap(term, rows, cols, mask0, mask1) for mask0, mask1 in MASKS_SUM]
+        first, second, third, fourth = [t.astype(f32) for t in terms]
+        term = (first + second) + (third + fourth)
         size = 8
         while size < rows:
-            first, second, third, fourth = [t.astype(f32) for t in terms]
-            term = (first + second) + (third + fourth)
-            other = swap(term, rows, cols, size, size)
-            terms = [term, other, jnp.zeros_like(term), jnp.zeros_like(term)]
+            term = term + swap(term, rows, cols, size, size)
             size *= 2
-        columns_rows = supernodes * rows_half
-        (packet,) = call(
-            lambda *refs: sum_kernel(refs[:4], refs[4], refs[5]),
-            [((2 * count + columns_rows, width), bf16)],
-            terms + [send.reshape(columns_rows, width)],
-        )
-        other = swap(packet, rows, cols, 1, 1)
-        mine, far = packet[: 2 * count], other[: 2 * count]
+        mine = term.astype(f16)
+        other = swap(
+            jnp.concatenate([mine, send.reshape(columns_rows, width).astype(f16)]), rows, cols, 1, 1
+        )
+        far = other[:count]
         (columns,) = call(
             columns_kernel,
             [((supernodes, 2, rows_half, width), bf16)],
-            [own.reshape(columns_rows, width), other[2 * count :]],
-        )
+            [own.reshape(columns_rows, width), other[count:].astype(f32)],
+        )
+        pieces = [v.astype(f32) for v in (mine, far, swap_core(mine), swap_core(far))]
         (diag,) = call(
-            final_kernel,
+            functools.partial(final_kernel, float(scale)),
             [((supernodes, 2, width, width), f32)],
-            [diag_inverse, mine, far, swap_core(mine), swap_core(far)],
+            [diag_inverse] + pieces,
         )
         return columns, diag
 

time: 35.4 us -> 34.5 us (0.975)
  waiting for transfers between devices: 16 us -> 15 us
    ppermute x9, waiting for transfers between devices: 13.9 us -> 11.7 us  [swap(): return lax.ppermute(value, AXES, pairs)]
    ppermute x5, waiting for transfers between devices: 2.11 us -> 3.25 us  [swap_core(): return lax.ppermute(value, 'pcol', [(0, 1), (1, 0)])]
    pallas_call x6 -> x5, Pallas kernels: 3.1 us -> 3.09 us  [call(): pl.pallas_call(kernel, out_shape=shapes, in_specs=[VMEM] * len(operands),...]
where the time goes in v4:
time: 34.5 us; the launch traced here: 34.3 us
  waiting for transfers between devices  15 us (43%)
  starting transfers between devices  14.2 us (41%)
  Pallas kernels  3.09 us (9%)
  local copies, waits for them, and re-layouts  1.17 us (3%)
  between operations  0.8 us (2%)
    ppermute x9, starting transfers between devices, swap(): return lax.ppermute(value, AXES, pairs)  14 us
    ppermute x9, waiting for transfers between devices, swap(): return lax.ppermute(value, AXES, pairs)  11.7 us
    ppermute x5, waiting for transfers between devices, swap_core(): return lax.ppermute(value, 'pcol', [(0, 1), (1, 0)])  3.25 us
    pallas_call x5, Pallas kernels, call(): pl.pallas_call(kernel, out_shape=shapes, in_specs=[VMEM] * len(operands),...  3.09 us
    reshape x1, local copies, waits for them, and re-layouts, local(): near = anc_inverse.reshape(2 * groups * rows_half, rows_dev).T  1.05 us
  transfers between devices with their start and end apart: 14, of which 10 were waited for; matrix products, arithmetic and copies ran while one was open for 3% of the time, Pallas kernels for 3%

profile of v4, /device:TPU:0, one launch (start us, length us, event | category | flops | bytes accessed | tf_op | source)
XLA Modules:
  0.0 34.3 jit_solution(3181595915590725206)
XLA Ops:
  0.6 3.0 %collective-permute-start.1 = (bf16[3,2,48,128]{3,2,1,0:T(8,128)(2,1)}, bf16[3,2,48,128]{3,2,1,0:T(8,128)(2,1)S(1)}, u32[]{:S(2)}, u32[]{:S(2)}) collective-permute-start(bf16[3,2,48,128]{3,2,1,0:T(8,128)(2,1)} %panels.1), channel_id=1, source_target_pairs={{0,2},{1,3},{2,0},{3,1},{4,6},{5,7},{6,4},{7,5},{8,10},{9,11},{10,... | collective-permute-start | bytes 221192 | tf_op jit(solution)/shard_map/ppermute | solution.py:24
  3.6 0.0 collective-permute-start.5
  3.6 1.1 %copy.7 = bf16[768,96]{0,1:T(8,128)(2,1)S(1)} copy(bf16[768,96]{1,0:T(8,128)(2,1)} %bitcast.18) | data formatting | bytes 294912 | tf_op jit(solution)/shard_map/reshape | solution.py:195
  4.7 0.0 copy-start
  4.7 0.2 collective-permute-start
  4.9 0.0 copy-start.2
  4.9 1.3 %collective-permute-done.1.panels_far = bf16[3,2,48,128]{3,2,1,0:T(8,128)(2,1)S(1)} collective-permute-done((bf16[3,2,48,128]{3,2,1,0:T(8,128)(2,1)}, bf16[3,2,48,128]{3,2,1,0:T(8,128)(2,1)S(1)}, u32[]{:S(2)}, u32[]{:S(2)}) %collective-permute-start.1) | collective-permute-done | bytes 73760 | tf_op jit(solution)/shard_map/ppermute | solution.py:24
  6.2 0.0 copy-done
  6.2 0.0 copy-done.2
  6.2 0.3 shard_map.59
  6.5 4.2 %collective-permute-start.2 = (bf16[2,48,384]{2,1,0:T(8,128)(2,1)S(1)}, bf16[2,48,384]{2,1,0:T(8,128)(2,1)S(1)}, u32[]{:S(2)}, u32[]{:S(2)}) collective-permute-start(bf16[2,48,384]{2,1,0:T(8,128)(2,1)S(1)} %shard_map.59), channel_id=1, source_target_pairs={{0,12},{1,13},{2,14},{3,15},{4,8},{5,9},{6,10},{7,11},{8,4},{9,5},... | collective-permute-start | bytes 221192 | tf_op jit(solution)/shard_map/ppermute | solution.py:24
  10.7 0.0 collective-permute-start.3
  10.7 0.6 %collective-permute-start.4 = (bf16[2,48,384]{2,1,0:T(8,128)(2,1)S(1)}, bf16[2,48,384]{2,1,0:T(8,128)(2,1)S(1)}, u32[]{:S(2)}, u32[]{:S(2)}) collective-permute-start(bf16[2,48,384]{2,1,0:T(8,128)(2,1)S(1)} %shard_map.59), channel_id=1, source_target_pairs={{0,8},{1,5},{2,10},{3,7},{4,12},{5,1},{6,14},{7,3},{8,0},{9,13},{1... | collective-permute-start | bytes 221192 | tf_op jit(solution)/shard_map/ppermute | solution.py:24
  11.4 2.3 %collective-permute-done.2 = bf16[2,48,384]{2,1,0:T(8,128)(2,1)S(1)} collective-permute-done((bf16[2,48,384]{2,1,0:T(8,128)(2,1)S(1)}, bf16[2,48,384]{2,1,0:T(8,128)(2,1)S(1)}, u32[]{:S(2)}, u32[]{:S(2)}) %collective-permute-start.2) | collective-permute-done | bytes 73760 | tf_op jit(solution)/shard_map/ppermute | solution.py:24
  13.7 0.0 collective-permute-start.6
  13.7 2.7 %collective-permute-done.3 = bf16[2,48,384]{2,1,0:T(8,128)(2,1)S(1)} collective-permute-done((bf16[2,48,384]{2,1,0:T(8,128)(2,1)S(1)}, bf16[2,48,384]{2,1,0:T(8,128)(2,1)S(1)}, u32[]{:S(2)}, u32[]{:S(2)}) %collective-permute-start.3) | collective-permute-done | bytes 73760 | tf_op jit(solution)/shard_map/ppermute | solution.py:24
  16.4 0.0 collective-permute-done.4
  16.5 0.0 collective-permute-done.5.panels_core
  16.5 0.0 collective-permute-done.6.panels_far_core
  16.5 0.0 collective-permute-done.far
  16.5 0.5 %shard_map.60.mine = f32[2,96,384]{2,1,0:T(8,128)S(1)} custom-call(bf16[96,768]{1,0:T(8,128)(2,1)S(1)} %bitcast.16, bf16[96,768]{1,0:T(8,128)(2,1)S(1)} %collective-permute-done.far, bf16[4,2,48,384]{3,2,1,0:T(8,128)(2,1)S(1)} %bitcast_dynamic-update-slice_fusion.held), custom_call_target="tpu_custom_call" | custom-call | tf_op jit(solution)/shard_map/pallas_call | solution.py:42
  17.0 0.1 collective-permute-start.7
  17.1 1.6 %collective-permute-done.7.theirs = f32[2,96,384]{2,1,0:T(8,128)S(1)} collective-permute-done((f32[2,96,384]{2,1,0:T(8,128)S(1)}, f32[2,96,384]{2,1,0:T(8,128)S(1)}, u32[]{:S(2)}, u32[]{:S(2)}) %collective-permute-start.7) | collective-permute-done | bytes 294944 | tf_op jit(solution)/shard_map/ppermute | solution.py:28
  18.6 0.7 %shard_map.61 = (bf16[3,48,128]{2,1,0:T(8,128)(2,1)S(1)}, bf16[3,48,128]{2,1,0:T(8,128)(2,1)S(1)}, f32[3,64,128]{2,1,0:T(8,128)S(1)}) custom-call(s32[3,6]{1,0:T(4,128)S(1)} %copy-done.2, f32[2,96,384]{2,1,0:T(8,128)S(1)} %shard_map.60.mine, f32[2,96,384]{2,1,0:T(8,128)S(1)} %collective-permute-done.7.theirs, bf16[3,2,48,128]{3,2,1,0:T(8,128)(2,1)S(1)} %copy-done, ...), custom_call_target="tpu_custom_call" | custom-call | tf_op jit(solution)/shard_map/pallas_call | solution.py:42
  19.3 2.5 %collective-permute-start.10 = (f16[192,128]{1,0:T(8,128)(2,1)S(1)}, f16[192,128]{1,0:T(8,128)(2,1)S(1)}, u32[]{:S(2)}, u32[]{:S(2)}) collective-permute-start(f16[192,128]{1,0:T(8,128)(2,1)S(1)} %bitcast.20), channel_id=1, source_target_pairs={{0,12},{1,13},{2,14},{3,15},{4,8},{5,9},{6,10},{7,11},{8,4},{9,5},... | collective-permute-start | bytes 147464 | tf_op jit(solution)/shard_map/ppermute | solution.py:24
  21.8 0.1 collective-permute-start.8
  21.9 1.8 %collective-permute-start.9 = (f16[192,128]{1,0:T(8,128)(2,1)S(1)}, f16[192,128]{1,0:T(8,128)(2,1)S(1)}, u32[]{:S(2)}, u32[]{:S(2)}) collective-permute-start(f16[192,128]{1,0:T(8,128)(2,1)S(1)} %bitcast.22), channel_id=1, source_target_pairs={{0,8},{1,9},{2,10},{3,11},{4,12},{5,13},{6,14},{7,15},{8,0},{9,1},... | collective-permute-start | bytes 147464 | tf_op jit(solution)/shard_map/ppermute | solution.py:24
  23.8 1.7 %collective-permute-done.10 = f16[192,128]{1,0:T(8,128)(2,1)S(1)} collective-permute-done((f16[192,128]{1,0:T(8,128)(2,1)S(1)}, f16[192,128]{1,0:T(8,128)(2,1)S(1)}, u32[]{:S(2)}, u32[]{:S(2)}) %collective-permute-start.10) | collective-permute-done | bytes 49184 | tf_op jit(solution)/shard_map/ppermute | solution.py:24
  25.5 1.1 %collective-permute-done.8 = f16[192,128]{1,0:T(8,128)(2,1)S(1)} collective-permute-done((f16[192,128]{1,0:T(8,128)(2,1)S(1)}, f16[192,128]{1,0:T(8,128)(2,1)S(1)}, u32[]{:S(2)}, u32[]{:S(2)}) %collective-permute-start.8) | collective-permute-done | bytes 49184 | tf_op jit(solution)/shard_map/ppermute | solution.py:24
  26.7 0.7 %collective-permute-done.9 = f16[192,128]{1,0:T(8,128)(2,1)S(1)} collective-permute-done((f16[192,128]{1,0:T(8,128)(2,1)S(1)}, f16[192,128]{1,0:T(8,128)(2,1)S(1)}, u32[]{:S(2)}, u32[]{:S(2)}) %collective-permute-start.9) | collective-permute-done | bytes 49184 | tf_op jit(solution)/shard_map/ppermute | solution.py:24
  27.5 1.6 %collective-permute-start.11 = (f16[336,128]{1,0:T(8,128)(2,1)S(1)}, f16[336,128]{1,0:T(8,128)(2,1)S(1)}, u32[]{:S(2)}, u32[]{:S(2)}) collective-permute-start(f16[336,128]{1,0:T(8,128)(2,1)S(1)} %pad_maximum_fusion), channel_id=1, source_target_pairs={{0,2},{1,3},{2,0},{3,1},{4,6},{5,7},{6,4},{7,5},{8,10},{9,11},{10,... | collective-permute-start | bytes 258056 | tf_op jit(solution)/shard_map/ppermute | solution.py:24
  29.1 0.0 collective-permute-start.12
  29.1 1.2 %collective-permute-done.12 = f16[192,128]{1,0:T(8,128)(2,1)S(1)} collective-permute-done((f16[192,128]{1,0:T(8,128)(2,1)S(1)}, f16[192,128]{1,0:T(8,128)(2,1)S(1)}, u32[]{:S(2)}, u32[]{:S(2)}) %collective-permute-start.12) | collective-permute-done | bytes 49184 | tf_op jit(solution)/shard_map/ppermute | solution.py:28
  30.3 1.7 %collective-permute-done.11 = f16[336,128]{1,0:T(8,128)(2,1)S(1)} collective-permute-done((f16[336,128]{1,0:T(8,128)(2,1)S(1)}, f16[336,128]{1,0:T(8,128)(2,1)S(1)}, u32[]{:S(2)}, u32[]{:S(2)}) %collective-permute-start.11) | collective-permute-done | bytes 86048 | tf_op jit(solution)/shard_map/ppermute | solution.py:24
  32.1 0.1 collective-permute-start.13
  32.2 0.0 copy-start.1
  32.2 0.7 %shard_map.62 = bf16[3,2,48,128]{3,2,1,0:T(8,128)(2,1)} custom-call(bf16[144,128]{1,0:T(8,128)(2,1)S(1)} %bitcast.17, f32[144,128]{1,0:T(8,128)S(1)} %slice_convert_fusion.other), custom_call_target="tpu_custom_call" | custom-call | tf_op jit(solution)/shard_map/pallas_call | solution.py:42
  32.9 0.5 %collective-permute-done.13 = f16[192,128]{1,0:T(8,128)(2,1)S(1)} collective-permute-done((f16[192,128]{1,0:T(8,128)(2,1)S(1)}, f16[192,128]{1,0:T(8,128)(2,1)S(1)}, u32[]{:S(2)}, u32[]{:S(2)}) %collective-permute-start.13) | collective-permute-done | bytes 49184 | tf_op jit(solution)/shard_map/ppermute | solution.py:28
  33.4 0.0 copy-done.1
  33.4 0.9 %shard_map.63 = f32[3,2,128,128]{3,2,1,0:T(8,128)} custom-call(bf16[3,2,128,128]{3,2,1,0:T(8,128)(2,1)S(1)} %copy-done.1, f32[192,128]{1,0:T(8,128)S(1)} %get-tuple-element.10.mine, f32[192,128]{1,0:T(8,128)S(1)} %get-tuple-element.13.far, f32[192,128]{1,0:T(8,128)S(1)} %convert_element_type.54.mine_core, f32[192,128]{1,0:T(8,128)S(1)} %convert_element_type.55.far_core), custom_call_target="tpu_custom_call" | custom-call | tf_op jit(solution)/shard_map/pallas_call | solution.py:42
  (13 shorter events, 0.2 us)
Async XLA Ops:
  0.6 5.5 %collective-permute-start.1 = (bf16[3,2,48,128]{3,2,1,0:T(8,128)(2,1)}, bf16[3,2,48,128]{3,2,1,0:T(8,128)(2,1)S(1)}, u32[]{:S(2)}, u32[]{:S(2)}) collective-permute-start(bf16[3,2,48,128]{3,2,1,0:T(8,128)(2,1)} %panels.1), channel_id=1, source_target_pairs={{0,2},{1,3},{2,0},{3,1},{4,6},{5,7},{6,4},{7,5},{8,10},{9,11},{10,... | collective-permute-start | bytes 221192 | tf_op jit(solution)/shard_map/ppermute | solution.py:24
  3.6 12.9 %collective-permute-start.5 = (bf16[3,2,48,128]{3,2,1,0:T(8,128)(2,1)}, bf16[3,2,48,128]{3,2,1,0:T(8,128)(2,1)S(1)}, u32[]{:S(2)}, u32[]{:S(2)}) collective-permute-start(bf16[3,2,48,128]{3,2,1,0:T(8,128)(2,1)} %panels.1), channel_id=1, source_target_pairs={{0,1},{1,0},{2,3},{3,2},{4,5},{5,4},{6,7},{7,6},{8,9},{9,8},{10,11... | collective-permute-start | bytes 221192 | tf_op jit(solution)/shard_map/ppermute | solution.py:28
  4.7 1.5 %copy-start = (bf16[3,2,48,128]{3,2,1,0:T(8,128)(2,1)S(1)}, bf16[3,2,48,128]{3,2,1,0:T(8,128)(2,1)}, u32[]{:S(2)}) copy-start(bf16[3,2,48,128]{3,2,1,0:T(8,128)(2,1)} %panels.1) | copy-start | bytes 221188
  4.7 11.8 %collective-permute-start = (bf16[96,768]{1,0:T(8,128)(2,1)S(1)}, bf16[96,768]{1,0:T(8,128)(2,1)S(1)}, u32[]{:S(2)}, u32[]{:S(2)}) collective-permute-start(bf16[96,768]{1,0:T(8,128)(2,1)S(1)} %bitcast.15), channel_id=1, source_target_pairs={{0,2},{1,3},{2,0},{3,1},{4,6},{5,7},{6,4},{7,5},{8,10},{9,11},{10,... | collective-permute-start | bytes 442376 | tf_op jit(solution)/shard_map/ppermute | solution.py:24
  4.9 1.3 %copy-start.2 = (s32[3,6]{1,0:T(4,128)S(1)}, s32[3,6]{1,0:T(4,128)}, u32[]{:S(2)}) copy-start(s32[3,6]{1,0:T(4,128)} %structure.3) | copy-start | bytes 220
  6.5 7.2 %collective-permute-start.2 = (bf16[2,48,384]{2,1,0:T(8,128)(2,1)S(1)}, bf16[2,48,384]{2,1,0:T(8,128)(2,1)S(1)}, u32[]{:S(2)}, u32[]{:S(2)}) collective-permute-start(bf16[2,48,384]{2,1,0:T(8,128)(2,1)S(1)} %shard_map.59), channel_id=1, source_target_pairs={{0,12},{1,13},{2,14},{3,15},{4,8},{5,9},{6,10},{7,11},{8,4},{9,5},... | collective-permute-start | bytes 221192 | tf_op jit(solution)/shard_map/ppermute | solution.py:24
  10.7 5.8 %collective-permute-start.3 = (bf16[2,48,384]{2,1,0:T(8,128)(2,1)S(1)}, bf16[2,48,384]{2,1,0:T(8,128)(2,1)S(1)}, u32[]{:S(2)}, u32[]{:S(2)}) collective-permute-start(bf16[2,48,384]{2,1,0:T(8,128)(2,1)S(1)} %shard_map.59), channel_id=1, source_target_pairs={{0,4},{1,9},{2,6},{3,11},{4,0},{5,13},{6,2},{7,15},{8,12},{9,1},{1... | collective-permute-start | bytes 221192 | tf_op jit(solution)/shard_map/ppermute | solution.py:24
  10.7 5.8 %collective-permute-start.4 = (bf16[2,48,384]{2,1,0:T(8,128)(2,1)S(1)}, bf16[2,48,384]{2,1,0:T(8,128)(2,1)S(1)}, u32[]{:S(2)}, u32[]{:S(2)}) collective-permute-start(bf16[2,48,384]{2,1,0:T(8,128)(2,1)S(1)} %shard_map.59), channel_id=1, source_target_pairs={{0,8},{1,5},{2,10},{3,7},{4,12},{5,1},{6,14},{7,3},{8,0},{9,13},{1... | collective-permute-start | bytes 221192 | tf_op jit(solution)/shard_map/ppermute | solution.py:24
  13.7 2.8 %collective-permute-start.6 = (bf16[3,2,48,128]{3,2,1,0:T(8,128)(2,1)S(1)}, bf16[3,2,48,128]{3,2,1,0:T(8,128)(2,1)S(1)}, u32[]{:S(2)}, u32[]{:S(2)}) collective-permute-start(bf16[3,2,48,128]{3,2,1,0:T(8,128)(2,1)S(1)} %collective-permute-done.1.panels_far), channel_id=1, source_target_pairs={{0,1},{1,0},{2,3},{3,2},{4,5},{5,4},{6,7},{7,6},{8,9},{9,8},{10,11... | collective-permute-start | bytes 221192 | tf_op jit(solution)/shard_map/ppermute | solution.py:28
  17.0 1.6 %collective-permute-start.7 = (f32[2,96,384]{2,1,0:T(8,128)S(1)}, f32[2,96,384]{2,1,0:T(8,128)S(1)}, u32[]{:S(2)}, u32[]{:S(2)}) collective-permute-start(f32[2,96,384]{2,1,0:T(8,128)S(1)} %shard_map.60.mine), channel_id=1, source_target_pairs={{0,1},{1,0},{2,3},{3,2},{4,5},{5,4},{6,7},{7,6},{8,9},{9,8},{10,11... | collective-permute-start | bytes 884744 | tf_op jit(solution)/shard_map/ppermute | solution.py:28
  19.3 6.2 %collective-permute-start.10 = (f16[192,128]{1,0:T(8,128)(2,1)S(1)}, f16[192,128]{1,0:T(8,128)(2,1)S(1)}, u32[]{:S(2)}, u32[]{:S(2)}) collective-permute-start(f16[192,128]{1,0:T(8,128)(2,1)S(1)} %bitcast.20), channel_id=1, source_target_pairs={{0,12},{1,13},{2,14},{3,15},{4,8},{5,9},{6,10},{7,11},{8,4},{9,5},... | collective-permute-start | bytes 147464 | tf_op jit(solution)/shard_map/ppermute | solution.py:24
  21.8 4.9 %collective-permute-start.8 = (f16[192,128]{1,0:T(8,128)(2,1)S(1)}, f16[192,128]{1,0:T(8,128)(2,1)S(1)}, u32[]{:S(2)}, u32[]{:S(2)}) collective-permute-start(f16[192,128]{1,0:T(8,128)(2,1)S(1)} %bitcast.21), channel_id=1, source_target_pairs={{0,4},{1,5},{2,6},{3,7},{4,0},{5,1},{6,2},{7,3},{8,12},{9,13},{10,... | collective-permute-start | bytes 147464 | tf_op jit(solution)/shard_map/ppermute | solution.py:24
  21.9 5.5 %collective-permute-start.9 = (f16[192,128]{1,0:T(8,128)(2,1)S(1)}, f16[192,128]{1,0:T(8,128)(2,1)S(1)}, u32[]{:S(2)}, u32[]{:S(2)}) collective-permute-start(f16[192,128]{1,0:T(8,128)(2,1)S(1)} %bitcast.22), channel_id=1, source_target_pairs={{0,8},{1,9},{2,10},{3,11},{4,12},{5,13},{6,14},{7,15},{8,0},{9,1},... | collective-permute-start | bytes 147464 | tf_op jit(solution)/shard_map/ppermute | solution.py:24
  27.5 4.6 %collective-permute-start.11 = (f16[336,128]{1,0:T(8,128)(2,1)S(1)}, f16[336,128]{1,0:T(8,128)(2,1)S(1)}, u32[]{:S(2)}, u32[]{:S(2)}) collective-permute-start(f16[336,128]{1,0:T(8,128)(2,1)S(1)} %pad_maximum_fusion), channel_id=1, source_target_pairs={{0,2},{1,3},{2,0},{3,1},{4,6},{5,7},{6,4},{7,5},{8,10},{9,11},{10,... | collective-permute-start | bytes 258056 | tf_op jit(solution)/shard_map/ppermute | solution.py:24
  29.1 1.2 %collective-permute-start.12 = (f16[192,128]{1,0:T(8,128)(2,1)S(1)}, f16[192,128]{1,0:T(8,128)(2,1)S(1)}, u32[]{:S(2)}, u32[]{:S(2)}) collective-permute-start(f16[192,128]{1,0:T(8,128)(2,1)S(1)} %get-tuple-element.11), channel_id=1, source_target_pairs={{0,1},{1,0},{2,3},{3,2},{4,5},{5,4},{6,7},{7,6},{8,9},{9,8},{10,11... | collective-permute-start | bytes 147464 | tf_op jit(solution)/shard_map/ppermute | solution.py:28
  32.1 1.3 %collective-permute-start.13 = (f16[192,128]{1,0:T(8,128)(2,1)S(1)}, f16[192,128]{1,0:T(8,128)(2,1)S(1)}, u32[]{:S(2)}, u32[]{:S(2)}) collective-permute-start(f16[192,128]{1,0:T(8,128)(2,1)S(1)} %get-tuple-element.12), channel_id=1, source_target_pairs={{0,1},{1,0},{2,3},{3,2},{4,5},{5,4},{6,7},{7,6},{8,9},{9,8},{10,11... | collective-permute-start | bytes 147464 | tf_op jit(solution)/shard_map/ppermute | solution.py:28
  32.2 1.2 %copy-start.1 = (bf16[3,2,128,128]{3,2,1,0:T(8,128)(2,1)S(1)}, bf16[3,2,128,128]{3,2,1,0:T(8,128)(2,1)}, u32[]{:S(2)}) copy-start(bf16[3,2,128,128]{3,2,1,0:T(8,128)(2,1)} %diag_inverse.1) | copy-start | bytes 589828

commit v5 on v4

v5 whole, which is shorter than its diff:
```python
import functools
import math

import jax
import jax.numpy as jnp
from jax import lax
from jax.experimental import pallas as pl
from jax.experimental.layout import Layout, with_layout_constraint
from jax.experimental.pallas import tpu as pltpu
from jax.sharding import PartitionSpec as P

AXES = ("prow", "pcol")
MASKS = (2, 4, 6)
MASKS_SUM = (6, 4, 2)
VMEM = pl.BlockSpec(memory_space=pltpu.VMEM)
HBM = pl.BlockSpec(memory_space=pltpu.HBM)


def swap(value, rows, cols, mask0, mask1):
    pairs = []
    for row in range(rows):
        for col in range(cols):
            mask = mask0 if col == 0 else mask1
            pairs.append((row * cols + col, (row ^ mask) * cols + col))
    return lax.ppermute(value, AXES, pairs)


def swap_core(value):
    return lax.ppermute(value, "pcol", [(0, 1), (1, 0)])


def after(value, *others):
    return lax.optimization_barrier((value,) + others)[0]


def plain(value):
    return with_layout_constraint(value, Layout(tuple(range(value.ndim))))


def call(kernel, outs, operands, scratch=(), cost=0, space=VMEM, limit=0):
    shapes = [jax.ShapeDtypeStruct(shape, dtype) for shape, dtype in outs]
    size = sum(v.size * v.dtype.itemsize for v in list(operands) + shapes)
    return pl.pallas_call(
        kernel,
        out_shape=shapes,
        in_specs=[space] * len(operands),
        out_specs=[VMEM] * len(shapes),
        scratch_shapes=list(scratch),
        cost_estimate=pl.CostEstimate(flops=0, bytes_accessed=cost or size, transcendentals=0),
        compiler_params=pltpu.CompilerParams(vmem_limit_bytes=limit or 2 * size + (4 << 20)),
    )(*operands)


def keep_rows(structure, node, start, count, width):
    blocks = structure.shape[1]
    row = start + lax.broadcasted_iota(jnp.int32, (count, blocks), 0)
    hit = row // width == lax.broadcasted_iota(jnp.int32, (count, blocks), 1)
    table = structure[node : node + 1, :].astype(jnp.float32)
    return jnp.sum(jnp.where(hit, table, 0.0), axis=1, keepdims=True)


def swap_halves(value):
    half = value.shape[-1] // 2
    return jnp.concatenate([value[:, half:], value[:, :half]], axis=-1)


def turned(value):
    lane = lax.broadcasted_iota(jnp.int32, value.shape, 1)
    other = swap_halves(value)
    return jnp.where(lane < value.shape[-1] // 2, -other, other)


def packed(source, node, low, parity):
    real = source[node, 0].astype(jnp.float32)
    imag = source[node, 1].astype(jnp.float32)
    left = jnp.where(low, real, swap_halves(imag))
    right = jnp.where(low, swap_halves(real), imag)
    return jnp.where(parity == 0, left, right)


def first_kernel(
    matrix_in, panels_in, diag_in, structure_in, across, panels, diag_inverse, keep, keep_far, own, matrix, structure, done
):
    pairs = ((panels_in, panels), (structure_in, structure), (matrix_in, matrix), (diag_in, diag_inverse))
    copies = [pltpu.make_async_copy(*pair, done.at[index]) for index, pair in enumerate(pairs)]
    for copy in copies:
        copy.start()
    for copy in copies:
        copy.wait()
    supernodes, _, rows_half, width = panels.shape
    groups, rows_dev = matrix.shape[1], matrix.shape[4]
    row_index, col_index = lax.axis_index("prow"), lax.axis_index("pcol")
    for part in range(2):
        across[part] = matrix[part].reshape(groups * rows_half, rows_dev).T
    low = lax.broadcasted_iota(jnp.int32, (rows_half, width), 1) < width // 2
    for node in range(supernodes):
        lanes = slice(node * width, (node + 1) * width)
        for far_or in range(2):
            start = (row_index ^ far_or) * rows_dev
            value = keep_rows(structure, node, start, rows_dev, width)
            keep[far_or, :, node : node + 1] = value
            part = keep_rows(structure, node, start + col_index * rows_half, rows_half, width)
            if far_or == 0:
                own[:, lanes] = (packed(panels, node, low, row_index % 2) * part).astype(jnp.bfloat16)
            else:
                keep_far[:, node : node + 1] = part


def pick_kernel(own, keep_far, panels_far, block):
    supernodes, _, rows_half, width = panels_far.shape
    parity = lax.axis_index("prow") % 2
    low = lax.broadcasted_iota(jnp.int32, (rows_half, width), 1) < width // 2
    block[parity] = own[...]
    for node in range(supernodes):
        lanes = slice(node * width, (node + 1) * width)
        value = packed(panels_far, node, low, parity) * keep_far[:, node : node + 1]
        block[1 - parity, :, lanes] = value.astype(jnp.bfloat16)


def merge_kernel(block, block_core, near, near_core, chip, first, second):
    carry = lax.axis_index("pcol") == 0
    _, rows_half, _ = block.shape
    for core, source in ((0, block_core), (1, block)):
        for x in range(2):
            rows = slice(x * rows_half, (x + 1) * rows_half)
            chip[core, rows] = source[x]
            first[core, rows] = jnp.where(carry, near[core, rows], source[x])
            second[core, rows] = jnp.where(carry, near_core[core, rows], source[x])


def product_kernel(width, near, near_core, far_0, far_1, held, out):
    count, _, rows_dev, lanes = held.shape
    depth = count * rows_dev
    rights = [held[:, core].reshape(depth, lanes) for core in range(2)]
    for far_or, lefts in ((0, (near_core, near)), (1, (far_0, far_1))):
        real, imag = [
            sum(
                jnp.dot(left[part], right, preferred_element_type=jnp.float32)
                for left, right in zip(lefts, rights)
            )
            for part in range(2)
        ]
        for node in range(lanes // width):
            part = slice(node * width, (node + 1) * width)
            out[far_or, :, part] = real[:, part] + turned(imag[:, part])


def left_kernel(panels, panels_far, panels_core, panels_far_core, out, rows):
    supernodes, _, rows_half, width = panels.shape
    for node in range(supernodes):
        for part in range(2):
            for far_or, (same, cross) in ((0, (panels, panels_core)), (1, (panels_far, panels_far_core))):
                rows[far_or, 0] = cross[node, part]
                rows[far_or, 1] = same[node, part]
            out[node, part] = rows[...].reshape(4 * rows_half, width).T


def diagonal_kernel(scale, kept, product, left, own, send, diag, columns):
    supernodes, _, width, _ = left.shape
    rows_dev = product.shape[1]
    rows_half = rows_dev // 2
    for node in range(supernodes):
        lanes = slice(node * width, (node + 1) * width)
        for far_or in range(2):
            keep = kept[far_or, :, node : node + 1]
            value = (-(product[far_or, :, lanes] * keep)).astype(jnp.bfloat16)
            columns[far_or] = value
            low, high = value[:rows_half], value[rows_half:]
            if far_or == 0:
                send[0, node], own[node] = low, high
            else:
                send[1, node], send[2, node] = low, high
        right = columns[...].reshape(2 * rows_dev, width)
        real = jnp.dot(left[node, 0], right, preferred_element_type=jnp.float32)
        imag = jnp.dot(left[node, 1], right, preferred_element_type=jnp.float32)
        diag[node] = (real + turned(imag)) * (1.0 / scale)


def unpack(near, far):
    parity = lax.axis_index("prow") % 2
    low = jnp.where(parity == 0, near, far)
    high = jnp.where(parity == 0, far, near)
    first = lax.broadcasted_iota(jnp.int32, near.shape, 1) < near.shape[1] // 2
    return jnp.where(first, low, swap_halves(high)), jnp.where(first, swap_halves(low), high)


def columns_kernel(own, own_core, other, other_core, out):
    supernodes, _, rows_half, width = out.shape
    first = lax.axis_index("pcol") == 0
    for node in range(supernodes):
        rows = slice(node * rows_half, (node + 1) * rows_half)
        near = jnp.where(first, own_core[rows].astype(jnp.float32), own[rows].astype(jnp.float32))
        far = jnp.where(first, other[rows], other_core[rows])
        real, imag = unpack(near, far)
        out[node, 0] = real.astype(jnp.bfloat16)
        out[node, 1] = imag.astype(jnp.bfloat16)


def final_kernel(scale, diag_inverse, mine, far, mine_core, far_core, out):
    supernodes, _, width, _ = out.shape
    first = lax.axis_index("pcol") == 0
    for node in range(supernodes):
        rows = slice(node * width, (node + 1) * width)
        near_value = jnp.where(first, mine_core[rows], mine[rows]) * scale
        far_value = jnp.where(first, far_core[rows], far[rows]) * scale
        real, imag = unpack(near_value, far_value)
        out[node, 0] = diag_inverse[node, 0].astype(jnp.float32) - real
        out[node, 1] = diag_inverse[node, 1].astype(jnp.float32) - imag


def solution(mesh):
    rows, cols = mesh.shape["prow"], mesh.shape["pcol"]

    def local(anc_inverse, panels, diag_inverse, structure):
        supernodes, _, rows_half, width = panels.shape
        half = width // 2
        groups = anc_inverse.shape[1]
        rows_dev = anc_inverse.shape[4]
        lanes = supernodes * width
        row_index = lax.axis_index("prow")
        col_index = lax.axis_index("pcol")
        here = row_index // 2
        bf16, f32 = jnp.bfloat16, jnp.float32

        panels = plain(panels)
        panels_far = plain(swap(panels, rows, cols, 1, 1))
        chip_shape = (2, rows_dev, lanes)
        shape = (2, rows_dev, groups * rows_half)
        near, panels, diag_inverse, keep, keep_far, own = call(
            first_kernel,
            [
                (shape, bf16),
                (panels.shape, bf16),
                (diag_inverse.shape, bf16),
                ((2, rows_dev, 128), f32),
                ((rows_half, 128), f32),
                ((rows_half, lanes), bf16),
            ],
            [pltpu.with_memory_space_constraint(v, pltpu.HBM) for v in (anc_inverse, panels, diag_inverse, structure)],
            [
                pltpu.VMEM(anc_inverse.shape, bf16),
                pltpu.VMEM(structure.shape, jnp.int32),
                pltpu.SemaphoreType.DMA((4,)),
            ],
            cost=12 << 20,
            space=HBM,
        )
        near_core = swap_core(near)
        panels_core = swap_core(panels)
        (block,) = call(pick_kernel, [((2, rows_half, lanes), bf16)], [own, keep_far, panels_far])
        if shape == chip_shape:
            chip, first, second = call(
                merge_kernel, [(chip_shape, bf16)] * 3, [block, swap_core(block), near, near_core]
            )
            far_0 = far_1 = None
        else:
            chip = first = second = jnp.stack([swap_core(block), block]).reshape(chip_shape)
            far_1 = swap(near, rows, cols, 1, 1)
            far_0 = swap_core(far_1)
        held = jnp.zeros((rows // 2,) + chip_shape, bf16)
        held = lax.dynamic_update_index_in_dim(held, chip, here, 0)
        arrived = [swap(value, rows, cols, 1, mask) for value, mask in zip((first, second, chip), MASKS)]
        if far_0 is None:
            far_0, far_1 = swap_core(arrived[0]), swap_core(arrived[1])
        panels_far_core = swap_core(panels_far)
        (left,) = call(
            left_kernel,
            [((supernodes, 2, width, 2 * rows_dev), bf16)],
            [panels, panels_far, panels_core, panels_far_core],
            [pltpu.VMEM((2, cols, rows_half, width), bf16)],
            cost=6 << 20,
        )
        for index, (mask, value) in enumerate(zip(MASKS, arrived)):
            held = lax.dynamic_update_index_in_dim(held, value, here ^ (mask // 2), 0)
            held = after(held, left) if index == 0 else held
        size = 8
        while size < rows:
            count = size // 2
            start = (here // count) * count
            own = lax.dynamic_slice_in_dim(held, start, count, 0)
            other = swap(own, rows, cols, 1, size)
            held = lax.dynamic_update_slice_in_dim(held, other, start ^ count, 0)
            size *= 2

        (product,) = call(
            functools.partial(product_kernel, width),
            [((2, rows_dev, lanes), f32)],
            [near, near_core, far_0, far_1, held],
        )
        scale = 2 ** max(0, math.ceil(math.log2(groups * 2 * rows_half / 24)))
        own, send, diag = call(
            functools.partial(diagonal_kernel, float(scale)),
            [
                ((supernodes, rows_half, width), bf16),
                ((3, supernodes, rows_half, width), bf16),
                ((supernodes, width, width), f32),
            ],
            [keep, product, left],
            [pltpu.VMEM((2, rows_dev, width), bf16)],
        )
        f16 = jnp.float16
        count = supernodes * width
        some = supernodes * rows_half
        term = diag.reshape(count, width).astype(f16)
        sent = swap_core(send.reshape(3 * some, width))
        last = jnp.concatenate([sent[some:].astype(f16), term[2 * some :]])
        last = jnp.where(col_index == 0, last, term)
        terms = [swap(v, rows, cols, 1, mask) for mask, v in zip(MASKS_SUM, (term, term, last))]
        other = terms[2]
        first, second, third = [t.astype(f32) for t in terms]
        total = (term.astype(f32) + first) + (second + third)
        size = 8
        while size < rows:
            total = total + swap(total, rows, cols, 1, size)
            size *= 2
        mine = total.astype(f16)
        far = swap(mine, rows, cols, 2, 1)
        (columns,) = call(
            columns_kernel,
            [((supernodes, 2, rows_half, width), bf16)],
            [own.reshape(some, width), sent[:some], other[:some].astype(f32), swap_core(other[some : 2 * some]).astype(f32)],
            cost=4 << 20,
        )
        far_sent = far
        far_sent = after(far, columns)
        pieces = [v.astype(f32) for v in (mine, far, swap_core(mine), swap_core(far_sent))]
        (diag,) = call(
            functools.partial(final_kernel, float(scale)),
            [((supernodes, 2, width, width), f32)],
            [diag_inverse] + pieces,
        )
        return columns, diag

    in_specs = (
        P("pole", None, "pcol", None, "prow"),
        P("pole", None, ("prow", "pcol"), None),
        P("pole", None, None, None),
        P(),
    )
    out_specs = (P("pole", None, ("prow", "pcol"), None), P("pole", None, None, None))
    return jax.shard_map(local, mesh=mesh, in_specs=in_specs, out_specs=out_specs, check_vma=False)
```

time: 34.5 us -> 33.6 us (0.974)
  waiting for transfers between devices: 15 us -> 11.2 us
  starting transfers between devices: 14.2 us -> 16.4 us
  Pallas kernels: 3.09 us -> 4.56 us
  local copies, waits for them, and re-layouts: 1.17 us -> 0.17 us
    ppermute x9 -> x8, waiting for transfers between devices: 11.7 us -> 8.03 us  [swap(): return lax.ppermute(value, AXES, pairs)]
    ppermute x5 -> x10, starting transfers between devices: 0.15 us -> 3.56 us  [swap_core(): return lax.ppermute(value, 'pcol', [(0, 1), (1, 0)])]
    pallas_call x5 -> x8, Pallas kernels: 3.09 us -> 4.56 us  [call(): pl.pallas_call(kernel, out_shape=shapes, in_specs=[space] * len(operands)...]
    ppermute x9 -> x8, starting transfers between devices: 14 us -> 12.9 us  [swap(): return lax.ppermute(value, AXES, pairs)]
    reshape x1 -> x0, local copies, waits for them, and re-layouts: 1.05 us -> none  [local(): near = anc_inverse.reshape(2 * groups * rows_half, rows_dev).T]
    ppermute x5 -> x10, waiting for transfers between devices: 3.25 us -> 3.2 us  [swap_core(): return lax.ppermute(value, 'pcol', [(0, 1), (1, 0)])]
  transfers between devices with their start and end apart: 14 -> 18, of which waited for: 10 -> 12; matrix products, arithmetic and copies ran while one was open for 3% -> 1% of each run, Pallas kernels for 3% -> 8%
where the time goes in v5:
time: 33.6 us; the launch traced here: 33.4 us
  starting transfers between devices  16.4 us (49%)
  waiting for transfers between devices  11.2 us (33%)
  Pallas kernels  4.56 us (14%)
  between operations  0.79 us (2%)
    ppermute x8, starting transfers between devices, swap(): return lax.ppermute(value, AXES, pairs)  12.9 us
    ppermute x8, waiting for transfers between devices, swap(): return lax.ppermute(value, AXES, pairs)  8.03 us
    pallas_call x8, Pallas kernels, call(): pl.pallas_call(kernel, out_shape=shapes, in_specs=[space] * len(operands)...  4.56 us
    ppermute x10, starting transfers between devices, swap_core(): return lax.ppermute(value, 'pcol', [(0, 1), (1, 0)])  3.56 us
    ppermute x10, waiting for transfers between devices, swap_core(): return lax.ppermute(value, 'pcol', [(0, 1), (1, 0)])  3.2 us
  transfers between devices with their start and end apart: 18, of which 12 were waited for; matrix products, arithmetic and copies ran while one was open for 1% of the time, Pallas kernels for 8%

profile of v5, /device:TPU:0, one launch (start us, length us, event | category | flops | bytes accessed | tf_op | source)
XLA Modules:
  0.0 33.4 jit_solution(16145801708125948520)
XLA Ops:
  0.6 3.0 %collective-permute-start.1 = (bf16[3,2,48,128]{3,2,1,0:T(8,128)(2,1)}, bf16[3,2,48,128]{3,2,1,0:T(8,128)(2,1)S(1)}, u32[]{:S(2)}, u32[]{:S(2)}) collective-permute-start(bf16[3,2,48,128]{3,2,1,0:T(8,128)(2,1)} %panels_in), channel_id=1, source_target_pairs={{0,2},{1,3},{2,0},{3,1},{4,6},{5,7},{6,4},{7,5},{8,10},{9,11},{10,... | collective-permute-start | bytes 221192 | tf_op jit(solution)/shard_map/ppermute | solution.py:25
  3.6 1.5 %shard_map.59 = (bf16[2,96,384]{2,1,0:T(8,128)(2,1)S(1)}, bf16[3,2,48,128]{3,2,1,0:T(8,128)(2,1)S(1)}, bf16[3,2,128,128]{3,2,1,0:T(8,128)(2,1)S(1)}, f32[2,96,12...) custom-call(bf16[2,8,1,48,96]{4,3,2,1,0:T(8,128)(2,1)} %matrix_in.1, ...), custom_call_target="tpu_custom_call" | custom-call | bytes 12582912 | tf_op jit(solution)/shard_map/pallas_call | solution.py:43
  5.1 0.1 collective-permute-start
  5.2 1.0 %collective-permute-done.1.panels_far = bf16[3,2,48,128]{3,2,1,0:T(8,128)(2,1)S(1)} collective-permute-done((bf16[3,2,48,128]{3,2,1,0:T(8,128)(2,1)}, bf16[3,2,48,128]{3,2,1,0:T(8,128)(2,1)S(1)}, u32[]{:S(2)}, u32[]{:S(2)}) %collective-permute-start.1) | collective-permute-done | bytes 73760 | tf_op jit(solution)/shard_map/ppermute | solution.py:25
  6.2 0.1 shard_map.60.block
  6.3 0.1 collective-permute-start.2
  6.4 0.5 %collective-permute-start.7 = (bf16[3,2,48,128]{3,2,1,0:T(8,128)(2,1)S(1)}, bf16[3,2,48,128]{3,2,1,0:T(8,128)(2,1)S(1)}, u32[]{:S(2)}, u32[]{:S(2)}) collective-permute-start(bf16[3,2,48,128]{3,2,1,0:T(8,128)(2,1)S(1)} %get-tuple-element.23.panels), channel_id=1, source_target_pairs={{0,1},{1,0},{2,3},{3,2},{4,5},{5,4},{6,7},{7,6},{8,9},{9,8},{10,11... | collective-permute-start | bytes 221192 | tf_op jit(solution)/shard_map/ppermute | solution.py:29
  6.9 0.1 collective-permute-start.8
  6.9 0.7 %collective-permute-done.2.block_core = bf16[2,48,384]{2,1,0:T(8,128)(2,1)S(1)} collective-permute-done((bf16[2,48,384]{2,1,0:T(8,128)(2,1)S(1)}, bf16[2,48,384]{2,1,0:T(8,128)(2,1)S(1)}, u32[]{:S(2)}, u32[]{:S(2)}) %collective-permute-start.2) | collective-permute-done | bytes 73760 | tf_op jit(solution)/shard_map/ppermute | solution.py:29
  7.6 0.0 collective-permute-done.near_core
  7.7 2.1 %collective-permute-start.3 = (bf16[2,96,384]{2,1,0:T(8,128)(2,1)S(1)}, bf16[2,96,384]{2,1,0:T(8,128)(2,1)S(1)}, u32[]{:S(2)}, u32[]{:S(2)}) collective-permute-start(bf16[2,96,384]{2,1,0:T(8,128)(2,1)S(1)} %get-tuple-element.20), channel_id=1, source_target_pairs={{0,2},{1,5},{2,0},{3,7},{4,6},{5,1},{6,4},{7,3},{8,10},{9,13},{10,... | collective-permute-start | bytes 442376 | tf_op jit(solution)/shard_map/ppermute | solution.py:25
  9.8 0.1 collective-permute-start.5
  9.8 1.9 %collective-permute-start.9 = (bf16[2,96,384]{2,1,0:T(8,128)(2,1)S(1)}, bf16[2,96,384]{2,1,0:T(8,128)(2,1)S(1)}, u32[]{:S(2)}, u32[]{:S(2)}) collective-permute-start(bf16[2,96,384]{2,1,0:T(8,128)(2,1)S(1)} %get-tuple-element.22), channel_id=1, source_target_pairs={{0,2},{1,13},{2,0},{3,15},{4,6},{5,9},{6,4},{7,11},{8,10},{9,5},{1... | collective-permute-start | bytes 442376 | tf_op jit(solution)/shard_map/ppermute | solution.py:25
  11.8 0.0 collective-permute-done.7.panels_core
  11.8 0.0 collective-permute-done.8.panels_far_core
  11.8 0.2 shard_map.62.left
  12.0 0.1 broadcast_in_dim.16
  12.1 0.8 %collective-permute-done.3 = bf16[2,96,384]{2,1,0:T(8,128)(2,1)S(1)} collective-permute-done((bf16[2,96,384]{2,1,0:T(8,128)(2,1)S(1)}, bf16[2,96,384]{2,1,0:T(8,128)(2,1)S(1)}, u32[]{:S(2)}, u32[]{:S(2)}) %collective-permute-start.3) | collective-permute-done | bytes 147488 | tf_op jit(solution)/shard_map/ppermute | solution.py:25
  12.9 0.1 collective-permute-start.4
  13.0 1.9 %collective-permute-done.5 = bf16[2,96,384]{2,1,0:T(8,128)(2,1)S(1)} collective-permute-done((bf16[2,96,384]{2,1,0:T(8,128)(2,1)S(1)}, bf16[2,96,384]{2,1,0:T(8,128)(2,1)S(1)}, u32[]{:S(2)}, u32[]{:S(2)}) %collective-permute-start.5) | collective-permute-done | bytes 147488 | tf_op jit(solution)/shard_map/ppermute | solution.py:25
  14.9 1.3 %collective-permute-start.6 = (bf16[2,96,384]{2,1,0:T(8,128)(2,1)S(1)}, bf16[2,96,384]{2,1,0:T(8,128)(2,1)S(1)}, u32[]{:S(2)}, u32[]{:S(2)}) collective-permute-start(bf16[2,96,384]{2,1,0:T(8,128)(2,1)S(1)} %collective-permute-done.5), channel_id=1, source_target_pairs={{0,1},{1,0},{2,3},{3,2},{4,5},{5,4},{6,7},{7,6},{8,9},{9,8},{10,11... | collective-permute-start | bytes 442376 | tf_op jit(solution)/shard_map/ppermute | solution.py:29
  16.2 0.3 collective-permute-done.9
  16.5 0.0 collective-permute-done.4.far_0
  16.5 0.7 %collective-permute-done.6.far_1 = bf16[2,96,384]{2,1,0:T(8,128)(2,1)S(1)} collective-permute-done((bf16[2,96,384]{2,1,0:T(8,128)(2,1)S(1)}, bf16[2,96,384]{2,1,0:T(8,128)(2,1)S(1)}, u32[]{:S(2)}, u32[]{:S(2)}) %collective-permute-start.6) | collective-permute-done | bytes 147488 | tf_op jit(solution)/shard_map/ppermute | solution.py:29
  17.2 0.7 %shard_map.63.product = f32[2,96,384]{2,1,0:T(8,128)S(1)} custom-call(bf16[2,96,384]{2,1,0:T(8,128)(2,1)S(1)} %get-tuple-element.17.near, bf16[2,96,384]{2,1,0:T(8,128)(2,1)S(1)} %collective-permute-done.near_core, bf16[2,96,384]{2,1,0:T(8,128)(2,1)S(1)} %collective-permute-done.4.far_0, bf16[2,96,384]{2,1,0:T(8,128)(2,1)S(1)} %collective-permute-done.6.far_1, ...), custom_call_target="tpu_custom_call" | custom-call | bytes 1474560 | tf_op jit(solution)/shard_map/pallas_call | solution.py:43
  17.9 0.4 %shard_map.64 = (bf16[3,48,128]{2,1,0:T(8,128)(2,1)S(1)}, bf16[3,3,48,128]{3,2,1,0:T(8,128)(2,1)S(1)}, f32[3,128,128]{2,1,0:T(8,128)S(1)}) custom-call(f32[2,96,128]{2,1,0:T(8,128)S(1)} %get-tuple-element.16.kept, f32[2,96,384]{2,1,0:T(8,128)S(1)} %shard_map.63.product, bf16[3,2,128,192]{3,2,1,0:T(8,128)(2,1)S(1)} %shard_map.62.left), custom_call_target="tpu_custom_call" | custom-call | bytes 1032192 | tf_op jit(solution)/shard_map/pallas_call | solution.py:43
  18.3 0.8 %collective-permute-start.10 = (bf16[432,128]{1,0:T(8,128)(2,1)S(1)}, bf16[432,128]{1,0:T(8,128)(2,1)S(1)}, u32[]{:S(2)}, u32[]{:S(2)}) collective-permute-start(bf16[432,128]{1,0:T(8,128)(2,1)S(1)} %bitcast.15), channel_id=1, source_target_pairs={{0,1},{1,0},{2,3},{3,2},{4,5},{5,4},{6,7},{7,6},{8,9},{9,8},{10,11... | collective-permute-start | bytes 331784 | tf_op jit(solution)/shard_map/ppermute | solution.py:29
  19.2 1.6 %collective-permute-start.13 = (f16[384,128]{1,0:T(8,128)(2,1)S(1)}, f16[384,128]{1,0:T(8,128)(2,1)S(1)}, u32[]{:S(2)}, u32[]{:S(2)}) collective-permute-start(f16[384,128]{1,0:T(8,128)(2,1)S(1)} %bitcast.17), channel_id=1, source_target_pairs={{0,2},{1,13},{2,0},{3,15},{4,6},{5,9},{6,4},{7,11},{8,10},{9,5},{1... | collective-permute-start | bytes 294920 | tf_op jit(solution)/shard_map/ppermute | solution.py:25
  20.7 0.5 %collective-permute-start.14 = (f16[384,128]{1,0:T(8,128)(2,1)S(1)}, f16[384,128]{1,0:T(8,128)(2,1)S(1)}, u32[]{:S(2)}, u32[]{:S(2)}) collective-permute-start(f16[384,128]{1,0:T(8,128)(2,1)S(1)} %bitcast.18), channel_id=1, source_target_pairs={{0,2},{1,9},{2,0},{3,11},{4,6},{5,13},{6,4},{7,15},{8,10},{9,1},{1... | collective-permute-start | bytes 294920 | tf_op jit(solution)/shard_map/ppermute | solution.py:25
  21.2 0.0 collective-permute-done.10
  21.3 1.6 %collective-permute-start.11 = (f16[384,128]{1,0:T(8,128)(2,1)S(1)}, f16[384,128]{1,0:T(8,128)(2,1)S(1)}, u32[]{:S(2)}, u32[]{:S(2)}) collective-permute-start(f16[384,128]{1,0:T(8,128)(2,1)S(1)} %maximum_select_fusion), channel_id=1, source_target_pairs={{0,2},{1,5},{2,0},{3,7},{4,6},{5,1},{6,4},{7,3},{8,10},{9,13},{10,... | collective-permute-start | bytes 294920 | tf_op jit(solution)/shard_map/ppermute | solution.py:25
  22.9 1.0 %collective-permute-done.13 = f16[384,128]{1,0:T(8,128)(2,1)S(1)} collective-permute-done((f16[384,128]{1,0:T(8,128)(2,1)S(1)}, f16[384,128]{1,0:T(8,128)(2,1)S(1)}, u32[]{:S(2)}, u32[]{:S(2)}) %collective-permute-start.13) | collective-permute-done | bytes 98336 | tf_op jit(solution)/shard_map/ppermute | solution.py:25
  23.8 1.5 %collective-permute-done.14 = f16[384,128]{1,0:T(8,128)(2,1)S(1)} collective-permute-done((f16[384,128]{1,0:T(8,128)(2,1)S(1)}, f16[384,128]{1,0:T(8,128)(2,1)S(1)}, u32[]{:S(2)}, u32[]{:S(2)}) %collective-permute-start.14) | collective-permute-done | bytes 98336 | tf_op jit(solution)/shard_map/ppermute | solution.py:25
  25.3 1.1 %collective-permute-done.11 = f16[384,128]{1,0:T(8,128)(2,1)S(1)} collective-permute-done((f16[384,128]{1,0:T(8,128)(2,1)S(1)}, f16[384,128]{1,0:T(8,128)(2,1)S(1)}, u32[]{:S(2)}, u32[]{:S(2)}) %collective-permute-start.11) | collective-permute-done | bytes 98336 | tf_op jit(solution)/shard_map/ppermute | solution.py:25
  26.4 0.1 fusion
  26.4 2.1 %collective-permute-start.15 = (f16[384,128]{1,0:T(8,128)(2,1)S(1)}, f16[384,128]{1,0:T(8,128)(2,1)S(1)}, u32[]{:S(2)}, u32[]{:S(2)}) collective-permute-start(f16[384,128]{1,0:T(8,128)(2,1)S(1)} %get-tuple-element.31), channel_id=1, source_target_pairs={{0,4},{1,3},{2,6},{3,1},{4,0},{5,7},{6,2},{7,5},{8,12},{9,11},{10,... | collective-permute-start | bytes 294920 | tf_op jit(solution)/shard_map/ppermute | solution.py:25
  28.6 0.3 %collective-permute-start.12 = (f16[144,128]{1,0:T(8,128)(2,1)S(1)}, f16[144,128]{1,0:T(8,128)(2,1)S(1)}, u32[]{:S(2)}, u32[]{:S(2)}) collective-permute-start(f16[144,128]{1,0:T(8,128)(2,1)S(1)} %get-tuple-element.32), channel_id=1, source_target_pairs={{0,1},{1,0},{2,3},{3,2},{4,5},{5,4},{6,7},{7,6},{8,9},{9,8},{10,11... | collective-permute-start | bytes 110600 | tf_op jit(solution)/shard_map/ppermute | solution.py:29
  28.9 0.2 collective-permute-start.16
  29.1 0.7 %collective-permute-done.12 = f16[144,128]{1,0:T(8,128)(2,1)S(1)} collective-permute-done((f16[144,128]{1,0:T(8,128)(2,1)S(1)}, f16[144,128]{1,0:T(8,128)(2,1)S(1)}, u32[]{:S(2)}, u32[]{:S(2)}) %collective-permute-start.12) | collective-permute-done | bytes 36896 | tf_op jit(solution)/shard_map/ppermute | solution.py:29
  29.9 0.7 %shard_map.65 = bf16[3,2,48,128]{3,2,1,0:T(8,128)(2,1)} custom-call(bf16[144,128]{1,0:T(8,128)(2,1)S(1)} %bitcast.14, bf16[144,128]{1,0:T(8,128)(2,1)S(1)} %slice.20.own_core, f32[144,128]{1,0:T(8,128)S(1)} %get-tuple-element.33.other, f32[144,128]{1,0:T(8,128)S(1)} %convert_element_type.46.other_core), custom_call_target="tpu_custom_call" | custom-call | bytes 4194304 | tf_op jit(solution)/shard_map/pallas_call | solution.py:43
  30.6 0.6 %collective-permute-done.15 = f16[384,128]{1,0:T(8,128)(2,1)S(1)} collective-permute-done((f16[384,128]{1,0:T(8,128)(2,1)S(1)}, f16[384,128]{1,0:T(8,128)(2,1)S(1)}, u32[]{:S(2)}, u32[]{:S(2)}) %collective-permute-start.15) | collective-permute-done | bytes 98336 | tf_op jit(solution)/shard_map/ppermute | solution.py:25
  31.1 0.1 collective-permute-start.17
  31.3 0.0 collective-permute-done.16
  31.3 1.1 %collective-permute-done.17 = f16[384,128]{1,0:T(8,128)(2,1)S(1)} collective-permute-done((f16[384,128]{1,0:T(8,128)(2,1)S(1)}, f16[384,128]{1,0:T(8,128)(2,1)S(1)}, u32[]{:S(2)}, u32[]{:S(2)}) %collective-permute-start.17) | collective-permute-done | bytes 98336 | tf_op jit(solution)/shard_map/ppermute | solution.py:29
  32.5 0.9 %shard_map.66 = f32[3,2,128,128]{3,2,1,0:T(8,128)} custom-call(bf16[3,2,128,128]{3,2,1,0:T(8,128)(2,1)S(1)} %get-tuple-element.28.diag_inverse, f32[384,128]{1,0:T(8,128)S(1)} %get-tuple-element.30.mine, f32[384,128]{1,0:T(8,128)S(1)} %convert_element_type.53.far, f32[384,128]{1,0:T(8,128)S(1)} %convert_element_type.54.mine_core, ...), custom_call_target="tpu_custom_call" | custom-call | bytes 1376256 | tf_op jit(solution)/shard_map/pallas_call | solution.py:43
  (15 shorter events, 0.3 us)
Async XLA Ops:
  0.6 5.5 %collective-permute-start.1 = (bf16[3,2,48,128]{3,2,1,0:T(8,128)(2,1)}, bf16[3,2,48,128]{3,2,1,0:T(8,128)(2,1)S(1)}, u32[]{:S(2)}, u32[]{:S(2)}) collective-permute-start(bf16[3,2,48,128]{3,2,1,0:T(8,128)(2,1)} %panels_in), channel_id=1, source_target_pairs={{0,2},{1,3},{2,0},{3,1},{4,6},{5,7},{6,4},{7,5},{8,10},{9,11},{10,... | collective-permute-start | bytes 221192 | tf_op jit(solution)/shard_map/ppermute | solution.py:25
  5.1 2.5 %collective-permute-start = (bf16[2,96,384]{2,1,0:T(8,128)(2,1)S(1)}, bf16[2,96,384]{2,1,0:T(8,128)(2,1)S(1)}, u32[]{:S(2)}, u32[]{:S(2)}) collective-permute-start(bf16[2,96,384]{2,1,0:T(8,128)(2,1)S(1)} %get-tuple-element.17.near), channel_id=1, source_target_pairs={{0,1},{1,0},{2,3},{3,2},{4,5},{5,4},{6,7},{7,6},{8,9},{9,8},{10,11... | collective-permute-start | bytes 442376 | tf_op jit(solution)/shard_map/ppermute | solution.py:29
  6.3 1.3 %collective-permute-start.2 = (bf16[2,48,384]{2,1,0:T(8,128)(2,1)S(1)}, bf16[2,48,384]{2,1,0:T(8,128)(2,1)S(1)}, u32[]{:S(2)}, u32[]{:S(2)}) collective-permute-start(bf16[2,48,384]{2,1,0:T(8,128)(2,1)S(1)} %shard_map.60.block), channel_id=1, source_target_pairs={{0,1},{1,0},{2,3},{3,2},{4,5},{5,4},{6,7},{7,6},{8,9},{9,8},{10,11... | collective-permute-start | bytes 221192 | tf_op jit(solution)/shard_map/ppermute | solution.py:29
  6.4 5.4 %collective-permute-start.7 = (bf16[3,2,48,128]{3,2,1,0:T(8,128)(2,1)S(1)}, bf16[3,2,48,128]{3,2,1,0:T(8,128)(2,1)S(1)}, u32[]{:S(2)}, u32[]{:S(2)}) collective-permute-start(bf16[3,2,48,128]{3,2,1,0:T(8,128)(2,1)S(1)} %get-tuple-element.23.panels), channel_id=1, source_target_pairs={{0,1},{1,0},{2,3},{3,2},{4,5},{5,4},{6,7},{7,6},{8,9},{9,8},{10,11... | collective-permute-start | bytes 221192 | tf_op jit(solution)/shard_map/ppermute | solution.py:29
  6.9 4.9 %collective-permute-start.8 = (bf16[3,2,48,128]{3,2,1,0:T(8,128)(2,1)S(1)}, bf16[3,2,48,128]{3,2,1,0:T(8,128)(2,1)S(1)}, u32[]{:S(2)}, u32[]{:S(2)}) collective-permute-start(bf16[3,2,48,128]{3,2,1,0:T(8,128)(2,1)S(1)} %collective-permute-done.1.panels_far), channel_id=1, source_target_pairs={{0,1},{1,0},{2,3},{3,2},{4,5},{5,4},{6,7},{7,6},{8,9},{9,8},{10,11... | collective-permute-start | bytes 221192 | tf_op jit(solution)/shard_map/ppermute | solution.py:29
  7.7 5.2 %collective-permute-start.3 = (bf16[2,96,384]{2,1,0:T(8,128)(2,1)S(1)}, bf16[2,96,384]{2,1,0:T(8,128)(2,1)S(1)}, u32[]{:S(2)}, u32[]{:S(2)}) collective-permute-start(bf16[2,96,384]{2,1,0:T(8,128)(2,1)S(1)} %get-tuple-element.20), channel_id=1, source_target_pairs={{0,2},{1,5},{2,0},{3,7},{4,6},{5,1},{6,4},{7,3},{8,10},{9,13},{10,... | collective-permute-start | bytes 442376 | tf_op jit(solution)/shard_map/ppermute | solution.py:25
  9.8 5.1 %collective-permute-start.5 = (bf16[2,96,384]{2,1,0:T(8,128)(2,1)S(1)}, bf16[2,96,384]{2,1,0:T(8,128)(2,1)S(1)}, u32[]{:S(2)}, u32[]{:S(2)}) collective-permute-start(bf16[2,96,384]{2,1,0:T(8,128)(2,1)S(1)} %get-tuple-element.21), channel_id=1, source_target_pairs={{0,2},{1,9},{2,0},{3,11},{4,6},{5,13},{6,4},{7,15},{8,10},{9,1},{1... | collective-permute-start | bytes 442376 | tf_op jit(solution)/shard_map/ppermute | solution.py:25
  9.8 6.6 %collective-permute-start.9 = (bf16[2,96,384]{2,1,0:T(8,128)(2,1)S(1)}, bf16[2,96,384]{2,1,0:T(8,128)(2,1)S(1)}, u32[]{:S(2)}, u32[]{:S(2)}) collective-permute-start(bf16[2,96,384]{2,1,0:T(8,128)(2,1)S(1)} %get-tuple-element.22), channel_id=1, source_target_pairs={{0,2},{1,13},{2,0},{3,15},{4,6},{5,9},{6,4},{7,11},{8,10},{9,5},{1... | collective-permute-start | bytes 442376 | tf_op jit(solution)/shard_map/ppermute | solution.py:25
  12.9 3.6 %collective-permute-start.4 = (bf16[2,96,384]{2,1,0:T(8,128)(2,1)S(1)}, bf16[2,96,384]{2,1,0:T(8,128)(2,1)S(1)}, u32[]{:S(2)}, u32[]{:S(2)}) collective-permute-start(bf16[2,96,384]{2,1,0:T(8,128)(2,1)S(1)} %collective-permute-done.3), channel_id=1, source_target_pairs={{0,1},{1,0},{2,3},{3,2},{4,5},{5,4},{6,7},{7,6},{8,9},{9,8},{10,11... | collective-permute-start | bytes 442376 | tf_op jit(solution)/shard_map/ppermute | solution.py:29
  14.9 2.3 %collective-permute-start.6 = (bf16[2,96,384]{2,1,0:T(8,128)(2,1)S(1)}, bf16[2,96,384]{2,1,0:T(8,128)(2,1)S(1)}, u32[]{:S(2)}, u32[]{:S(2)}) collective-permute-start(bf16[2,96,384]{2,1,0:T(8,128)(2,1)S(1)} %collective-permute-done.5), channel_id=1, source_target_pairs={{0,1},{1,0},{2,3},{3,2},{4,5},{5,4},{6,7},{7,6},{8,9},{9,8},{10,11... | collective-permute-start | bytes 442376 | tf_op jit(solution)/shard_map/ppermute | solution.py:29
  18.3 2.9 %collective-permute-start.10 = (bf16[432,128]{1,0:T(8,128)(2,1)S(1)}, bf16[432,128]{1,0:T(8,128)(2,1)S(1)}, u32[]{:S(2)}, u32[]{:S(2)}) collective-permute-start(bf16[432,128]{1,0:T(8,128)(2,1)S(1)} %bitcast.15), channel_id=1, source_target_pairs={{0,1},{1,0},{2,3},{3,2},{4,5},{5,4},{6,7},{7,6},{8,9},{9,8},{10,11... | collective-permute-start | bytes 331784 | tf_op jit(solution)/shard_map/ppermute | solution.py:29
  19.2 4.7 %collective-permute-start.13 = (f16[384,128]{1,0:T(8,128)(2,1)S(1)}, f16[384,128]{1,0:T(8,128)(2,1)S(1)}, u32[]{:S(2)}, u32[]{:S(2)}) collective-permute-start(f16[384,128]{1,0:T(8,128)(2,1)S(1)} %bitcast.17), channel_id=1, source_target_pairs={{0,2},{1,13},{2,0},{3,15},{4,6},{5,9},{6,4},{7,11},{8,10},{9,5},{1... | collective-permute-start | bytes 294920 | tf_op jit(solution)/shard_map/ppermute | solution.py:25
  20.7 4.6 %collective-permute-start.14 = (f16[384,128]{1,0:T(8,128)(2,1)S(1)}, f16[384,128]{1,0:T(8,128)(2,1)S(1)}, u32[]{:S(2)}, u32[]{:S(2)}) collective-permute-start(f16[384,128]{1,0:T(8,128)(2,1)S(1)} %bitcast.18), channel_id=1, source_target_pairs={{0,2},{1,9},{2,0},{3,11},{4,6},{5,13},{6,4},{7,15},{8,10},{9,1},{1... | collective-permute-start | bytes 294920 | tf_op jit(solution)/shard_map/ppermute | solution.py:25
  21.3 5.1 %collective-permute-start.11 = (f16[384,128]{1,0:T(8,128)(2,1)S(1)}, f16[384,128]{1,0:T(8,128)(2,1)S(1)}, u32[]{:S(2)}, u32[]{:S(2)}) collective-permute-start(f16[384,128]{1,0:T(8,128)(2,1)S(1)} %maximum_select_fusion), channel_id=1, source_target_pairs={{0,2},{1,5},{2,0},{3,7},{4,6},{5,1},{6,4},{7,3},{8,10},{9,13},{10,... | collective-permute-start | bytes 294920 | tf_op jit(solution)/shard_map/ppermute | solution.py:25
  26.4 4.7 %collective-permute-start.15 = (f16[384,128]{1,0:T(8,128)(2,1)S(1)}, f16[384,128]{1,0:T(8,128)(2,1)S(1)}, u32[]{:S(2)}, u32[]{:S(2)}) collective-permute-start(f16[384,128]{1,0:T(8,128)(2,1)S(1)} %get-tuple-element.31), channel_id=1, source_target_pairs={{0,4},{1,3},{2,6},{3,1},{4,0},{5,7},{6,2},{7,5},{8,12},{9,11},{10,... | collective-permute-start | bytes 294920 | tf_op jit(solution)/shard_map/ppermute | solution.py:25
  28.6 1.3 %collective-permute-start.12 = (f16[144,128]{1,0:T(8,128)(2,1)S(1)}, f16[144,128]{1,0:T(8,128)(2,1)S(1)}, u32[]{:S(2)}, u32[]{:S(2)}) collective-permute-start(f16[144,128]{1,0:T(8,128)(2,1)S(1)} %get-tuple-element.32), channel_id=1, source_target_pairs={{0,1},{1,0},{2,3},{3,2},{4,5},{5,4},{6,7},{7,6},{8,9},{9,8},{10,11... | collective-permute-start | bytes 110600 | tf_op jit(solution)/shard_map/ppermute | solution.py:29
  28.9 2.4 %collective-permute-start.16 = (f16[384,128]{1,0:T(8,128)(2,1)S(1)}, f16[384,128]{1,0:T(8,128)(2,1)S(1)}, u32[]{:S(2)}, u32[]{:S(2)}) collective-permute-start(f16[384,128]{1,0:T(8,128)(2,1)S(1)} %get-tuple-element.31), channel_id=1, source_target_pairs={{0,1},{1,0},{2,3},{3,2},{4,5},{5,4},{6,7},{7,6},{8,9},{9,8},{10,11... | collective-permute-start | bytes 294920 | tf_op jit(solution)/shard_map/ppermute | solution.py:29
  31.1 1.3 %collective-permute-start.17 = (f16[384,128]{1,0:T(8,128)(2,1)S(1)}, f16[384,128]{1,0:T(8,128)(2,1)S(1)}, u32[]{:S(2)}, u32[]{:S(2)}) collective-permute-start(f16[384,128]{1,0:T(8,128)(2,1)S(1)} %collective-permute-done.15), channel_id=1, source_target_pairs={{0,1},{1,0},{2,3},{3,2},{4,5},{5,4},{6,7},{7,6},{8,9},{9,8},{10,11... | collective-permute-start | bytes 294920 | tf_op jit(solution)/shard_map/ppermute | solution.py:29

commit v6 on v5

--- a/solution.py
+++ b/solution.py
@@ -10,10 +10,17 @@
 from jax.sharding import PartitionSpec as P
 
 AXES = ("prow", "pcol")
-MASKS = (2, 4, 6)
-MASKS_SUM = (6, 4, 2)
+MASKS = (4, 2, 6)
+MASKS_SUM = (4, 2, 6)
 VMEM = pl.BlockSpec(memory_space=pltpu.VMEM)
 HBM = pl.BlockSpec(memory_space=pltpu.HBM)
+
+
+def steps_of(count):
+    steps = [0] + [mask // 2 for mask in MASKS]
+    while len(steps) < count:
+        steps = steps + [step ^ len(steps) for step in steps]
+    return steps
 
 
 def swap(value, rows, cols, mask0, mask1):
@@ -37,14 +44,14 @@
     return with_layout_constraint(value, Layout(tuple(range(value.ndim))))
 
 
-def call(kernel, outs, operands, scratch=(), cost=0, space=VMEM, limit=0):
+def call(kernel, outs, operands, scratch=(), cost=0, space=VMEM, out_space=VMEM, limit=0):
     shapes = [jax.ShapeDtypeStruct(shape, dtype) for shape, dtype in outs]
     size = sum(v.size * v.dtype.itemsize for v in list(operands) + shapes)
     return pl.pallas_call(
         kernel,
         out_shape=shapes,
         in_specs=[space] * len(operands),
-        out_specs=[VMEM] * len(shapes),
+        out_specs=[out_space] * len(shapes),
         scratch_shapes=list(scratch),
         cost_estimate=pl.CostEstimate(flops=0, bytes_accessed=cost or size, transcendentals=0),
         compiler_params=pltpu.CompilerParams(vmem_limit_bytes=limit or 2 * size + (4 << 20)),
@@ -90,8 +97,10 @@
     supernodes, _, rows_half, width = panels.shape
     groups, rows_dev = matrix.shape[1], matrix.shape[4]
     row_index, col_index = lax.axis_index("prow"), lax.axis_index("pcol")
+    here = row_index // 2
     for part in range(2):
-        across[part] = matrix[part].reshape(groups * rows_half, rows_dev).T
+        pieces = [matrix[part, pl.ds(2 * (here ^ step), 2)] for step in steps_of(groups // 2)]
+        across[part] = jnp.concatenate(pieces).reshape(groups * rows_half, rows_dev).T
     low = lax.broadcasted_iota(jnp.int32, (rows_half, width), 1) < width // 2
     for node in range(supernodes):
         lanes = slice(node * width, (node + 1) * width)
@@ -128,21 +137,43 @@
             second[core, rows] = jnp.where(carry, near_core[core, rows], source[x])
 
 
-def product_kernel(width, near, near_core, far_0, far_1, held, out):
+def product_kernel(near, near_core, far_0, far_1, held, out):
     count, _, rows_dev, lanes = held.shape
     depth = count * rows_dev
-    rights = [held[:, core].reshape(depth, lanes) for core in range(2)]
-    for far_or, lefts in ((0, (near_core, near)), (1, (far_0, far_1))):
-        real, imag = [
-            sum(
-                jnp.dot(left[part], right, preferred_element_type=jnp.float32)
-                for left, right in zip(lefts, rights)
-            )
-            for part in range(2)
-        ]
-        for node in range(lanes // width):
-            part = slice(node * width, (node + 1) * width)
-            out[far_or, :, part] = real[:, part] + turned(imag[:, part])
+    for core, lefts in ((0, (near_core, far_0)), (1, (near, far_1))):
+        right = held[:, core].reshape(depth, lanes)
+        for far_or, left in enumerate(lefts):
+            value = jnp.dot(left[...].reshape(2 * rows_dev, depth), right, preferred_element_type=jnp.float32)
+            value = value.reshape(out.shape[1:])
+            out[far_or] = value if core == 0 else out[far_or] + value
+
+
+def whole_kernel(scale, near, near_core, far_0, far_1, block_0, block_1, block_2, block_3, kept, left, own, send, diag, columns):
+    supernodes, rows_half, width = own.shape
+    _, rows_dev, depth = near.shape
+    blocks = (block_0, block_1, block_2, block_3)
+    right = jnp.concatenate([block[core] for core in range(2) for block in blocks])
+    for far_or, pair in enumerate(((near_core, near), (far_0, far_1))):
+        both = jnp.concatenate([part[...].reshape(2 * rows_dev, depth) for part in pair], axis=1)
+        value = jnp.dot(both, right, preferred_element_type=jnp.float32)
+        for node in range(supernodes):
+            lanes = slice(node * width, (node + 1) * width)
+            keep = kept[far_or, :, node : node + 1]
+            column = value[:rows_dev, lanes] + turned(value[rows_dev:, lanes])
+            column = (-(column * keep)).astype(jnp.bfloat16)
+            columns[node, far_or] = column
+            low, high = column[:rows_half], column[rows_half:]
+            if far_or == 0:
+                send[0, node], own[node] = low, high
+            else:
+                send[1, node], send[2, node] = low, high
+    for node in range(supernodes):
+        both = jnp.dot(
+            left[node].reshape(2 * width, 2 * rows_dev),
+            columns[node].reshape(2 * rows_dev, width),
+            preferred_element_type=jnp.float32,
+        )
+        diag[node] = (both[:width] + turned(both[width:])) * (1.0 / scale)
 
 
 def left_kernel(panels, panels_far, panels_core, panels_far_core, out, rows):
@@ -157,13 +188,14 @@
 
 def diagonal_kernel(scale, kept, product, left, own, send, diag, columns):
     supernodes, _, width, _ = left.shape
-    rows_dev = product.shape[1]
+    rows_dev = product.shape[2]
     rows_half = rows_dev // 2
     for node in range(supernodes):
         lanes = slice(node * width, (node + 1) * width)
         for far_or in range(2):
             keep = kept[far_or, :, node : node + 1]
-            value = (-(product[far_or, :, lanes] * keep)).astype(jnp.bfloat16)
+            value = product[far_or, 0, :, lanes] + turned(product[far_or, 1, :, lanes])
+            value = (-(value * keep)).astype(jnp.bfloat16)
             columns[far_or] = value
             low, high = value[:rows_half], value[rows_half:]
             if far_or == 0:
@@ -171,9 +203,8 @@
             else:
                 send[1, node], send[2, node] = low, high
         right = columns[...].reshape(2 * rows_dev, width)
-        real = jnp.dot(left[node, 0], right, preferred_element_type=jnp.float32)
-        imag = jnp.dot(left[node, 1], right, preferred_element_type=jnp.float32)
-        diag[node] = (real + turned(imag)) * (1.0 / scale)
+        both = jnp.dot(left[node].reshape(2 * width, 2 * rows_dev), right, preferred_element_type=jnp.float32)
+        diag[node] = (both[:width] + turned(both[width:])) * (1.0 / scale)
 
 
 def unpack(near, far):
@@ -196,16 +227,20 @@
         out[node, 1] = imag.astype(jnp.bfloat16)
 
 
-def final_kernel(scale, diag_inverse, mine, far, mine_core, far_core, out):
+def final_kernel(scale, diag_inverse, mine, far, mine_core, far_core, out, value, done):
     supernodes, _, width, _ = out.shape
     first = lax.axis_index("pcol") == 0
+    copies = [pltpu.make_async_copy(value.at[node], out.at[node], done.at[node]) for node in range(supernodes)]
     for node in range(supernodes):
         rows = slice(node * width, (node + 1) * width)
         near_value = jnp.where(first, mine_core[rows], mine[rows]) * scale
         far_value = jnp.where(first, far_core[rows], far[rows]) * scale
         real, imag = unpack(near_value, far_value)
-        out[node, 0] = diag_inverse[node, 0].astype(jnp.float32) - real
-        out[node, 1] = diag_inverse[node, 1].astype(jnp.float32) - imag
+        value[node, 0] = diag_inverse[node, 0].astype(jnp.float32) - real
+        value[node, 1] = diag_inverse[node, 1].astype(jnp.float32) - imag
+        copies[node].start()
+    for copy in copies:
+        copy.wait()
 
 
 def solution(mesh):
@@ -257,8 +292,6 @@
             chip = first = second = jnp.stack([swap_core(block), block]).reshape(chip_shape)
             far_1 = swap(near, rows, cols, 1, 1)
             far_0 = swap_core(far_1)
-        held = jnp.zeros((rows // 2,) + chip_shape, bf16)
-        held = lax.dynamic_update_index_in_dim(held, chip, here, 0)
         arrived = [swap(value, rows, cols, 1, mask) for value, mask in zip((first, second, chip), MASKS)]
         if far_0 is None:
             far_0, far_1 = swap_core(arrived[0]), swap_core(arrived[1])
@@ -268,36 +301,34 @@
             [((supernodes, 2, width, 2 * rows_dev), bf16)],
             [panels, panels_far, panels_core, panels_far_core],
             [pltpu.VMEM((2, cols, rows_half, width), bf16)],
-            cost=6 << 20,
-        )
-        for index, (mask, value) in enumerate(zip(MASKS, arrived)):
-            held = lax.dynamic_update_index_in_dim(held, value, here ^ (mask // 2), 0)
-            held = after(held, left) if index == 0 else held
-        size = 8
-        while size < rows:
-            count = size // 2
-            start = (here // count) * count
-            own = lax.dynamic_slice_in_dim(held, start, count, 0)
-            other = swap(own, rows, cols, 1, size)
-            held = lax.dynamic_update_slice_in_dim(held, other, start ^ count, 0)
-            size *= 2
-
-        (product,) = call(
-            functools.partial(product_kernel, width),
-            [((2, rows_dev, lanes), f32)],
-            [near, near_core, far_0, far_1, held],
         )
         scale = 2 ** max(0, math.ceil(math.log2(groups * 2 * rows_half / 24)))
-        own, send, diag = call(
-            functools.partial(diagonal_kernel, float(scale)),
-            [
-                ((supernodes, rows_half, width), bf16),
-                ((3, supernodes, rows_half, width), bf16),
-                ((supernodes, width, width), f32),
-            ],
-            [keep, product, left],
-            [pltpu.VMEM((2, rows_dev, width), bf16)],
-        )
+        outs = [
+            ((supernodes, rows_half, width), bf16),
+            ((3, supernodes, rows_half, width), bf16),
+            ((supernodes, width, width), f32),
+        ]
+        sums = (2, 2, rows_dev, lanes)
+        columns_scratch = pltpu.VMEM((2, rows_dev, width), bf16)
+        lefts = [near, near_core, far_0, far_1]
+        arrived = list(lax.optimization_barrier(tuple(arrived)))
+        if rows == 8:
+            own, send, diag = call(
+                functools.partial(whole_kernel, float(scale)),
+                outs,
+                lefts + [chip] + arrived + [keep, left],
+                [pltpu.VMEM((supernodes, 2, rows_dev, width), bf16)],
+            )
+        else:
+            held = jnp.stack([chip] + arrived)
+            size = 8
+            while size < rows:
+                held = jnp.concatenate([held, swap(held, rows, cols, 1, size)])
+                size *= 2
+            (product,) = call(product_kernel, [(sums, f32)], lefts + [held])
+            own, send, diag = call(
+                functools.partial(diagonal_kernel, float(scale)), outs, [keep, product, left], [columns_scratch]
+            )
         f16 = jnp.float16
         count = supernodes * width
         some = supernodes * rows_half
@@ -328,6 +359,8 @@
             functools.partial(final_kernel, float(scale)),
             [((supernodes, 2, width, width), f32)],
             [diag_inverse] + pieces,
+            [pltpu.VMEM((supernodes, 2, width, width), f32), pltpu.SemaphoreType.DMA((supernodes,))],
+            out_space=HBM,
         )
         return columns, diag
 

time: 33.6 us -> 33.3 us (level)
  starting transfers between devices: 16.4 us -> 18 us
  waiting for transfers between devices: 11.2 us -> 9.87 us
    ppermute x10, starting transfers between devices: 3.56 us -> 6.05 us  [swap_core(): return lax.ppermute(value, 'pcol', [(0, 1), (1, 0)])]
    ppermute x8, waiting for transfers between devices: 8.03 us -> 5.91 us  [swap(): return lax.ppermute(value, AXES, pairs)]
    ppermute x8, starting transfers between devices: 12.9 us -> 11.9 us  [swap(): return lax.ppermute(value, AXES, pairs)]
    ppermute x10, waiting for transfers between devices: 3.2 us -> 3.95 us  [swap_core(): return lax.ppermute(value, 'pcol', [(0, 1), (1, 0)])]
    pallas_call x8 -> x7, Pallas kernels: 4.56 us -> 4.31 us  [call(): pl.pallas_call(kernel, out_shape=shapes, in_specs=[space] * len(operands)...]
  transfers between devices with their start and end apart: 18 -> 18, of which waited for: 12 -> 11; matrix products, arithmetic and copies ran while one was open for 1% -> 0% of each run, Pallas kernels for 8% -> 7%
where the time goes in v6:
time: 33.3 us; the launch traced here: 33.1 us
  starting transfers between devices  18 us (54%)
  waiting for transfers between devices  9.87 us (30%)
  Pallas kernels  4.31 us (13%)
  between operations  0.77 us (2%)
    ppermute x8, starting transfers between devices, swap(): return lax.ppermute(value, AXES, pairs)  11.9 us
    ppermute x10, starting transfers between devices, swap_core(): return lax.ppermute(value, 'pcol', [(0, 1), (1, 0)])  6.05 us
    ppermute x8, waiting for transfers between devices, swap(): return lax.ppermute(value, AXES, pairs)  5.91 us
    pallas_call x7, Pallas kernels, call(): pl.pallas_call(kernel, out_shape=shapes, in_specs=[space] * len(operands)...  4.31 us
    ppermute x10, waiting for transfers between devices, swap_core(): return lax.ppermute(value, 'pcol', [(0, 1), (1, 0)])  3.95 us
  transfers between devices with their start and end apart: 18, of which 11 were waited for; matrix products, arithmetic and copies ran while one was open for 0% of the time, Pallas kernels for 7%

profile of v6, /device:TPU:0, one launch (start us, length us, event | category | flops | bytes accessed | tf_op | source)
XLA Modules:
  0.0 33.1 jit_solution(17529188374448456462)
XLA Ops:
  0.6 3.0 %collective-permute-start.1 = (bf16[3,2,48,128]{3,2,1,0:T(8,128)(2,1)}, bf16[3,2,48,128]{3,2,1,0:T(8,128)(2,1)S(1)}, u32[]{:S(2)}, u32[]{:S(2)}) collective-permute-start(bf16[3,2,48,128]{3,2,1,0:T(8,128)(2,1)} %panels_in), channel_id=1, source_target_pairs={{0,2},{1,3},{2,0},{3,1},{4,6},{5,7},{6,4},{7,5},{8,10},{9,11},{10,... | collective-permute-start | bytes 221192 | tf_op jit(solution)/shard_map/ppermute | solution.py:32
  3.6 1.5 %shard_map.59 = (bf16[2,96,384]{2,1,0:T(8,128)(2,1)S(1)}, bf16[3,2,48,128]{3,2,1,0:T(8,128)(2,1)S(1)}, bf16[3,2,128,128]{3,2,1,0:T(8,128)(2,1)S(1)}, f32[2,96,12...) custom-call(bf16[2,8,1,48,96]{4,3,2,1,0:T(8,128)(2,1)} %matrix_in.1, ...), custom_call_target="tpu_custom_call" | custom-call | bytes 12582912 | tf_op jit(solution)/shard_map/pallas_call | solution.py:50
  5.1 0.1 collective-permute-start
  5.2 1.0 %collective-permute-done.1.panels_far = bf16[3,2,48,128]{3,2,1,0:T(8,128)(2,1)S(1)} collective-permute-done((bf16[3,2,48,128]{3,2,1,0:T(8,128)(2,1)}, bf16[3,2,48,128]{3,2,1,0:T(8,128)(2,1)S(1)}, u32[]{:S(2)}, u32[]{:S(2)}) %collective-permute-start.1) | collective-permute-done | bytes 73760 | tf_op jit(solution)/shard_map/ppermute | solution.py:32
  6.2 0.1 shard_map.60.block
  6.3 0.1 collective-permute-start.2
  6.4 1.3 %collective-permute-done.2.block_core = bf16[2,48,384]{2,1,0:T(8,128)(2,1)S(1)} collective-permute-done((bf16[2,48,384]{2,1,0:T(8,128)(2,1)S(1)}, bf16[2,48,384]{2,1,0:T(8,128)(2,1)S(1)}, u32[]{:S(2)}, u32[]{:S(2)}) %collective-permute-start.2) | collective-permute-done | bytes 73760 | tf_op jit(solution)/shard_map/ppermute | solution.py:36
  7.6 0.0 collective-permute-done.near_core
  7.7 2.1 %collective-permute-start.3 = (bf16[2,96,384]{2,1,0:T(8,128)(2,1)S(1)}, bf16[2,96,384]{2,1,0:T(8,128)(2,1)S(1)}, u32[]{:S(2)}, u32[]{:S(2)}) collective-permute-start(bf16[2,96,384]{2,1,0:T(8,128)(2,1)S(1)} %get-tuple-element.21), channel_id=1, source_target_pairs={{0,2},{1,9},{2,0},{3,11},{4,6},{5,13},{6,4},{7,15},{8,10},{9,1},{1... | collective-permute-start | bytes 442376 | tf_op jit(solution)/shard_map/ppermute | solution.py:32
  9.8 0.1 collective-permute-start.5
  9.8 1.9 %collective-permute-start.7 = (bf16[2,96,384]{2,1,0:T(8,128)(2,1)S(1)}, bf16[2,96,384]{2,1,0:T(8,128)(2,1)S(1)}, u32[]{:S(2)}, u32[]{:S(2)}) collective-permute-start(bf16[2,96,384]{2,1,0:T(8,128)(2,1)S(1)} %get-tuple-element.23.block_0), channel_id=1, source_target_pairs={{0,2},{1,13},{2,0},{3,15},{4,6},{5,9},{6,4},{7,11},{8,10},{9,5},{1... | collective-permute-start | bytes 442376 | tf_op jit(solution)/shard_map/ppermute | solution.py:32
  11.8 1.1 %collective-permute-done.3.block_1 = bf16[2,96,384]{2,1,0:T(8,128)(2,1)S(1)} collective-permute-done((bf16[2,96,384]{2,1,0:T(8,128)(2,1)S(1)}, bf16[2,96,384]{2,1,0:T(8,128)(2,1)S(1)}, u32[]{:S(2)}, u32[]{:S(2)}) %collective-permute-start.3) | collective-permute-done | bytes 147488 | tf_op jit(solution)/shard_map/ppermute | solution.py:32
  12.9 2.1 %collective-permute-start.4 = (bf16[2,96,384]{2,1,0:T(8,128)(2,1)S(1)}, bf16[2,96,384]{2,1,0:T(8,128)(2,1)S(1)}, u32[]{:S(2)}, u32[]{:S(2)}) collective-permute-start(bf16[2,96,384]{2,1,0:T(8,128)(2,1)S(1)} %collective-permute-done.3.block_1), channel_id=1, source_target_pairs={{0,1},{1,0},{2,3},{3,2},{4,5},{5,4},{6,7},{7,6},{8,9},{9,8},{10,11... | collective-permute-start | bytes 442376 | tf_op jit(solution)/shard_map/ppermute | solution.py:36
  15.0 0.0 collective-permute-done.5.block_2
  15.0 0.5 %collective-permute-start.6 = (bf16[2,96,384]{2,1,0:T(8,128)(2,1)S(1)}, bf16[2,96,384]{2,1,0:T(8,128)(2,1)S(1)}, u32[]{:S(2)}, u32[]{:S(2)}) collective-permute-start(bf16[2,96,384]{2,1,0:T(8,128)(2,1)S(1)} %collective-permute-done.5.block_2), channel_id=1, source_target_pairs={{0,1},{1,0},{2,3},{3,2},{4,5},{5,4},{6,7},{7,6},{8,9},{9,8},{10,11... | collective-permute-start | bytes 442376 | tf_op jit(solution)/shard_map/ppermute | solution.py:36
  15.4 0.0 collective-permute-start.8
  15.5 0.5 %collective-permute-start.9 = (bf16[3,2,48,128]{3,2,1,0:T(8,128)(2,1)S(1)}, bf16[3,2,48,128]{3,2,1,0:T(8,128)(2,1)S(1)}, u32[]{:S(2)}, u32[]{:S(2)}) collective-permute-start(bf16[3,2,48,128]{3,2,1,0:T(8,128)(2,1)S(1)} %collective-permute-done.1.panels_far), channel_id=1, source_target_pairs={{0,1},{1,0},{2,3},{3,2},{4,5},{5,4},{6,7},{7,6},{8,9},{9,8},{10,11... | collective-permute-start | bytes 221192 | tf_op jit(solution)/shard_map/ppermute | solution.py:36
  16.0 0.8 %collective-permute-done.8.panels_core = bf16[3,2,48,128]{3,2,1,0:T(8,128)(2,1)S(1)} collective-permute-done((bf16[3,2,48,128]{3,2,1,0:T(8,128)(2,1)S(1)}, bf16[3,2,48,128]{3,2,1,0:T(8,128)(2,1)S(1)}, u32[]{:S(2)}, u32[]{:S(2)}) %collective-permute-start.8) | collective-permute-done | bytes 73760 | tf_op jit(solution)/shard_map/ppermute | solution.py:36
  16.7 0.2 collective-permute-done.9.panels_far_core
  16.9 0.2 shard_map.62.left
  17.0 0.0 collective-permute-done.7.block_3
  17.1 0.0 collective-permute-done.4.far_0
  17.1 0.0 collective-permute-done.6.far_1
  17.1 0.9 %shard_map.63 = (bf16[3,48,128]{2,1,0:T(8,128)(2,1)S(1)}, bf16[3,3,48,128]{3,2,1,0:T(8,128)(2,1)S(1)}, f32[3,128,128]{2,1,0:T(8,128)S(1)}) custom-call(bf16[2,96,384]{2,1,0:T(8,128)(2,1)S(1)} %get-tuple-element.18.near, bf16[2,96,384]{2,1,0:T(8,128)(2,1)S(1)} %collective-permute-done.near_core, bf16[2,96,384]{2,1,0:T(8,128)(2,1)S(1)} %collective-permute-done.4.far_0, ...), custom_call_target="tpu_custom_call" | custom-call | bytes 1916928 | tf_op jit(solution)/shard_map/pallas_call | solution.py:50
  18.0 0.9 %collective-permute-start.10 = (bf16[432,128]{1,0:T(8,128)(2,1)S(1)}, bf16[432,128]{1,0:T(8,128)(2,1)S(1)}, u32[]{:S(2)}, u32[]{:S(2)}) collective-permute-start(bf16[432,128]{1,0:T(8,128)(2,1)S(1)} %bitcast.7), channel_id=1, source_target_pairs={{0,1},{1,0},{2,3},{3,2},{4,5},{5,4},{6,7},{7,6},{8,9},{9,8},{10,11... | collective-permute-start | bytes 331784 | tf_op jit(solution)/shard_map/ppermute | solution.py:36
  18.9 1.6 %collective-permute-start.13 = (f16[384,128]{1,0:T(8,128)(2,1)S(1)}, f16[384,128]{1,0:T(8,128)(2,1)S(1)}, u32[]{:S(2)}, u32[]{:S(2)}) collective-permute-start(f16[384,128]{1,0:T(8,128)(2,1)S(1)} %bitcast.9), channel_id=1, source_target_pairs={{0,2},{1,9},{2,0},{3,11},{4,6},{5,13},{6,4},{7,15},{8,10},{9,1},{1... | collective-permute-start | bytes 294920 | tf_op jit(solution)/shard_map/ppermute | solution.py:32
  20.5 0.5 %collective-permute-start.14 = (f16[384,128]{1,0:T(8,128)(2,1)S(1)}, f16[384,128]{1,0:T(8,128)(2,1)S(1)}, u32[]{:S(2)}, u32[]{:S(2)}) collective-permute-start(f16[384,128]{1,0:T(8,128)(2,1)S(1)} %bitcast.10), channel_id=1, source_target_pairs={{0,2},{1,5},{2,0},{3,7},{4,6},{5,1},{6,4},{7,3},{8,10},{9,13},{10,... | collective-permute-start | bytes 294920 | tf_op jit(solution)/shard_map/ppermute | solution.py:32
  21.0 0.0 collective-permute-done.10
  21.1 1.6 %collective-permute-start.11 = (f16[384,128]{1,0:T(8,128)(2,1)S(1)}, f16[384,128]{1,0:T(8,128)(2,1)S(1)}, u32[]{:S(2)}, u32[]{:S(2)}) collective-permute-start(f16[384,128]{1,0:T(8,128)(2,1)S(1)} %maximum_select_fusion), channel_id=1, source_target_pairs={{0,2},{1,13},{2,0},{3,15},{4,6},{5,9},{6,4},{7,11},{8,10},{9,5},{1... | collective-permute-start | bytes 294920 | tf_op jit(solution)/shard_map/ppermute | solution.py:32
  22.7 1.0 %collective-permute-done.13 = f16[384,128]{1,0:T(8,128)(2,1)S(1)} collective-permute-done((f16[384,128]{1,0:T(8,128)(2,1)S(1)}, f16[384,128]{1,0:T(8,128)(2,1)S(1)}, u32[]{:S(2)}, u32[]{:S(2)}) %collective-permute-start.13) | collective-permute-done | bytes 98336 | tf_op jit(solution)/shard_map/ppermute | solution.py:32
  23.6 1.5 %collective-permute-done.14 = f16[384,128]{1,0:T(8,128)(2,1)S(1)} collective-permute-done((f16[384,128]{1,0:T(8,128)(2,1)S(1)}, f16[384,128]{1,0:T(8,128)(2,1)S(1)}, u32[]{:S(2)}, u32[]{:S(2)}) %collective-permute-start.14) | collective-permute-done | bytes 98336 | tf_op jit(solution)/shard_map/ppermute | solution.py:32
  25.1 1.1 %collective-permute-done.11 = f16[384,128]{1,0:T(8,128)(2,1)S(1)} collective-permute-done((f16[384,128]{1,0:T(8,128)(2,1)S(1)}, f16[384,128]{1,0:T(8,128)(2,1)S(1)}, u32[]{:S(2)}, u32[]{:S(2)}) %collective-permute-start.11) | collective-permute-done | bytes 98336 | tf_op jit(solution)/shard_map/ppermute | solution.py:32
  26.2 0.1 fusion
  26.2 1.2 %collective-permute-start.15 = (f16[384,128]{1,0:T(8,128)(2,1)S(1)}, f16[384,128]{1,0:T(8,128)(2,1)S(1)}, u32[]{:S(2)}, u32[]{:S(2)}) collective-permute-start(f16[384,128]{1,0:T(8,128)(2,1)S(1)} %get-tuple-element.35), channel_id=1, source_target_pairs={{0,4},{1,3},{2,6},{3,1},{4,0},{5,7},{6,2},{7,5},{8,12},{9,11},{10,... | collective-permute-start | bytes 294920 | tf_op jit(solution)/shard_map/ppermute | solution.py:32
  27.4 1.6 %collective-permute-start.12 = (f16[144,128]{1,0:T(8,128)(2,1)S(1)}, f16[144,128]{1,0:T(8,128)(2,1)S(1)}, u32[]{:S(2)}, u32[]{:S(2)}) collective-permute-start(f16[144,128]{1,0:T(8,128)(2,1)S(1)} %get-tuple-element.36), channel_id=1, source_target_pairs={{0,1},{1,0},{2,3},{3,2},{4,5},{5,4},{6,7},{7,6},{8,9},{9,8},{10,11... | collective-permute-start | bytes 110600 | tf_op jit(solution)/shard_map/ppermute | solution.py:36
  29.0 0.1 collective-permute-start.16
  29.1 0.8 %collective-permute-done.12 = f16[144,128]{1,0:T(8,128)(2,1)S(1)} collective-permute-done((f16[144,128]{1,0:T(8,128)(2,1)S(1)}, f16[144,128]{1,0:T(8,128)(2,1)S(1)}, u32[]{:S(2)}, u32[]{:S(2)}) %collective-permute-start.12) | collective-permute-done | bytes 36896 | tf_op jit(solution)/shard_map/ppermute | solution.py:36
  29.9 0.7 %shard_map.64 = bf16[3,2,48,128]{3,2,1,0:T(8,128)(2,1)} custom-call(bf16[144,128]{1,0:T(8,128)(2,1)S(1)} %bitcast.6, bf16[144,128]{1,0:T(8,128)(2,1)S(1)} %slice.20.own_core, f32[144,128]{1,0:T(8,128)S(1)} %get-tuple-element.37.other, f32[144,128]{1,0:T(8,128)S(1)} %convert_element_type.46.other_core), custom_call_target="tpu_custom_call" | custom-call | bytes 4194304 | tf_op jit(solution)/shard_map/pallas_call | solution.py:50
  30.6 0.3 collective-permute-done.15
  30.9 0.2 collective-permute-start.17
  31.2 0.0 collective-permute-done.16
  31.2 1.0 %collective-permute-done.17 = f16[384,128]{1,0:T(8,128)(2,1)S(1)} collective-permute-done((f16[384,128]{1,0:T(8,128)(2,1)S(1)}, f16[384,128]{1,0:T(8,128)(2,1)S(1)}, u32[]{:S(2)}, u32[]{:S(2)}) %collective-permute-start.17) | collective-permute-done | bytes 98336 | tf_op jit(solution)/shard_map/ppermute | solution.py:36
  32.2 0.9 %shard_map.65 = f32[3,2,128,128]{3,2,1,0:T(8,128)} custom-call(bf16[3,2,128,128]{3,2,1,0:T(8,128)(2,1)S(1)} %get-tuple-element.32.diag_inverse, f32[384,128]{1,0:T(8,128)S(1)} %get-tuple-element.34.mine, f32[384,128]{1,0:T(8,128)S(1)} %convert_element_type.53.far, f32[384,128]{1,0:T(8,128)S(1)} %convert_element_type.54.mine_core, ...), custom_call_target="tpu_custom_call" | custom-call | bytes 1376256 | tf_op jit(solution)/shard_map/pallas_call | solution.py:50
  (11 shorter events, 0.2 us)
Async XLA Ops:
  0.6 5.5 %collective-permute-start.1 = (bf16[3,2,48,128]{3,2,1,0:T(8,128)(2,1)}, bf16[3,2,48,128]{3,2,1,0:T(8,128)(2,1)S(1)}, u32[]{:S(2)}, u32[]{:S(2)}) collective-permute-start(bf16[3,2,48,128]{3,2,1,0:T(8,128)(2,1)} %panels_in), channel_id=1, source_target_pairs={{0,2},{1,3},{2,0},{3,1},{4,6},{5,7},{6,4},{7,5},{8,10},{9,11},{10,... | collective-permute-start | bytes 221192 | tf_op jit(solution)/shard_map/ppermute | solution.py:32
  5.1 2.5 %collective-permute-start = (bf16[2,96,384]{2,1,0:T(8,128)(2,1)S(1)}, bf16[2,96,384]{2,1,0:T(8,128)(2,1)S(1)}, u32[]{:S(2)}, u32[]{:S(2)}) collective-permute-start(bf16[2,96,384]{2,1,0:T(8,128)(2,1)S(1)} %get-tuple-element.18.near), channel_id=1, source_target_pairs={{0,1},{1,0},{2,3},{3,2},{4,5},{5,4},{6,7},{7,6},{8,9},{9,8},{10,11... | collective-permute-start | bytes 442376 | tf_op jit(solution)/shard_map/ppermute | solution.py:36
  6.3 1.3 %collective-permute-start.2 = (bf16[2,48,384]{2,1,0:T(8,128)(2,1)S(1)}, bf16[2,48,384]{2,1,0:T(8,128)(2,1)S(1)}, u32[]{:S(2)}, u32[]{:S(2)}) collective-permute-start(bf16[2,48,384]{2,1,0:T(8,128)(2,1)S(1)} %shard_map.60.block), channel_id=1, source_target_pairs={{0,1},{1,0},{2,3},{3,2},{4,5},{5,4},{6,7},{7,6},{8,9},{9,8},{10,11... | collective-permute-start | bytes 221192 | tf_op jit(solution)/shard_map/ppermute | solution.py:36
  7.7 5.2 %collective-permute-start.3 = (bf16[2,96,384]{2,1,0:T(8,128)(2,1)S(1)}, bf16[2,96,384]{2,1,0:T(8,128)(2,1)S(1)}, u32[]{:S(2)}, u32[]{:S(2)}) collective-permute-start(bf16[2,96,384]{2,1,0:T(8,128)(2,1)S(1)} %get-tuple-element.21), channel_id=1, source_target_pairs={{0,2},{1,9},{2,0},{3,11},{4,6},{5,13},{6,4},{7,15},{8,10},{9,1},{1... | collective-permute-start | bytes 442376 | tf_op jit(solution)/shard_map/ppermute | solution.py:32
  9.8 5.2 %collective-permute-start.5 = (bf16[2,96,384]{2,1,0:T(8,128)(2,1)S(1)}, bf16[2,96,384]{2,1,0:T(8,128)(2,1)S(1)}, u32[]{:S(2)}, u32[]{:S(2)}) collective-permute-start(bf16[2,96,384]{2,1,0:T(8,128)(2,1)S(1)} %get-tuple-element.22), channel_id=1, source_target_pairs={{0,2},{1,5},{2,0},{3,7},{4,6},{5,1},{6,4},{7,3},{8,10},{9,13},{10,... | collective-permute-start | bytes 442376 | tf_op jit(solution)/shard_map/ppermute | solution.py:32
  9.8 7.2 %collective-permute-start.7 = (bf16[2,96,384]{2,1,0:T(8,128)(2,1)S(1)}, bf16[2,96,384]{2,1,0:T(8,128)(2,1)S(1)}, u32[]{:S(2)}, u32[]{:S(2)}) collective-permute-start(bf16[2,96,384]{2,1,0:T(8,128)(2,1)S(1)} %get-tuple-element.23.block_0), channel_id=1, source_target_pairs={{0,2},{1,13},{2,0},{3,15},{4,6},{5,9},{6,4},{7,11},{8,10},{9,5},{1... | collective-permute-start | bytes 442376 | tf_op jit(solution)/shard_map/ppermute | solution.py:32
  12.9 4.2 %collective-permute-start.4 = (bf16[2,96,384]{2,1,0:T(8,128)(2,1)S(1)}, bf16[2,96,384]{2,1,0:T(8,128)(2,1)S(1)}, u32[]{:S(2)}, u32[]{:S(2)}) collective-permute-start(bf16[2,96,384]{2,1,0:T(8,128)(2,1)S(1)} %collective-permute-done.3.block_1), channel_id=1, source_target_pairs={{0,1},{1,0},{2,3},{3,2},{4,5},{5,4},{6,7},{7,6},{8,9},{9,8},{10,11... | collective-permute-start | bytes 442376 | tf_op jit(solution)/shard_map/ppermute | solution.py:36
  15.0 2.1 %collective-permute-start.6 = (bf16[2,96,384]{2,1,0:T(8,128)(2,1)S(1)}, bf16[2,96,384]{2,1,0:T(8,128)(2,1)S(1)}, u32[]{:S(2)}, u32[]{:S(2)}) collective-permute-start(bf16[2,96,384]{2,1,0:T(8,128)(2,1)S(1)} %collective-permute-done.5.block_2), channel_id=1, source_target_pairs={{0,1},{1,0},{2,3},{3,2},{4,5},{5,4},{6,7},{7,6},{8,9},{9,8},{10,11... | collective-permute-start | bytes 442376 | tf_op jit(solution)/shard_map/ppermute | solution.py:36
  15.4 1.3 %collective-permute-start.8 = (bf16[3,2,48,128]{3,2,1,0:T(8,128)(2,1)S(1)}, bf16[3,2,48,128]{3,2,1,0:T(8,128)(2,1)S(1)}, u32[]{:S(2)}, u32[]{:S(2)}) collective-permute-start(bf16[3,2,48,128]{3,2,1,0:T(8,128)(2,1)S(1)} %get-tuple-element.28.panels), channel_id=1, source_target_pairs={{0,1},{1,0},{2,3},{3,2},{4,5},{5,4},{6,7},{7,6},{8,9},{9,8},{10,11... | collective-permute-start | bytes 221192 | tf_op jit(solution)/shard_map/ppermute | solution.py:36
  15.5 1.4 %collective-permute-start.9 = (bf16[3,2,48,128]{3,2,1,0:T(8,128)(2,1)S(1)}, bf16[3,2,48,128]{3,2,1,0:T(8,128)(2,1)S(1)}, u32[]{:S(2)}, u32[]{:S(2)}) collective-permute-start(bf16[3,2,48,128]{3,2,1,0:T(8,128)(2,1)S(1)} %collective-permute-done.1.panels_far), channel_id=1, source_target_pairs={{0,1},{1,0},{2,3},{3,2},{4,5},{5,4},{6,7},{7,6},{8,9},{9,8},{10,11... | collective-permute-start | bytes 221192 | tf_op jit(solution)/shard_map/ppermute | solution.py:36
  18.0 3.1 %collective-permute-start.10 = (bf16[432,128]{1,0:T(8,128)(2,1)S(1)}, bf16[432,128]{1,0:T(8,128)(2,1)S(1)}, u32[]{:S(2)}, u32[]{:S(2)}) collective-permute-start(bf16[432,128]{1,0:T(8,128)(2,1)S(1)} %bitcast.7), channel_id=1, source_target_pairs={{0,1},{1,0},{2,3},{3,2},{4,5},{5,4},{6,7},{7,6},{8,9},{9,8},{10,11... | collective-permute-start | bytes 331784 | tf_op jit(solution)/shard_map/ppermute | solution.py:36
  18.9 4.7 %collective-permute-start.13 = (f16[384,128]{1,0:T(8,128)(2,1)S(1)}, f16[384,128]{1,0:T(8,128)(2,1)S(1)}, u32[]{:S(2)}, u32[]{:S(2)}) collective-permute-start(f16[384,128]{1,0:T(8,128)(2,1)S(1)} %bitcast.9), channel_id=1, source_target_pairs={{0,2},{1,9},{2,0},{3,11},{4,6},{5,13},{6,4},{7,15},{8,10},{9,1},{1... | collective-permute-start | bytes 294920 | tf_op jit(solution)/shard_map/ppermute | solution.py:32
  20.5 4.6 %collective-permute-start.14 = (f16[384,128]{1,0:T(8,128)(2,1)S(1)}, f16[384,128]{1,0:T(8,128)(2,1)S(1)}, u32[]{:S(2)}, u32[]{:S(2)}) collective-permute-start(f16[384,128]{1,0:T(8,128)(2,1)S(1)} %bitcast.10), channel_id=1, source_target_pairs={{0,2},{1,5},{2,0},{3,7},{4,6},{5,1},{6,4},{7,3},{8,10},{9,13},{10,... | collective-permute-start | bytes 294920 | tf_op jit(solution)/shard_map/ppermute | solution.py:32
  21.1 5.1 %collective-permute-start.11 = (f16[384,128]{1,0:T(8,128)(2,1)S(1)}, f16[384,128]{1,0:T(8,128)(2,1)S(1)}, u32[]{:S(2)}, u32[]{:S(2)}) collective-permute-start(f16[384,128]{1,0:T(8,128)(2,1)S(1)} %maximum_select_fusion), channel_id=1, source_target_pairs={{0,2},{1,13},{2,0},{3,15},{4,6},{5,9},{6,4},{7,11},{8,10},{9,5},{1... | collective-permute-start | bytes 294920 | tf_op jit(solution)/shard_map/ppermute | solution.py:32
  26.2 4.7 %collective-permute-start.15 = (f16[384,128]{1,0:T(8,128)(2,1)S(1)}, f16[384,128]{1,0:T(8,128)(2,1)S(1)}, u32[]{:S(2)}, u32[]{:S(2)}) collective-permute-start(f16[384,128]{1,0:T(8,128)(2,1)S(1)} %get-tuple-element.35), channel_id=1, source_target_pairs={{0,4},{1,3},{2,6},{3,1},{4,0},{5,7},{6,2},{7,5},{8,12},{9,11},{10,... | collective-permute-start | bytes 294920 | tf_op jit(solution)/shard_map/ppermute | solution.py:32
  27.4 2.5 %collective-permute-start.12 = (f16[144,128]{1,0:T(8,128)(2,1)S(1)}, f16[144,128]{1,0:T(8,128)(2,1)S(1)}, u32[]{:S(2)}, u32[]{:S(2)}) collective-permute-start(f16[144,128]{1,0:T(8,128)(2,1)S(1)} %get-tuple-element.36), channel_id=1, source_target_pairs={{0,1},{1,0},{2,3},{3,2},{4,5},{5,4},{6,7},{7,6},{8,9},{9,8},{10,11... | collective-permute-start | bytes 110600 | tf_op jit(solution)/shard_map/ppermute | solution.py:36
  29.0 2.2 %collective-permute-start.16 = (f16[384,128]{1,0:T(8,128)(2,1)S(1)}, f16[384,128]{1,0:T(8,128)(2,1)S(1)}, u32[]{:S(2)}, u32[]{:S(2)}) collective-permute-start(f16[384,128]{1,0:T(8,128)(2,1)S(1)} %get-tuple-element.35), channel_id=1, source_target_pairs={{0,1},{1,0},{2,3},{3,2},{4,5},{5,4},{6,7},{7,6},{8,9},{9,8},{10,11... | collective-permute-start | bytes 294920 | tf_op jit(solution)/shard_map/ppermute | solution.py:36
  30.9 1.3 %collective-permute-start.17 = (f16[384,128]{1,0:T(8,128)(2,1)S(1)}, f16[384,128]{1,0:T(8,128)(2,1)S(1)}, u32[]{:S(2)}, u32[]{:S(2)}) collective-permute-start(f16[384,128]{1,0:T(8,128)(2,1)S(1)} %collective-permute-done.15), channel_id=1, source_target_pairs={{0,1},{1,0},{2,3},{3,2},{4,5},{5,4},{6,7},{7,6},{8,9},{9,8},{10,11... | collective-permute-start | bytes 294920 | tf_op jit(solution)/shard_map/ppermute | solution.py:36

commit v7 on v6

--- a/solution.py
+++ b/solution.py
@@ -11,7 +11,8 @@
 
 AXES = ("prow", "pcol")
 MASKS = (4, 2, 6)
-MASKS_SUM = (4, 2, 6)
+MASKS_SUM = (2, 4, 6)
+STEP, LEVELS, LEVEL_ROWS = 16, 5, 16
 VMEM = pl.BlockSpec(memory_space=pltpu.VMEM)
 HBM = pl.BlockSpec(memory_space=pltpu.HBM)
 
@@ -30,6 +31,24 @@
             mask = mask0 if col == 0 else mask1
             pairs.append((row * cols + col, (row ^ mask) * cols + col))
     return lax.ppermute(value, AXES, pairs)
+
+
+def power(level, first, step):
+    value = jnp.full(level.shape, 2.0**first, jnp.float32)
+    for count in range(1, LEVELS + 1):
+        value = jnp.where(level > count - 0.5, 2.0 ** (first + step * count), value)
+    return value
+
+
+def level_of(peak, head):
+    level = jnp.zeros(peak.shape, jnp.float32)
+    for count in range(1, LEVELS + 1):
+        level += jnp.where(peak < 2.0 ** (head - STEP * count), 1.0, 0.0)
+    return level
+
+
+def largest(value):
+    return jnp.max(jnp.max(jnp.abs(value), axis=0, keepdims=True), axis=1, keepdims=True)
 
 
 def swap_core(value):
@@ -148,63 +167,74 @@
             out[far_or] = value if core == 0 else out[far_or] + value
 
 
-def whole_kernel(scale, near, near_core, far_0, far_1, block_0, block_1, block_2, block_3, kept, left, own, send, diag, columns):
+def left_kernel(panels, panels_far, panels_core, panels_far_core, out, rows):
+    supernodes, _, rows_half, width = panels.shape
+    for node in range(supernodes):
+        for part in range(2):
+            for far_or, (same, cross) in ((0, (panels, panels_core)), (1, (panels_far, panels_far_core))):
+                rows[far_or, 0] = cross[node, part]
+                rows[far_or, 1] = same[node, part]
+            out[node, part] = rows[...].reshape(4 * rows_half, width).T
+
+
+def columns_and_diagonal(orders, head, value_of, kept, left, own, send, diag, columns):
     supernodes, rows_half, width = own.shape
-    _, rows_dev, depth = near.shape
-    blocks = (block_0, block_1, block_2, block_3)
-    right = jnp.concatenate([block[core] for core in range(2) for block in blocks])
-    for far_or, pair in enumerate(((near_core, near), (far_0, far_1))):
-        both = jnp.concatenate([part[...].reshape(2 * rows_dev, depth) for part in pair], axis=1)
-        value = jnp.dot(both, right, preferred_element_type=jnp.float32)
+    rows_dev = 2 * rows_half
+    some = supernodes * rows_half
+    peak = jnp.zeros((1, 1), jnp.float32)
+    for far_or in range(2):
+        real, imag = value_of(far_or)
         for node in range(supernodes):
             lanes = slice(node * width, (node + 1) * width)
             keep = kept[far_or, :, node : node + 1]
-            column = value[:rows_dev, lanes] + turned(value[rows_dev:, lanes])
-            column = (-(column * keep)).astype(jnp.bfloat16)
+            column = (-((real[:, lanes] + turned(imag[:, lanes])) * keep)).astype(jnp.bfloat16)
             columns[node, far_or] = column
-            low, high = column[:rows_half], column[rows_half:]
             if far_or == 0:
-                send[0, node], own[node] = low, high
+                send[node * rows_half : (node + 1) * rows_half] = column[:rows_half]
+                own[node] = column[rows_half:]
             else:
-                send[1, node], send[2, node] = low, high
+                peak = jnp.maximum(peak, largest(column.astype(jnp.float32)))
+    level = level_of(peak, 13)
+    factor = power(level, 0, STEP)
+    send[3 * some :] = jnp.broadcast_to(level, (LEVEL_ROWS, width)).astype(jnp.bfloat16)
+    for node in range(supernodes):
+        column = (columns[node, 1].astype(jnp.float32) * factor).astype(jnp.bfloat16)
+        start = some + node * rows_half
+        send[start : start + rows_half] = column[:rows_half]
+        send[start + some : start + some + rows_half] = column[rows_half:]
+    values = []
+    peak = jnp.zeros((1, 1), jnp.float32)
     for node in range(supernodes):
         both = jnp.dot(
             left[node].reshape(2 * width, 2 * rows_dev),
             columns[node].reshape(2 * rows_dev, width),
             preferred_element_type=jnp.float32,
         )
-        diag[node] = (both[:width] + turned(both[width:])) * (1.0 / scale)
-
-
-def left_kernel(panels, panels_far, panels_core, panels_far_core, out, rows):
-    supernodes, _, rows_half, width = panels.shape
-    for node in range(supernodes):
-        for part in range(2):
-            for far_or, (same, cross) in ((0, (panels, panels_core)), (1, (panels_far, panels_far_core))):
-                rows[far_or, 0] = cross[node, part]
-                rows[far_or, 1] = same[node, part]
-            out[node, part] = rows[...].reshape(4 * rows_half, width).T
-
-
-def diagonal_kernel(scale, kept, product, left, own, send, diag, columns):
-    supernodes, _, width, _ = left.shape
-    rows_dev = product.shape[2]
-    rows_half = rows_dev // 2
-    for node in range(supernodes):
-        lanes = slice(node * width, (node + 1) * width)
-        for far_or in range(2):
-            keep = kept[far_or, :, node : node + 1]
-            value = product[far_or, 0, :, lanes] + turned(product[far_or, 1, :, lanes])
-            value = (-(value * keep)).astype(jnp.bfloat16)
-            columns[far_or] = value
-            low, high = value[:rows_half], value[rows_half:]
-            if far_or == 0:
-                send[0, node], own[node] = low, high
-            else:
-                send[1, node], send[2, node] = low, high
-        right = columns[...].reshape(2 * rows_dev, width)
-        both = jnp.dot(left[node].reshape(2 * width, 2 * rows_dev), right, preferred_element_type=jnp.float32)
-        diag[node] = (both[:width] + turned(both[width:])) * (1.0 / scale)
+        values.append(both[:width] + turned(both[width:]))
+        peak = jnp.maximum(peak, largest(values[-1]))
+    level = level_of(peak, head + orders)
+    factor = power(level, -orders, STEP)
+    for node, value in enumerate(values):
+        diag[node * width : (node + 1) * width] = value * factor
+    diag[supernodes * width :] = jnp.broadcast_to(level, (LEVEL_ROWS, width))
+
+
+def diagonal_kernel(orders, head, product, *refs):
+    columns_and_diagonal(orders, head, lambda far_or: (product[far_or, 0], product[far_or, 1]), *refs)
+
+
+def whole_kernel(orders, head, near, near_core, far_0, far_1, block_0, block_1, block_2, block_3, *refs):
+    _, rows_dev, depth = near.shape
+    blocks = (block_0, block_1, block_2, block_3)
+    right = jnp.concatenate([block[core] for core in range(2) for block in blocks])
+
+    def value_of(far_or):
+        pair = ((near_core, near), (far_0, far_1))[far_or]
+        both = jnp.concatenate([part[...].reshape(2 * rows_dev, depth) for part in pair], axis=1)
+        value = jnp.dot(both, right, preferred_element_type=jnp.float32)
+        return value[:rows_dev], value[rows_dev:]
+
+    columns_and_diagonal(orders, head, value_of, *refs)
 
 
 def unpack(near, far):
@@ -221,20 +251,24 @@
     for node in range(supernodes):
         rows = slice(node * rows_half, (node + 1) * rows_half)
         near = jnp.where(first, own_core[rows].astype(jnp.float32), own[rows].astype(jnp.float32))
-        far = jnp.where(first, other[rows], other_core[rows])
+        far = jnp.where(first, other[rows].astype(jnp.float32), other_core[rows].astype(jnp.float32))
         real, imag = unpack(near, far)
         out[node, 0] = real.astype(jnp.bfloat16)
         out[node, 1] = imag.astype(jnp.bfloat16)
 
 
-def final_kernel(scale, diag_inverse, mine, far, mine_core, far_core, out, value, done):
+def final_kernel(orders, diag_inverse, mine, far, mine_core, far_core, out, value, done):
     supernodes, _, width, _ = out.shape
     first = lax.axis_index("pcol") == 0
+    end = supernodes * width
+    near_level = jnp.where(first, mine_core[end : end + 1], mine[end : end + 1])
+    far_level = jnp.where(first, far_core[end : end + 1], far[end : end + 1])
+    near_scale, far_scale = power(near_level, orders, -STEP), power(far_level, orders, -STEP)
     copies = [pltpu.make_async_copy(value.at[node], out.at[node], done.at[node]) for node in range(supernodes)]
     for node in range(supernodes):
         rows = slice(node * width, (node + 1) * width)
-        near_value = jnp.where(first, mine_core[rows], mine[rows]) * scale
-        far_value = jnp.where(first, far_core[rows], far[rows]) * scale
+        near_value = jnp.where(first, mine_core[rows], mine[rows]) * near_scale
+        far_value = jnp.where(first, far_core[rows], far[rows]) * far_scale
         real, imag = unpack(near_value, far_value)
         value[node, 0] = diag_inverse[node, 0].astype(jnp.float32) - real
         value[node, 1] = diag_inverse[node, 1].astype(jnp.float32) - imag
@@ -302,22 +336,25 @@
             [panels, panels_far, panels_core, panels_far_core],
             [pltpu.VMEM((2, cols, rows_half, width), bf16)],
         )
-        scale = 2 ** max(0, math.ceil(math.log2(groups * 2 * rows_half / 24)))
+        orders = max(0, math.ceil(math.log2(groups * 2 * rows_half / 24)))
+        head = 15 - int(math.log2(rows // 2))
+        count = supernodes * width
+        some = supernodes * rows_half
         outs = [
             ((supernodes, rows_half, width), bf16),
-            ((3, supernodes, rows_half, width), bf16),
-            ((supernodes, width, width), f32),
+            ((3 * some + LEVEL_ROWS, width), bf16),
+            ((count + LEVEL_ROWS, width), f32),
         ]
         sums = (2, 2, rows_dev, lanes)
-        columns_scratch = pltpu.VMEM((2, rows_dev, width), bf16)
+        columns_scratch = pltpu.VMEM((supernodes, 2, rows_dev, width), bf16)
         lefts = [near, near_core, far_0, far_1]
         arrived = list(lax.optimization_barrier(tuple(arrived)))
         if rows == 8:
             own, send, diag = call(
-                functools.partial(whole_kernel, float(scale)),
+                functools.partial(whole_kernel, orders, head),
                 outs,
                 lefts + [chip] + arrived + [keep, left],
-                [pltpu.VMEM((supernodes, 2, rows_dev, width), bf16)],
+                [columns_scratch],
             )
         else:
             held = jnp.stack([chip] + arrived)
@@ -327,36 +364,39 @@
                 size *= 2
             (product,) = call(product_kernel, [(sums, f32)], lefts + [held])
             own, send, diag = call(
-                functools.partial(diagonal_kernel, float(scale)), outs, [keep, product, left], [columns_scratch]
+                functools.partial(diagonal_kernel, orders, head), outs, [product, keep, left], [columns_scratch]
             )
         f16 = jnp.float16
-        count = supernodes * width
-        some = supernodes * rows_half
-        term = diag.reshape(count, width).astype(f16)
-        sent = swap_core(send.reshape(3 * some, width))
-        last = jnp.concatenate([sent[some:].astype(f16), term[2 * some :]])
+        term = diag.astype(f16)
+        sent = swap_core(send)
+        last = jnp.concatenate([sent[some:].astype(f16), term[2 * some + LEVEL_ROWS :]])
         last = jnp.where(col_index == 0, last, term)
         terms = [swap(v, rows, cols, 1, mask) for mask, v in zip(MASKS_SUM, (term, term, last))]
-        other = terms[2]
-        first, second, third = [t.astype(f32) for t in terms]
-        total = (term.astype(f32) + first) + (second + third)
+        wide = [t.astype(f32) for t in [term] + terms]
+        levels = [t[count : count + 1] for t in wide]
+        mine, first, second, third = [t[:count] * power(v, orders, -STEP) for t, v in zip(wide, levels)]
+        total = (mine + first) + (second + third)
+        level = functools.reduce(jnp.minimum, levels)
         size = 8
         while size < rows:
-            total = total + swap(total, rows, cols, 1, size)
+            other = swap(jnp.concatenate([total, jnp.broadcast_to(level, (8, width))]), rows, cols, 1, size)
+            total, level = total + other[:count], jnp.minimum(level, other[count : count + 1])
             size *= 2
-        mine = total.astype(f16)
+        total = total * power(level, -orders, STEP)
+        mine = jnp.concatenate([total, jnp.broadcast_to(level, (LEVEL_ROWS, width))]).astype(f16)
         far = swap(mine, rows, cols, 2, 1)
+        other = wide[3][: 2 * some] * power(wide[3][2 * some : 2 * some + 1], 0, -STEP)
+        other = other.astype(bf16)
         (columns,) = call(
             columns_kernel,
             [((supernodes, 2, rows_half, width), bf16)],
-            [own.reshape(some, width), sent[:some], other[:some].astype(f32), swap_core(other[some : 2 * some]).astype(f32)],
-            cost=4 << 20,
+            [own.reshape(some, width), sent[:some], other[:some], swap_core(other[some:])],
         )
         far_sent = far
         far_sent = after(far, columns)
         pieces = [v.astype(f32) for v in (mine, far, swap_core(mine), swap_core(far_sent))]
         (diag,) = call(
-            functools.partial(final_kernel, float(scale)),
+            functools.partial(final_kernel, orders),
             [((supernodes, 2, width, width), f32)],
             [diag_inverse] + pieces,
             [pltpu.VMEM((supernodes, 2, width, width), f32), pltpu.SemaphoreType.DMA((supernodes,))],

time: 33.3 us -> 33.7 us (1.012)
  transfers between devices with their start and end apart: 18 -> 18, of which waited for: 11 -> 11; matrix products, arithmetic and copies ran while one was open for 0% -> 1% of each run, Pallas kernels for 7% -> 7%
where the time goes in v7:
time: 33.7 us; the launch traced here: 33.6 us
  starting transfers between devices  18.1 us (54%)
  waiting for transfers between devices  9.8 us (29%)
  Pallas kernels  4.47 us (13%)
  between operations  0.82 us (2%)
    ppermute x8, starting transfers between devices, swap(): return lax.ppermute(value, AXES, pairs)  11.9 us
    ppermute x10, starting transfers between devices, swap_core(): return lax.ppermute(value, 'pcol', [(0, 1), (1, 0)])  6.2 us
    ppermute x8, waiting for transfers between devices, swap(): return lax.ppermute(value, AXES, pairs)  5.93 us
    pallas_call x7, Pallas kernels, call(): pl.pallas_call(kernel, out_shape=shapes, in_specs=[space] * len(operands)...  4.47 us
    ppermute x10, waiting for transfers between devices, swap_core(): return lax.ppermute(value, 'pcol', [(0, 1), (1, 0)])  3.88 us
  transfers between devices with their start and end apart: 18, of which 11 were waited for; matrix products, arithmetic and copies ran while one was open for 1% of the time, Pallas kernels for 7%

profile of v7, /device:TPU:0, one launch (start us, length us, event | category | flops | bytes accessed | tf_op | source)
XLA Modules:
  0.0 33.6 jit_solution(6772796854672339114)
XLA Ops:
  0.6 3.0 %collective-permute-start.1 = (bf16[3,2,48,128]{3,2,1,0:T(8,128)(2,1)}, bf16[3,2,48,128]{3,2,1,0:T(8,128)(2,1)S(1)}, u32[]{:S(2)}, u32[]{:S(2)}) collective-permute-start(bf16[3,2,48,128]{3,2,1,0:T(8,128)(2,1)} %panels_in), channel_id=1, source_target_pairs={{0,2},{1,3},{2,0},{3,1},{4,6},{5,7},{6,4},{7,5},{8,10},{9,11},{10,... | collective-permute-start | bytes 221192 | tf_op jit(solution)/shard_map/ppermute | solution.py:33
  3.6 1.5 %shard_map.59 = (bf16[2,96,384]{2,1,0:T(8,128)(2,1)S(1)}, bf16[3,2,48,128]{3,2,1,0:T(8,128)(2,1)S(1)}, bf16[3,2,128,128]{3,2,1,0:T(8,128)(2,1)S(1)}, f32[2,96,12...) custom-call(bf16[2,8,1,48,96]{4,3,2,1,0:T(8,128)(2,1)} %matrix_in.1, ...), custom_call_target="tpu_custom_call" | custom-call | bytes 12582912 | tf_op jit(solution)/shard_map/pallas_call | solution.py:69
  5.1 0.1 collective-permute-start
  5.2 1.0 %collective-permute-done.1.panels_far = bf16[3,2,48,128]{3,2,1,0:T(8,128)(2,1)S(1)} collective-permute-done((bf16[3,2,48,128]{3,2,1,0:T(8,128)(2,1)}, bf16[3,2,48,128]{3,2,1,0:T(8,128)(2,1)S(1)}, u32[]{:S(2)}, u32[]{:S(2)}) %collective-permute-start.1) | collective-permute-done | bytes 73760 | tf_op jit(solution)/shard_map/ppermute | solution.py:33
  6.2 0.1 shard_map.60.block
  6.3 0.1 collective-permute-start.2
  6.4 1.3 %collective-permute-done.2.block_core = bf16[2,48,384]{2,1,0:T(8,128)(2,1)S(1)} collective-permute-done((bf16[2,48,384]{2,1,0:T(8,128)(2,1)S(1)}, bf16[2,48,384]{2,1,0:T(8,128)(2,1)S(1)}, u32[]{:S(2)}, u32[]{:S(2)}) %collective-permute-start.2) | collective-permute-done | bytes 73760 | tf_op jit(solution)/shard_map/ppermute | solution.py:55
  7.6 0.0 collective-permute-done.near_core
  7.7 2.1 %collective-permute-start.3 = (bf16[2,96,384]{2,1,0:T(8,128)(2,1)S(1)}, bf16[2,96,384]{2,1,0:T(8,128)(2,1)S(1)}, u32[]{:S(2)}, u32[]{:S(2)}) collective-permute-start(bf16[2,96,384]{2,1,0:T(8,128)(2,1)S(1)} %get-tuple-element.21), channel_id=1, source_target_pairs={{0,2},{1,9},{2,0},{3,11},{4,6},{5,13},{6,4},{7,15},{8,10},{9,1},{1... | collective-permute-start | bytes 442376 | tf_op jit(solution)/shard_map/ppermute | solution.py:33
  9.8 0.1 collective-permute-start.5
  9.8 1.9 %collective-permute-start.7 = (bf16[2,96,384]{2,1,0:T(8,128)(2,1)S(1)}, bf16[2,96,384]{2,1,0:T(8,128)(2,1)S(1)}, u32[]{:S(2)}, u32[]{:S(2)}) collective-permute-start(bf16[2,96,384]{2,1,0:T(8,128)(2,1)S(1)} %get-tuple-element.23.block_0), channel_id=1, source_target_pairs={{0,2},{1,13},{2,0},{3,15},{4,6},{5,9},{6,4},{7,11},{8,10},{9,5},{1... | collective-permute-start | bytes 442376 | tf_op jit(solution)/shard_map/ppermute | solution.py:33
  11.8 1.1 %collective-permute-done.3.block_1 = bf16[2,96,384]{2,1,0:T(8,128)(2,1)S(1)} collective-permute-done((bf16[2,96,384]{2,1,0:T(8,128)(2,1)S(1)}, bf16[2,96,384]{2,1,0:T(8,128)(2,1)S(1)}, u32[]{:S(2)}, u32[]{:S(2)}) %collective-permute-start.3) | collective-permute-done | bytes 147488 | tf_op jit(solution)/shard_map/ppermute | solution.py:33
  12.9 2.1 %collective-permute-start.4 = (bf16[2,96,384]{2,1,0:T(8,128)(2,1)S(1)}, bf16[2,96,384]{2,1,0:T(8,128)(2,1)S(1)}, u32[]{:S(2)}, u32[]{:S(2)}) collective-permute-start(bf16[2,96,384]{2,1,0:T(8,128)(2,1)S(1)} %collective-permute-done.3.block_1), channel_id=1, source_target_pairs={{0,1},{1,0},{2,3},{3,2},{4,5},{5,4},{6,7},{7,6},{8,9},{9,8},{10,11... | collective-permute-start | bytes 442376 | tf_op jit(solution)/shard_map/ppermute | solution.py:55
  15.0 0.0 collective-permute-done.5.block_2
  15.0 0.5 %collective-permute-start.6 = (bf16[2,96,384]{2,1,0:T(8,128)(2,1)S(1)}, bf16[2,96,384]{2,1,0:T(8,128)(2,1)S(1)}, u32[]{:S(2)}, u32[]{:S(2)}) collective-permute-start(bf16[2,96,384]{2,1,0:T(8,128)(2,1)S(1)} %collective-permute-done.5.block_2), channel_id=1, source_target_pairs={{0,1},{1,0},{2,3},{3,2},{4,5},{5,4},{6,7},{7,6},{8,9},{9,8},{10,11... | collective-permute-start | bytes 442376 | tf_op jit(solution)/shard_map/ppermute | solution.py:55
  15.4 0.0 collective-permute-start.8
  15.5 0.5 %collective-permute-start.9 = (bf16[3,2,48,128]{3,2,1,0:T(8,128)(2,1)S(1)}, bf16[3,2,48,128]{3,2,1,0:T(8,128)(2,1)S(1)}, u32[]{:S(2)}, u32[]{:S(2)}) collective-permute-start(bf16[3,2,48,128]{3,2,1,0:T(8,128)(2,1)S(1)} %collective-permute-done.1.panels_far), channel_id=1, source_target_pairs={{0,1},{1,0},{2,3},{3,2},{4,5},{5,4},{6,7},{7,6},{8,9},{9,8},{10,11... | collective-permute-start | bytes 221192 | tf_op jit(solution)/shard_map/ppermute | solution.py:55
  16.0 0.8 %collective-permute-done.8.panels_core = bf16[3,2,48,128]{3,2,1,0:T(8,128)(2,1)S(1)} collective-permute-done((bf16[3,2,48,128]{3,2,1,0:T(8,128)(2,1)S(1)}, bf16[3,2,48,128]{3,2,1,0:T(8,128)(2,1)S(1)}, u32[]{:S(2)}, u32[]{:S(2)}) %collective-permute-start.8) | collective-permute-done | bytes 73760 | tf_op jit(solution)/shard_map/ppermute | solution.py:55
  16.7 0.2 collective-permute-done.9.panels_far_core
  16.9 0.2 shard_map.62.refs_1_
  17.1 0.0 collective-permute-done.7.block_3
  17.1 0.0 collective-permute-done.4.far_0
  17.1 0.0 collective-permute-done.6.far_1
  17.1 1.1 %shard_map.63 = (bf16[3,48,128]{2,1,0:T(8,128)(2,1)S(1)}, bf16[448,128]{1,0:T(8,128)(2,1)S(1)}, f32[400,128]{1,0:T(8,128)S(1)}) custom-call(bf16[2,96,384]{2,1,0:T(8,128)(2,1)S(1)} %get-tuple-element.18.near, bf16[2,96,384]{2,1,0:T(8,128)(2,1)S(1)} %collective-permute-done.near_core, bf16[2,96,384]{2,1,0:T(8,128)(2,1)S(1)} %collective-permute-done.4.far_0, ...), custom_call_target="tpu_custom_call" | custom-call | bytes 1929216 | tf_op jit(solution)/shard_map/pallas_call | solution.py:69
  18.1 0.9 %collective-permute-start.10 = (bf16[448,128]{1,0:T(8,128)(2,1)S(1)}, bf16[448,128]{1,0:T(8,128)(2,1)S(1)}, u32[]{:S(2)}, u32[]{:S(2)}) collective-permute-start(bf16[448,128]{1,0:T(8,128)(2,1)S(1)} %get-tuple-element.30), channel_id=1, source_target_pairs={{0,1},{1,0},{2,3},{3,2},{4,5},{5,4},{6,7},{7,6},{8,9},{9,8},{10,11... | collective-permute-start | bytes 344072 | tf_op jit(solution)/shard_map/ppermute | solution.py:55
  19.1 1.6 %collective-permute-start.13 = (f16[400,128]{1,0:T(8,128)(2,1)S(1)}, f16[400,128]{1,0:T(8,128)(2,1)S(1)}, u32[]{:S(2)}, u32[]{:S(2)}) collective-permute-start(f16[400,128]{1,0:T(8,128)(2,1)S(1)} %get-tuple-element.37), channel_id=1, source_target_pairs={{0,2},{1,5},{2,0},{3,7},{4,6},{5,1},{6,4},{7,3},{8,10},{9,13},{10,... | collective-permute-start | bytes 307208 | tf_op jit(solution)/shard_map/ppermute | solution.py:33
  20.7 0.5 %collective-permute-start.14 = (f16[400,128]{1,0:T(8,128)(2,1)S(1)}, f16[400,128]{1,0:T(8,128)(2,1)S(1)}, u32[]{:S(2)}, u32[]{:S(2)}) collective-permute-start(f16[400,128]{1,0:T(8,128)(2,1)S(1)} %get-tuple-element.37), channel_id=1, source_target_pairs={{0,2},{1,9},{2,0},{3,11},{4,6},{5,13},{6,4},{7,15},{8,10},{9,1},{1... | collective-permute-start | bytes 307208 | tf_op jit(solution)/shard_map/ppermute | solution.py:33
  21.2 0.0 collective-permute-done.10
  21.3 1.6 %collective-permute-start.11 = (f16[400,128]{1,0:T(8,128)(2,1)S(1)}, f16[400,128]{1,0:T(8,128)(2,1)S(1)}, u32[]{:S(2)}, u32[]{:S(2)}) collective-permute-start(f16[400,128]{1,0:T(8,128)(2,1)S(1)} %maximum_select_fusion), channel_id=1, source_target_pairs={{0,2},{1,13},{2,0},{3,15},{4,6},{5,9},{6,4},{7,11},{8,10},{9,5},{1... | collective-permute-start | bytes 307208 | tf_op jit(solution)/shard_map/ppermute | solution.py:33
  22.8 1.0 %collective-permute-done.13 = f16[400,128]{1,0:T(8,128)(2,1)S(1)} collective-permute-done((f16[400,128]{1,0:T(8,128)(2,1)S(1)}, f16[400,128]{1,0:T(8,128)(2,1)S(1)}, u32[]{:S(2)}, u32[]{:S(2)}) %collective-permute-start.13) | collective-permute-done | bytes 102432 | tf_op jit(solution)/shard_map/ppermute | solution.py:33
  23.9 1.5 %collective-permute-done.14 = f16[400,128]{1,0:T(8,128)(2,1)S(1)} collective-permute-done((f16[400,128]{1,0:T(8,128)(2,1)S(1)}, f16[400,128]{1,0:T(8,128)(2,1)S(1)}, u32[]{:S(2)}, u32[]{:S(2)}) %collective-permute-start.14) | collective-permute-done | bytes 102432 | tf_op jit(solution)/shard_map/ppermute | solution.py:33
  25.3 1.1 %collective-permute-done.11 = f16[400,128]{1,0:T(8,128)(2,1)S(1)} collective-permute-done((f16[400,128]{1,0:T(8,128)(2,1)S(1)}, f16[400,128]{1,0:T(8,128)(2,1)S(1)}, u32[]{:S(2)}, u32[]{:S(2)}) %collective-permute-start.11) | collective-permute-done | bytes 102432 | tf_op jit(solution)/shard_map/ppermute | solution.py:33
  26.5 0.1 fusion.3
  26.6 1.2 %collective-permute-start.15 = (f16[400,128]{1,0:T(8,128)(2,1)S(1)}, f16[400,128]{1,0:T(8,128)(2,1)S(1)}, u32[]{:S(2)}, u32[]{:S(2)}) collective-permute-start(f16[400,128]{1,0:T(8,128)(2,1)S(1)} %get-tuple-element.43), channel_id=1, source_target_pairs={{0,4},{1,3},{2,6},{3,1},{4,0},{5,7},{6,2},{7,5},{8,12},{9,11},{10,... | collective-permute-start | bytes 307208 | tf_op jit(solution)/shard_map/ppermute | solution.py:33
  27.8 1.7 %collective-permute-start.12 = (bf16[144,128]{1,0:T(8,128)(2,1)S(1)}, bf16[144,128]{1,0:T(8,128)(2,1)S(1)}, u32[]{:S(2)}, u32[]{:S(2)}) collective-permute-start(bf16[144,128]{1,0:T(8,128)(2,1)S(1)} %get-tuple-element.45), channel_id=1, source_target_pairs={{0,1},{1,0},{2,3},{3,2},{4,5},{5,4},{6,7},{7,6},{8,9},{9,8},{10,11... | collective-permute-start | bytes 110600 | tf_op jit(solution)/shard_map/ppermute | solution.py:55
  29.5 0.1 collective-permute-start.16
  29.6 0.8 %collective-permute-done.12.other_core = bf16[144,128]{1,0:T(8,128)(2,1)S(1)} collective-permute-done((bf16[144,128]{1,0:T(8,128)(2,1)S(1)}, bf16[144,128]{1,0:T(8,128)(2,1)S(1)}, u32[]{:S(2)}, u32[]{:S(2)}) %collective-permute-start.12) | collective-permute-done | bytes 36896 | tf_op jit(solution)/shard_map/ppermute | solution.py:55
  30.3 0.7 %shard_map.64 = bf16[3,2,48,128]{3,2,1,0:T(8,128)(2,1)} custom-call(bf16[144,128]{1,0:T(8,128)(2,1)S(1)} %bitcast.15, bf16[144,128]{1,0:T(8,128)(2,1)S(1)} %slice.60.own_core, bf16[144,128]{1,0:T(8,128)(2,1)S(1)} %get-tuple-element.46.other, bf16[144,128]{1,0:T(8,128)(2,1)S(1)} %collective-permute-done.12.other_core), custom_call_target="tpu_custom_call" | custom-call | bytes 221184 | tf_op jit(solution)/shard_map/pallas_call | solution.py:69
  31.1 0.3 collective-permute-done.15
  31.3 0.3 collective-permute-start.17
  31.7 0.0 collective-permute-done.16
  31.7 0.9 %collective-permute-done.17 = f16[400,128]{1,0:T(8,128)(2,1)S(1)} collective-permute-done((f16[400,128]{1,0:T(8,128)(2,1)S(1)}, f16[400,128]{1,0:T(8,128)(2,1)S(1)}, u32[]{:S(2)}, u32[]{:S(2)}) %collective-permute-start.17) | collective-permute-done | bytes 102432 | tf_op jit(solution)/shard_map/ppermute | solution.py:55
  32.7 0.9 %shard_map.65 = f32[3,2,128,128]{3,2,1,0:T(8,128)} custom-call(bf16[3,2,128,128]{3,2,1,0:T(8,128)(2,1)S(1)} %get-tuple-element.32.diag_inverse, f32[400,128]{1,0:T(8,128)S(1)} %get-tuple-element.44.mine, f32[400,128]{1,0:T(8,128)S(1)} %convert_element_type.42.far, f32[400,128]{1,0:T(8,128)S(1)} %convert_element_type.43.mine_core, ...), custom_call_target="tpu_custom_call" | custom-call | bytes 1409024 | tf_op jit(solution)/shard_map/pallas_call | solution.py:69
  (18 shorter events, 0.3 us)
Async XLA Ops:
  0.6 5.5 %collective-permute-start.1 = (bf16[3,2,48,128]{3,2,1,0:T(8,128)(2,1)}, bf16[3,2,48,128]{3,2,1,0:T(8,128)(2,1)S(1)}, u32[]{:S(2)}, u32[]{:S(2)}) collective-permute-start(bf16[3,2,48,128]{3,2,1,0:T(8,128)(2,1)} %panels_in), channel_id=1, source_target_pairs={{0,2},{1,3},{2,0},{3,1},{4,6},{5,7},{6,4},{7,5},{8,10},{9,11},{10,... | collective-permute-start | bytes 221192 | tf_op jit(solution)/shard_map/ppermute | solution.py:33
  5.1 2.5 %collective-permute-start = (bf16[2,96,384]{2,1,0:T(8,128)(2,1)S(1)}, bf16[2,96,384]{2,1,0:T(8,128)(2,1)S(1)}, u32[]{:S(2)}, u32[]{:S(2)}) collective-permute-start(bf16[2,96,384]{2,1,0:T(8,128)(2,1)S(1)} %get-tuple-element.18.near), channel_id=1, source_target_pairs={{0,1},{1,0},{2,3},{3,2},{4,5},{5,4},{6,7},{7,6},{8,9},{9,8},{10,11... | collective-permute-start | bytes 442376 | tf_op jit(solution)/shard_map/ppermute | solution.py:55
  6.3 1.3 %collective-permute-start.2 = (bf16[2,48,384]{2,1,0:T(8,128)(2,1)S(1)}, bf16[2,48,384]{2,1,0:T(8,128)(2,1)S(1)}, u32[]{:S(2)}, u32[]{:S(2)}) collective-permute-start(bf16[2,48,384]{2,1,0:T(8,128)(2,1)S(1)} %shard_map.60.block), channel_id=1, source_target_pairs={{0,1},{1,0},{2,3},{3,2},{4,5},{5,4},{6,7},{7,6},{8,9},{9,8},{10,11... | collective-permute-start | bytes 221192 | tf_op jit(solution)/shard_map/ppermute | solution.py:55
  7.7 5.2 %collective-permute-start.3 = (bf16[2,96,384]{2,1,0:T(8,128)(2,1)S(1)}, bf16[2,96,384]{2,1,0:T(8,128)(2,1)S(1)}, u32[]{:S(2)}, u32[]{:S(2)}) collective-permute-start(bf16[2,96,384]{2,1,0:T(8,128)(2,1)S(1)} %get-tuple-element.21), channel_id=1, source_target_pairs={{0,2},{1,9},{2,0},{3,11},{4,6},{5,13},{6,4},{7,15},{8,10},{9,1},{1... | collective-permute-start | bytes 442376 | tf_op jit(solution)/shard_map/ppermute | solution.py:33
  9.8 5.2 %collective-permute-start.5 = (bf16[2,96,384]{2,1,0:T(8,128)(2,1)S(1)}, bf16[2,96,384]{2,1,0:T(8,128)(2,1)S(1)}, u32[]{:S(2)}, u32[]{:S(2)}) collective-permute-start(bf16[2,96,384]{2,1,0:T(8,128)(2,1)S(1)} %get-tuple-element.22), channel_id=1, source_target_pairs={{0,2},{1,5},{2,0},{3,7},{4,6},{5,1},{6,4},{7,3},{8,10},{9,13},{10,... | collective-permute-start | bytes 442376 | tf_op jit(solution)/shard_map/ppermute | solution.py:33
  9.8 7.2 %collective-permute-start.7 = (bf16[2,96,384]{2,1,0:T(8,128)(2,1)S(1)}, bf16[2,96,384]{2,1,0:T(8,128)(2,1)S(1)}, u32[]{:S(2)}, u32[]{:S(2)}) collective-permute-start(bf16[2,96,384]{2,1,0:T(8,128)(2,1)S(1)} %get-tuple-element.23.block_0), channel_id=1, source_target_pairs={{0,2},{1,13},{2,0},{3,15},{4,6},{5,9},{6,4},{7,11},{8,10},{9,5},{1... | collective-permute-start | bytes 442376 | tf_op jit(solution)/shard_map/ppermute | solution.py:33
  12.9 4.2 %collective-permute-start.4 = (bf16[2,96,384]{2,1,0:T(8,128)(2,1)S(1)}, bf16[2,96,384]{2,1,0:T(8,128)(2,1)S(1)}, u32[]{:S(2)}, u32[]{:S(2)}) collective-permute-start(bf16[2,96,384]{2,1,0:T(8,128)(2,1)S(1)} %collective-permute-done.3.block_1), channel_id=1, source_target_pairs={{0,1},{1,0},{2,3},{3,2},{4,5},{5,4},{6,7},{7,6},{8,9},{9,8},{10,11... | collective-permute-start | bytes 442376 | tf_op jit(solution)/shard_map/ppermute | solution.py:55
  15.0 2.1 %collective-permute-start.6 = (bf16[2,96,384]{2,1,0:T(8,128)(2,1)S(1)}, bf16[2,96,384]{2,1,0:T(8,128)(2,1)S(1)}, u32[]{:S(2)}, u32[]{:S(2)}) collective-permute-start(bf16[2,96,384]{2,1,0:T(8,128)(2,1)S(1)} %collective-permute-done.5.block_2), channel_id=1, source_target_pairs={{0,1},{1,0},{2,3},{3,2},{4,5},{5,4},{6,7},{7,6},{8,9},{9,8},{10,11... | collective-permute-start | bytes 442376 | tf_op jit(solution)/shard_map/ppermute | solution.py:55
  15.4 1.3 %collective-permute-start.8 = (bf16[3,2,48,128]{3,2,1,0:T(8,128)(2,1)S(1)}, bf16[3,2,48,128]{3,2,1,0:T(8,128)(2,1)S(1)}, u32[]{:S(2)}, u32[]{:S(2)}) collective-permute-start(bf16[3,2,48,128]{3,2,1,0:T(8,128)(2,1)S(1)} %get-tuple-element.28.panels), channel_id=1, source_target_pairs={{0,1},{1,0},{2,3},{3,2},{4,5},{5,4},{6,7},{7,6},{8,9},{9,8},{10,11... | collective-permute-start | bytes 221192 | tf_op jit(solution)/shard_map/ppermute | solution.py:55
  15.5 1.4 %collective-permute-start.9 = (bf16[3,2,48,128]{3,2,1,0:T(8,128)(2,1)S(1)}, bf16[3,2,48,128]{3,2,1,0:T(8,128)(2,1)S(1)}, u32[]{:S(2)}, u32[]{:S(2)}) collective-permute-start(bf16[3,2,48,128]{3,2,1,0:T(8,128)(2,1)S(1)} %collective-permute-done.1.panels_far), channel_id=1, source_target_pairs={{0,1},{1,0},{2,3},{3,2},{4,5},{5,4},{6,7},{7,6},{8,9},{9,8},{10,11... | collective-permute-start | bytes 221192 | tf_op jit(solution)/shard_map/ppermute | solution.py:55
  18.1 3.1 %collective-permute-start.10 = (bf16[448,128]{1,0:T(8,128)(2,1)S(1)}, bf16[448,128]{1,0:T(8,128)(2,1)S(1)}, u32[]{:S(2)}, u32[]{:S(2)}) collective-permute-start(bf16[448,128]{1,0:T(8,128)(2,1)S(1)} %get-tuple-element.30), channel_id=1, source_target_pairs={{0,1},{1,0},{2,3},{3,2},{4,5},{5,4},{6,7},{7,6},{8,9},{9,8},{10,11... | collective-permute-start | bytes 344072 | tf_op jit(solution)/shard_map/ppermute | solution.py:55
  19.1 4.7 %collective-permute-start.13 = (f16[400,128]{1,0:T(8,128)(2,1)S(1)}, f16[400,128]{1,0:T(8,128)(2,1)S(1)}, u32[]{:S(2)}, u32[]{:S(2)}) collective-permute-start(f16[400,128]{1,0:T(8,128)(2,1)S(1)} %get-tuple-element.37), channel_id=1, source_target_pairs={{0,2},{1,5},{2,0},{3,7},{4,6},{5,1},{6,4},{7,3},{8,10},{9,13},{10,... | collective-permute-start | bytes 307208 | tf_op jit(solution)/shard_map/ppermute | solution.py:33
  20.7 4.7 %collective-permute-start.14 = (f16[400,128]{1,0:T(8,128)(2,1)S(1)}, f16[400,128]{1,0:T(8,128)(2,1)S(1)}, u32[]{:S(2)}, u32[]{:S(2)}) collective-permute-start(f16[400,128]{1,0:T(8,128)(2,1)S(1)} %get-tuple-element.37), channel_id=1, source_target_pairs={{0,2},{1,9},{2,0},{3,11},{4,6},{5,13},{6,4},{7,15},{8,10},{9,1},{1... | collective-permute-start | bytes 307208 | tf_op jit(solution)/shard_map/ppermute | solution.py:33
  21.3 5.1 %collective-permute-start.11 = (f16[400,128]{1,0:T(8,128)(2,1)S(1)}, f16[400,128]{1,0:T(8,128)(2,1)S(1)}, u32[]{:S(2)}, u32[]{:S(2)}) collective-permute-start(f16[400,128]{1,0:T(8,128)(2,1)S(1)} %maximum_select_fusion), channel_id=1, source_target_pairs={{0,2},{1,13},{2,0},{3,15},{4,6},{5,9},{6,4},{7,11},{8,10},{9,5},{1... | collective-permute-start | bytes 307208 | tf_op jit(solution)/shard_map/ppermute | solution.py:33
  26.6 4.7 %collective-permute-start.15 = (f16[400,128]{1,0:T(8,128)(2,1)S(1)}, f16[400,128]{1,0:T(8,128)(2,1)S(1)}, u32[]{:S(2)}, u32[]{:S(2)}) collective-permute-start(f16[400,128]{1,0:T(8,128)(2,1)S(1)} %get-tuple-element.43), channel_id=1, source_target_pairs={{0,4},{1,3},{2,6},{3,1},{4,0},{5,7},{6,2},{7,5},{8,12},{9,11},{10,... | collective-permute-start | bytes 307208 | tf_op jit(solution)/shard_map/ppermute | solution.py:33
  27.8 2.5 %collective-permute-start.12 = (bf16[144,128]{1,0:T(8,128)(2,1)S(1)}, bf16[144,128]{1,0:T(8,128)(2,1)S(1)}, u32[]{:S(2)}, u32[]{:S(2)}) collective-permute-start(bf16[144,128]{1,0:T(8,128)(2,1)S(1)} %get-tuple-element.45), channel_id=1, source_target_pairs={{0,1},{1,0},{2,3},{3,2},{4,5},{5,4},{6,7},{7,6},{8,9},{9,8},{10,11... | collective-permute-start | bytes 110600 | tf_op jit(solution)/shard_map/ppermute | solution.py:55
  29.5 2.2 %collective-permute-start.16 = (f16[400,128]{1,0:T(8,128)(2,1)S(1)}, f16[400,128]{1,0:T(8,128)(2,1)S(1)}, u32[]{:S(2)}, u32[]{:S(2)}) collective-permute-start(f16[400,128]{1,0:T(8,128)(2,1)S(1)} %get-tuple-element.43), channel_id=1, source_target_pairs={{0,1},{1,0},{2,3},{3,2},{4,5},{5,4},{6,7},{7,6},{8,9},{9,8},{10,11... | collective-permute-start | bytes 307208 | tf_op jit(solution)/shard_map/ppermute | solution.py:55
  31.3 1.3 %collective-permute-start.17 = (f16[400,128]{1,0:T(8,128)(2,1)S(1)}, f16[400,128]{1,0:T(8,128)(2,1)S(1)}, u32[]{:S(2)}, u32[]{:S(2)}) collective-permute-start(f16[400,128]{1,0:T(8,128)(2,1)S(1)} %collective-permute-done.15), channel_id=1, source_target_pairs={{0,1},{1,0},{2,3},{3,2},{4,5},{5,4},{6,7},{7,6},{8,9},{9,8},{10,11... | collective-permute-start | bytes 307208 | tf_op jit(solution)/shard_map/ppermute | solution.py:55

commit v8 on v7

--- a/solution.py
+++ b/solution.py
@@ -181,7 +181,7 @@
     supernodes, rows_half, width = own.shape
     rows_dev = 2 * rows_half
     some = supernodes * rows_half
-    peak = jnp.zeros((1, 1), jnp.float32)
+    peaks = []
     for far_or in range(2):
         real, imag = value_of(far_or)
         for node in range(supernodes):
@@ -193,8 +193,8 @@
                 send[node * rows_half : (node + 1) * rows_half] = column[:rows_half]
                 own[node] = column[rows_half:]
             else:
-                peak = jnp.maximum(peak, largest(column.astype(jnp.float32)))
-    level = level_of(peak, 13)
+                peaks.append(jnp.abs(column.astype(jnp.float32)))
+    level = level_of(largest(functools.reduce(jnp.maximum, peaks)), 13)
     factor = power(level, 0, STEP)
     send[3 * some :] = jnp.broadcast_to(level, (LEVEL_ROWS, width)).astype(jnp.bfloat16)
     for node in range(supernodes):
@@ -203,7 +203,6 @@
         send[start : start + rows_half] = column[:rows_half]
         send[start + some : start + some + rows_half] = column[rows_half:]
     values = []
-    peak = jnp.zeros((1, 1), jnp.float32)
     for node in range(supernodes):
         both = jnp.dot(
             left[node].reshape(2 * width, 2 * rows_dev),
@@ -211,8 +210,7 @@
             preferred_element_type=jnp.float32,
         )
         values.append(both[:width] + turned(both[width:]))
-        peak = jnp.maximum(peak, largest(values[-1]))
-    level = level_of(peak, head + orders)
+    level = level_of(largest(functools.reduce(jnp.maximum, [jnp.abs(value) for value in values])), head + orders)
     factor = power(level, -orders, STEP)
     for node, value in enumerate(values):
         diag[node * width : (node + 1) * width] = value * factor
@@ -374,16 +372,16 @@
         terms = [swap(v, rows, cols, 1, mask) for mask, v in zip(MASKS_SUM, (term, term, last))]
         wide = [t.astype(f32) for t in [term] + terms]
         levels = [t[count : count + 1] for t in wide]
-        mine, first, second, third = [t[:count] * power(v, orders, -STEP) for t, v in zip(wide, levels)]
+        mine, first, second, third = [t * power(v, orders, -STEP) for t, v in zip(wide, levels)]
         total = (mine + first) + (second + third)
         level = functools.reduce(jnp.minimum, levels)
+        is_level = lax.broadcasted_iota(jnp.int32, total.shape, 0) >= count
         size = 8
         while size < rows:
-            other = swap(jnp.concatenate([total, jnp.broadcast_to(level, (8, width))]), rows, cols, 1, size)
-            total, level = total + other[:count], jnp.minimum(level, other[count : count + 1])
+            other = swap(jnp.where(is_level, level, total), rows, cols, 1, size)
+            total, level = total + other, jnp.minimum(level, other[count : count + 1])
             size *= 2
-        total = total * power(level, -orders, STEP)
-        mine = jnp.concatenate([total, jnp.broadcast_to(level, (LEVEL_ROWS, width))]).astype(f16)
+        mine = jnp.where(is_level, level, total * power(level, -orders, STEP)).astype(f16)
         far = swap(mine, rows, cols, 2, 1)
         other = wide[3][: 2 * some] * power(wide[3][2 * some : 2 * some + 1], 0, -STEP)
         other = other.astype(bf16)

time: 33.7 us -> 33.7 us (level)
  no operation moved by 1% of the time
where the time goes in v8:
time: 33.7 us; the launch traced here: 33.5 us
  starting transfers between devices  18.1 us (54%)
  waiting for transfers between devices  9.8 us (29%)
  Pallas kernels  4.46 us (13%)
  between operations  0.8 us (2%)
  other arithmetic  0.35 us (1%)
    ppermute x8, starting transfers between devices, swap(): return lax.ppermute(value, AXES, pairs)  11.9 us
    ppermute x10, starting transfers between devices, swap_core(): return lax.ppermute(value, 'pcol', [(0, 1), (1, 0)])  6.2 us
    ppermute x8, waiting for transfers between devices, swap(): return lax.ppermute(value, AXES, pairs)  5.92 us
    pallas_call x7, Pallas kernels, call(): pl.pallas_call(kernel, out_shape=shapes, in_specs=[space] * len(operands)...  4.46 us
    ppermute x10, waiting for transfers between devices, swap_core(): return lax.ppermute(value, 'pcol', [(0, 1), (1, 0)])  3.88 us
  transfers between devices with their start and end apart: 18, of which 11 were waited for; matrix products, arithmetic and copies ran while one was open for 1% of the time, Pallas kernels for 7%

profile of v8, /device:TPU:0, one launch (start us, length us, event | category | flops | bytes accessed | tf_op | source)
XLA Modules:
  0.0 33.5 jit_solution(7505734961959584848)
XLA Ops:
  0.6 3.0 %collective-permute-start.1 = (bf16[3,2,48,128]{3,2,1,0:T(8,128)(2,1)}, bf16[3,2,48,128]{3,2,1,0:T(8,128)(2,1)S(1)}, u32[]{:S(2)}, u32[]{:S(2)}) collective-permute-start(bf16[3,2,48,128]{3,2,1,0:T(8,128)(2,1)} %panels_in), channel_id=1, source_target_pairs={{0,2},{1,3},{2,0},{3,1},{4,6},{5,7},{6,4},{7,5},{8,10},{9,11},{10,... | collective-permute-start | bytes 221192 | tf_op jit(solution)/shard_map/ppermute | solution.py:33
  3.6 1.5 %shard_map.59 = (bf16[2,96,384]{2,1,0:T(8,128)(2,1)S(1)}, bf16[3,2,48,128]{3,2,1,0:T(8,128)(2,1)S(1)}, bf16[3,2,128,128]{3,2,1,0:T(8,128)(2,1)S(1)}, f32[2,96,12...) custom-call(bf16[2,8,1,48,96]{4,3,2,1,0:T(8,128)(2,1)} %matrix_in.1, ...), custom_call_target="tpu_custom_call" | custom-call | bytes 12582912 | tf_op jit(solution)/shard_map/pallas_call | solution.py:69
  5.1 0.1 collective-permute-start
  5.2 1.0 %collective-permute-done.1.panels_far = bf16[3,2,48,128]{3,2,1,0:T(8,128)(2,1)S(1)} collective-permute-done((bf16[3,2,48,128]{3,2,1,0:T(8,128)(2,1)}, bf16[3,2,48,128]{3,2,1,0:T(8,128)(2,1)S(1)}, u32[]{:S(2)}, u32[]{:S(2)}) %collective-permute-start.1) | collective-permute-done | bytes 73760 | tf_op jit(solution)/shard_map/ppermute | solution.py:33
  6.2 0.1 shard_map.60.block
  6.3 0.1 collective-permute-start.2
  6.4 1.3 %collective-permute-done.2.block_core = bf16[2,48,384]{2,1,0:T(8,128)(2,1)S(1)} collective-permute-done((bf16[2,48,384]{2,1,0:T(8,128)(2,1)S(1)}, bf16[2,48,384]{2,1,0:T(8,128)(2,1)S(1)}, u32[]{:S(2)}, u32[]{:S(2)}) %collective-permute-start.2) | collective-permute-done | bytes 73760 | tf_op jit(solution)/shard_map/ppermute | solution.py:55
  7.6 0.0 collective-permute-done.near_core
  7.7 2.1 %collective-permute-start.3 = (bf16[2,96,384]{2,1,0:T(8,128)(2,1)S(1)}, bf16[2,96,384]{2,1,0:T(8,128)(2,1)S(1)}, u32[]{:S(2)}, u32[]{:S(2)}) collective-permute-start(bf16[2,96,384]{2,1,0:T(8,128)(2,1)S(1)} %get-tuple-element.21), channel_id=1, source_target_pairs={{0,2},{1,9},{2,0},{3,11},{4,6},{5,13},{6,4},{7,15},{8,10},{9,1},{1... | collective-permute-start | bytes 442376 | tf_op jit(solution)/shard_map/ppermute | solution.py:33
  9.8 0.1 collective-permute-start.5
  9.8 1.9 %collective-permute-start.7 = (bf16[2,96,384]{2,1,0:T(8,128)(2,1)S(1)}, bf16[2,96,384]{2,1,0:T(8,128)(2,1)S(1)}, u32[]{:S(2)}, u32[]{:S(2)}) collective-permute-start(bf16[2,96,384]{2,1,0:T(8,128)(2,1)S(1)} %get-tuple-element.23.block_0), channel_id=1, source_target_pairs={{0,2},{1,13},{2,0},{3,15},{4,6},{5,9},{6,4},{7,11},{8,10},{9,5},{1... | collective-permute-start | bytes 442376 | tf_op jit(solution)/shard_map/ppermute | solution.py:33
  11.8 1.1 %collective-permute-done.3.block_1 = bf16[2,96,384]{2,1,0:T(8,128)(2,1)S(1)} collective-permute-done((bf16[2,96,384]{2,1,0:T(8,128)(2,1)S(1)}, bf16[2,96,384]{2,1,0:T(8,128)(2,1)S(1)}, u32[]{:S(2)}, u32[]{:S(2)}) %collective-permute-start.3) | collective-permute-done | bytes 147488 | tf_op jit(solution)/shard_map/ppermute | solution.py:33
  12.9 2.1 %collective-permute-start.4 = (bf16[2,96,384]{2,1,0:T(8,128)(2,1)S(1)}, bf16[2,96,384]{2,1,0:T(8,128)(2,1)S(1)}, u32[]{:S(2)}, u32[]{:S(2)}) collective-permute-start(bf16[2,96,384]{2,1,0:T(8,128)(2,1)S(1)} %collective-permute-done.3.block_1), channel_id=1, source_target_pairs={{0,1},{1,0},{2,3},{3,2},{4,5},{5,4},{6,7},{7,6},{8,9},{9,8},{10,11... | collective-permute-start | bytes 442376 | tf_op jit(solution)/shard_map/ppermute | solution.py:55
  15.0 0.0 collective-permute-done.5.block_2
  15.0 0.5 %collective-permute-start.6 = (bf16[2,96,384]{2,1,0:T(8,128)(2,1)S(1)}, bf16[2,96,384]{2,1,0:T(8,128)(2,1)S(1)}, u32[]{:S(2)}, u32[]{:S(2)}) collective-permute-start(bf16[2,96,384]{2,1,0:T(8,128)(2,1)S(1)} %collective-permute-done.5.block_2), channel_id=1, source_target_pairs={{0,1},{1,0},{2,3},{3,2},{4,5},{5,4},{6,7},{7,6},{8,9},{9,8},{10,11... | collective-permute-start | bytes 442376 | tf_op jit(solution)/shard_map/ppermute | solution.py:55
  15.4 0.0 collective-permute-start.8
  15.5 0.5 %collective-permute-start.9 = (bf16[3,2,48,128]{3,2,1,0:T(8,128)(2,1)S(1)}, bf16[3,2,48,128]{3,2,1,0:T(8,128)(2,1)S(1)}, u32[]{:S(2)}, u32[]{:S(2)}) collective-permute-start(bf16[3,2,48,128]{3,2,1,0:T(8,128)(2,1)S(1)} %collective-permute-done.1.panels_far), channel_id=1, source_target_pairs={{0,1},{1,0},{2,3},{3,2},{4,5},{5,4},{6,7},{7,6},{8,9},{9,8},{10,11... | collective-permute-start | bytes 221192 | tf_op jit(solution)/shard_map/ppermute | solution.py:55
  16.0 0.8 %collective-permute-done.8.panels_core = bf16[3,2,48,128]{3,2,1,0:T(8,128)(2,1)S(1)} collective-permute-done((bf16[3,2,48,128]{3,2,1,0:T(8,128)(2,1)S(1)}, bf16[3,2,48,128]{3,2,1,0:T(8,128)(2,1)S(1)}, u32[]{:S(2)}, u32[]{:S(2)}) %collective-permute-start.8) | collective-permute-done | bytes 73760 | tf_op jit(solution)/shard_map/ppermute | solution.py:55
  16.7 0.2 collective-permute-done.9.panels_far_core
  16.9 0.2 shard_map.62.refs_1_
  17.1 0.0 collective-permute-done.7.block_3
  17.1 0.0 collective-permute-done.4.far_0
  17.1 0.0 collective-permute-done.6.far_1
  17.1 1.1 %shard_map.63 = (bf16[3,48,128]{2,1,0:T(8,128)(2,1)S(1)}, bf16[448,128]{1,0:T(8,128)(2,1)S(1)}, f32[400,128]{1,0:T(8,128)S(1)}) custom-call(bf16[2,96,384]{2,1,0:T(8,128)(2,1)S(1)} %get-tuple-element.18.near, bf16[2,96,384]{2,1,0:T(8,128)(2,1)S(1)} %collective-permute-done.near_core, bf16[2,96,384]{2,1,0:T(8,128)(2,1)S(1)} %collective-permute-done.4.far_0, ...), custom_call_target="tpu_custom_call" | custom-call | bytes 1929216 | tf_op jit(solution)/shard_map/pallas_call | solution.py:69
  18.1 0.9 %collective-permute-start.10 = (bf16[448,128]{1,0:T(8,128)(2,1)S(1)}, bf16[448,128]{1,0:T(8,128)(2,1)S(1)}, u32[]{:S(2)}, u32[]{:S(2)}) collective-permute-start(bf16[448,128]{1,0:T(8,128)(2,1)S(1)} %get-tuple-element.30), channel_id=1, source_target_pairs={{0,1},{1,0},{2,3},{3,2},{4,5},{5,4},{6,7},{7,6},{8,9},{9,8},{10,11... | collective-permute-start | bytes 344072 | tf_op jit(solution)/shard_map/ppermute | solution.py:55
  19.1 1.6 %collective-permute-start.13 = (f16[400,128]{1,0:T(8,128)(2,1)S(1)}, f16[400,128]{1,0:T(8,128)(2,1)S(1)}, u32[]{:S(2)}, u32[]{:S(2)}) collective-permute-start(f16[400,128]{1,0:T(8,128)(2,1)S(1)} %get-tuple-element.39), channel_id=1, source_target_pairs={{0,2},{1,5},{2,0},{3,7},{4,6},{5,1},{6,4},{7,3},{8,10},{9,13},{10,... | collective-permute-start | bytes 307208 | tf_op jit(solution)/shard_map/ppermute | solution.py:33
  20.7 0.5 %collective-permute-start.14 = (f16[400,128]{1,0:T(8,128)(2,1)S(1)}, f16[400,128]{1,0:T(8,128)(2,1)S(1)}, u32[]{:S(2)}, u32[]{:S(2)}) collective-permute-start(f16[400,128]{1,0:T(8,128)(2,1)S(1)} %get-tuple-element.39), channel_id=1, source_target_pairs={{0,2},{1,9},{2,0},{3,11},{4,6},{5,13},{6,4},{7,15},{8,10},{9,1},{1... | collective-permute-start | bytes 307208 | tf_op jit(solution)/shard_map/ppermute | solution.py:33
  21.2 0.0 collective-permute-done.10
  21.3 1.6 %collective-permute-start.11 = (f16[400,128]{1,0:T(8,128)(2,1)S(1)}, f16[400,128]{1,0:T(8,128)(2,1)S(1)}, u32[]{:S(2)}, u32[]{:S(2)}) collective-permute-start(f16[400,128]{1,0:T(8,128)(2,1)S(1)} %maximum_select_fusion), channel_id=1, source_target_pairs={{0,2},{1,13},{2,0},{3,15},{4,6},{5,9},{6,4},{7,11},{8,10},{9,5},{1... | collective-permute-start | bytes 307208 | tf_op jit(solution)/shard_map/ppermute | solution.py:33
  22.8 1.0 %collective-permute-done.13 = f16[400,128]{1,0:T(8,128)(2,1)S(1)} collective-permute-done((f16[400,128]{1,0:T(8,128)(2,1)S(1)}, f16[400,128]{1,0:T(8,128)(2,1)S(1)}, u32[]{:S(2)}, u32[]{:S(2)}) %collective-permute-start.13) | collective-permute-done | bytes 102432 | tf_op jit(solution)/shard_map/ppermute | solution.py:33
  23.9 1.5 %collective-permute-done.14 = f16[400,128]{1,0:T(8,128)(2,1)S(1)} collective-permute-done((f16[400,128]{1,0:T(8,128)(2,1)S(1)}, f16[400,128]{1,0:T(8,128)(2,1)S(1)}, u32[]{:S(2)}, u32[]{:S(2)}) %collective-permute-start.14) | collective-permute-done | bytes 102432 | tf_op jit(solution)/shard_map/ppermute | solution.py:33
  25.3 1.1 %collective-permute-done.11 = f16[400,128]{1,0:T(8,128)(2,1)S(1)} collective-permute-done((f16[400,128]{1,0:T(8,128)(2,1)S(1)}, f16[400,128]{1,0:T(8,128)(2,1)S(1)}, u32[]{:S(2)}, u32[]{:S(2)}) %collective-permute-start.11) | collective-permute-done | bytes 102432 | tf_op jit(solution)/shard_map/ppermute | solution.py:33
  26.5 0.1 fusion.7
  26.6 1.2 %collective-permute-start.15 = (f16[400,128]{1,0:T(8,128)(2,1)S(1)}, f16[400,128]{1,0:T(8,128)(2,1)S(1)}, u32[]{:S(2)}, u32[]{:S(2)}) collective-permute-start(f16[400,128]{1,0:T(8,128)(2,1)S(1)} %get-tuple-element.35), channel_id=1, source_target_pairs={{0,4},{1,3},{2,6},{3,1},{4,0},{5,7},{6,2},{7,5},{8,12},{9,11},{10,... | collective-permute-start | bytes 307208 | tf_op jit(solution)/shard_map/ppermute | solution.py:33
  27.8 1.7 %collective-permute-start.12 = (bf16[144,128]{1,0:T(8,128)(2,1)S(1)}, bf16[144,128]{1,0:T(8,128)(2,1)S(1)}, u32[]{:S(2)}, u32[]{:S(2)}) collective-permute-start(bf16[144,128]{1,0:T(8,128)(2,1)S(1)} %get-tuple-element.45), channel_id=1, source_target_pairs={{0,1},{1,0},{2,3},{3,2},{4,5},{5,4},{6,7},{7,6},{8,9},{9,8},{10,11... | collective-permute-start | bytes 110600 | tf_op jit(solution)/shard_map/ppermute | solution.py:55
  29.5 0.1 collective-permute-start.16
  29.5 0.8 %collective-permute-done.12.other_core = bf16[144,128]{1,0:T(8,128)(2,1)S(1)} collective-permute-done((bf16[144,128]{1,0:T(8,128)(2,1)S(1)}, bf16[144,128]{1,0:T(8,128)(2,1)S(1)}, u32[]{:S(2)}, u32[]{:S(2)}) %collective-permute-start.12) | collective-permute-done | bytes 36896 | tf_op jit(solution)/shard_map/ppermute | solution.py:55
  30.3 0.7 %shard_map.64 = bf16[3,2,48,128]{3,2,1,0:T(8,128)(2,1)} custom-call(bf16[144,128]{1,0:T(8,128)(2,1)S(1)} %bitcast.14, bf16[144,128]{1,0:T(8,128)(2,1)S(1)} %slice.44.own_core, bf16[144,128]{1,0:T(8,128)(2,1)S(1)} %get-tuple-element.46.other, bf16[144,128]{1,0:T(8,128)(2,1)S(1)} %collective-permute-done.12.other_core), custom_call_target="tpu_custom_call" | custom-call | bytes 221184 | tf_op jit(solution)/shard_map/pallas_call | solution.py:69
  31.1 0.3 collective-permute-done.15
  31.3 0.3 collective-permute-start.17
  31.7 0.0 collective-permute-done.16
  31.7 0.9 %collective-permute-done.17 = f16[400,128]{1,0:T(8,128)(2,1)S(1)} collective-permute-done((f16[400,128]{1,0:T(8,128)(2,1)S(1)}, f16[400,128]{1,0:T(8,128)(2,1)S(1)}, u32[]{:S(2)}, u32[]{:S(2)}) %collective-permute-start.17) | collective-permute-done | bytes 102432 | tf_op jit(solution)/shard_map/ppermute | solution.py:55
  32.7 0.9 %shard_map.65 = f32[3,2,128,128]{3,2,1,0:T(8,128)} custom-call(bf16[3,2,128,128]{3,2,1,0:T(8,128)(2,1)S(1)} %get-tuple-element.32.diag_inverse, f32[400,128]{1,0:T(8,128)S(1)} %get-tuple-element.34.mine, f32[400,128]{1,0:T(8,128)S(1)} %convert_element_type.45.far, f32[400,128]{1,0:T(8,128)S(1)} %convert_element_type.46.mine_core, ...), custom_call_target="tpu_custom_call" | custom-call | bytes 1409024 | tf_op jit(solution)/shard_map/pallas_call | solution.py:69
  (16 shorter events, 0.3 us)
Async XLA Ops:
  0.6 5.5 %collective-permute-start.1 = (bf16[3,2,48,128]{3,2,1,0:T(8,128)(2,1)}, bf16[3,2,48,128]{3,2,1,0:T(8,128)(2,1)S(1)}, u32[]{:S(2)}, u32[]{:S(2)}) collective-permute-start(bf16[3,2,48,128]{3,2,1,0:T(8,128)(2,1)} %panels_in), channel_id=1, source_target_pairs={{0,2},{1,3},{2,0},{3,1},{4,6},{5,7},{6,4},{7,5},{8,10},{9,11},{10,... | collective-permute-start | bytes 221192 | tf_op jit(solution)/shard_map/ppermute | solution.py:33
  5.1 2.5 %collective-permute-start = (bf16[2,96,384]{2,1,0:T(8,128)(2,1)S(1)}, bf16[2,96,384]{2,1,0:T(8,128)(2,1)S(1)}, u32[]{:S(2)}, u32[]{:S(2)}) collective-permute-start(bf16[2,96,384]{2,1,0:T(8,128)(2,1)S(1)} %get-tuple-element.18.near), channel_id=1, source_target_pairs={{0,1},{1,0},{2,3},{3,2},{4,5},{5,4},{6,7},{7,6},{8,9},{9,8},{10,11... | collective-permute-start | bytes 442376 | tf_op jit(solution)/shard_map/ppermute | solution.py:55
  6.3 1.3 %collective-permute-start.2 = (bf16[2,48,384]{2,1,0:T(8,128)(2,1)S(1)}, bf16[2,48,384]{2,1,0:T(8,128)(2,1)S(1)}, u32[]{:S(2)}, u32[]{:S(2)}) collective-permute-start(bf16[2,48,384]{2,1,0:T(8,128)(2,1)S(1)} %shard_map.60.block), channel_id=1, source_target_pairs={{0,1},{1,0},{2,3},{3,2},{4,5},{5,4},{6,7},{7,6},{8,9},{9,8},{10,11... | collective-permute-start | bytes 221192 | tf_op jit(solution)/shard_map/ppermute | solution.py:55
  7.7 5.2 %collective-permute-start.3 = (bf16[2,96,384]{2,1,0:T(8,128)(2,1)S(1)}, bf16[2,96,384]{2,1,0:T(8,128)(2,1)S(1)}, u32[]{:S(2)}, u32[]{:S(2)}) collective-permute-start(bf16[2,96,384]{2,1,0:T(8,128)(2,1)S(1)} %get-tuple-element.21), channel_id=1, source_target_pairs={{0,2},{1,9},{2,0},{3,11},{4,6},{5,13},{6,4},{7,15},{8,10},{9,1},{1... | collective-permute-start | bytes 442376 | tf_op jit(solution)/shard_map/ppermute | solution.py:33
  9.8 5.2 %collective-permute-start.5 = (bf16[2,96,384]{2,1,0:T(8,128)(2,1)S(1)}, bf16[2,96,384]{2,1,0:T(8,128)(2,1)S(1)}, u32[]{:S(2)}, u32[]{:S(2)}) collective-permute-start(bf16[2,96,384]{2,1,0:T(8,128)(2,1)S(1)} %get-tuple-element.22), channel_id=1, source_target_pairs={{0,2},{1,5},{2,0},{3,7},{4,6},{5,1},{6,4},{7,3},{8,10},{9,13},{10,... | collective-permute-start | bytes 442376 | tf_op jit(solution)/shard_map/ppermute | solution.py:33
  9.8 7.2 %collective-permute-start.7 = (bf16[2,96,384]{2,1,0:T(8,128)(2,1)S(1)}, bf16[2,96,384]{2,1,0:T(8,128)(2,1)S(1)}, u32[]{:S(2)}, u32[]{:S(2)}) collective-permute-start(bf16[2,96,384]{2,1,0:T(8,128)(2,1)S(1)} %get-tuple-element.23.block_0), channel_id=1, source_target_pairs={{0,2},{1,13},{2,0},{3,15},{4,6},{5,9},{6,4},{7,11},{8,10},{9,5},{1... | collective-permute-start | bytes 442376 | tf_op jit(solution)/shard_map/ppermute | solution.py:33
  12.9 4.2 %collective-permute-start.4 = (bf16[2,96,384]{2,1,0:T(8,128)(2,1)S(1)}, bf16[2,96,384]{2,1,0:T(8,128)(2,1)S(1)}, u32[]{:S(2)}, u32[]{:S(2)}) collective-permute-start(bf16[2,96,384]{2,1,0:T(8,128)(2,1)S(1)} %collective-permute-done.3.block_1), channel_id=1, source_target_pairs={{0,1},{1,0},{2,3},{3,2},{4,5},{5,4},{6,7},{7,6},{8,9},{9,8},{10,11... | collective-permute-start | bytes 442376 | tf_op jit(solution)/shard_map/ppermute | solution.py:55
  15.0 2.1 %collective-permute-start.6 = (bf16[2,96,384]{2,1,0:T(8,128)(2,1)S(1)}, bf16[2,96,384]{2,1,0:T(8,128)(2,1)S(1)}, u32[]{:S(2)}, u32[]{:S(2)}) collective-permute-start(bf16[2,96,384]{2,1,0:T(8,128)(2,1)S(1)} %collective-permute-done.5.block_2), channel_id=1, source_target_pairs={{0,1},{1,0},{2,3},{3,2},{4,5},{5,4},{6,7},{7,6},{8,9},{9,8},{10,11... | collective-permute-start | bytes 442376 | tf_op jit(solution)/shard_map/ppermute | solution.py:55
  15.4 1.3 %collective-permute-start.8 = (bf16[3,2,48,128]{3,2,1,0:T(8,128)(2,1)S(1)}, bf16[3,2,48,128]{3,2,1,0:T(8,128)(2,1)S(1)}, u32[]{:S(2)}, u32[]{:S(2)}) collective-permute-start(bf16[3,2,48,128]{3,2,1,0:T(8,128)(2,1)S(1)} %get-tuple-element.28.panels), channel_id=1, source_target_pairs={{0,1},{1,0},{2,3},{3,2},{4,5},{5,4},{6,7},{7,6},{8,9},{9,8},{10,11... | collective-permute-start | bytes 221192 | tf_op jit(solution)/shard_map/ppermute | solution.py:55
  15.5 1.4 %collective-permute-start.9 = (bf16[3,2,48,128]{3,2,1,0:T(8,128)(2,1)S(1)}, bf16[3,2,48,128]{3,2,1,0:T(8,128)(2,1)S(1)}, u32[]{:S(2)}, u32[]{:S(2)}) collective-permute-start(bf16[3,2,48,128]{3,2,1,0:T(8,128)(2,1)S(1)} %collective-permute-done.1.panels_far), channel_id=1, source_target_pairs={{0,1},{1,0},{2,3},{3,2},{4,5},{5,4},{6,7},{7,6},{8,9},{9,8},{10,11... | collective-permute-start | bytes 221192 | tf_op jit(solution)/shard_map/ppermute | solution.py:55
  18.1 3.1 %collective-permute-start.10 = (bf16[448,128]{1,0:T(8,128)(2,1)S(1)}, bf16[448,128]{1,0:T(8,128)(2,1)S(1)}, u32[]{:S(2)}, u32[]{:S(2)}) collective-permute-start(bf16[448,128]{1,0:T(8,128)(2,1)S(1)} %get-tuple-element.30), channel_id=1, source_target_pairs={{0,1},{1,0},{2,3},{3,2},{4,5},{5,4},{6,7},{7,6},{8,9},{9,8},{10,11... | collective-permute-start | bytes 344072 | tf_op jit(solution)/shard_map/ppermute | solution.py:55
  19.1 4.7 %collective-permute-start.13 = (f16[400,128]{1,0:T(8,128)(2,1)S(1)}, f16[400,128]{1,0:T(8,128)(2,1)S(1)}, u32[]{:S(2)}, u32[]{:S(2)}) collective-permute-start(f16[400,128]{1,0:T(8,128)(2,1)S(1)} %get-tuple-element.39), channel_id=1, source_target_pairs={{0,2},{1,5},{2,0},{3,7},{4,6},{5,1},{6,4},{7,3},{8,10},{9,13},{10,... | collective-permute-start | bytes 307208 | tf_op jit(solution)/shard_map/ppermute | solution.py:33
  20.7 4.7 %collective-permute-start.14 = (f16[400,128]{1,0:T(8,128)(2,1)S(1)}, f16[400,128]{1,0:T(8,128)(2,1)S(1)}, u32[]{:S(2)}, u32[]{:S(2)}) collective-permute-start(f16[400,128]{1,0:T(8,128)(2,1)S(1)} %get-tuple-element.39), channel_id=1, source_target_pairs={{0,2},{1,9},{2,0},{3,11},{4,6},{5,13},{6,4},{7,15},{8,10},{9,1},{1... | collective-permute-start | bytes 307208 | tf_op jit(solution)/shard_map/ppermute | solution.py:33
  21.3 5.1 %collective-permute-start.11 = (f16[400,128]{1,0:T(8,128)(2,1)S(1)}, f16[400,128]{1,0:T(8,128)(2,1)S(1)}, u32[]{:S(2)}, u32[]{:S(2)}) collective-permute-start(f16[400,128]{1,0:T(8,128)(2,1)S(1)} %maximum_select_fusion), channel_id=1, source_target_pairs={{0,2},{1,13},{2,0},{3,15},{4,6},{5,9},{6,4},{7,11},{8,10},{9,5},{1... | collective-permute-start | bytes 307208 | tf_op jit(solution)/shard_map/ppermute | solution.py:33
  26.6 4.7 %collective-permute-start.15 = (f16[400,128]{1,0:T(8,128)(2,1)S(1)}, f16[400,128]{1,0:T(8,128)(2,1)S(1)}, u32[]{:S(2)}, u32[]{:S(2)}) collective-permute-start(f16[400,128]{1,0:T(8,128)(2,1)S(1)} %get-tuple-element.35), channel_id=1, source_target_pairs={{0,4},{1,3},{2,6},{3,1},{4,0},{5,7},{6,2},{7,5},{8,12},{9,11},{10,... | collective-permute-start | bytes 307208 | tf_op jit(solution)/shard_map/ppermute | solution.py:33
  27.8 2.5 %collective-permute-start.12 = (bf16[144,128]{1,0:T(8,128)(2,1)S(1)}, bf16[144,128]{1,0:T(8,128)(2,1)S(1)}, u32[]{:S(2)}, u32[]{:S(2)}) collective-permute-start(bf16[144,128]{1,0:T(8,128)(2,1)S(1)} %get-tuple-element.45), channel_id=1, source_target_pairs={{0,1},{1,0},{2,3},{3,2},{4,5},{5,4},{6,7},{7,6},{8,9},{9,8},{10,11... | collective-permute-start | bytes 110600 | tf_op jit(solution)/shard_map/ppermute | solution.py:55
  29.5 2.2 %collective-permute-start.16 = (f16[400,128]{1,0:T(8,128)(2,1)S(1)}, f16[400,128]{1,0:T(8,128)(2,1)S(1)}, u32[]{:S(2)}, u32[]{:S(2)}) collective-permute-start(f16[400,128]{1,0:T(8,128)(2,1)S(1)} %get-tuple-element.35), channel_id=1, source_target_pairs={{0,1},{1,0},{2,3},{3,2},{4,5},{5,4},{6,7},{7,6},{8,9},{9,8},{10,11... | collective-permute-start | bytes 307208 | tf_op jit(solution)/shard_map/ppermute | solution.py:55
  31.3 1.3 %collective-permute-start.17 = (f16[400,128]{1,0:T(8,128)(2,1)S(1)}, f16[400,128]{1,0:T(8,128)(2,1)S(1)}, u32[]{:S(2)}, u32[]{:S(2)}) collective-permute-start(f16[400,128]{1,0:T(8,128)(2,1)S(1)} %collective-permute-done.15), channel_id=1, source_target_pairs={{0,1},{1,0},{2,3},{3,2},{4,5},{5,4},{6,7},{7,6},{8,9},{9,8},{10,11... | collective-permute-start | bytes 307208 | tf_op jit(solution)/shard_map/ppermute | solution.py:55

commit v9 on v8

--- a/solution.py
+++ b/solution.py
@@ -210,10 +210,9 @@
             preferred_element_type=jnp.float32,
         )
         values.append(both[:width] + turned(both[width:]))
+    for node, value in enumerate(values):
+        diag[node * width : (node + 1) * width] = value
     level = level_of(largest(functools.reduce(jnp.maximum, [jnp.abs(value) for value in values])), head + orders)
-    factor = power(level, -orders, STEP)
-    for node, value in enumerate(values):
-        diag[node * width : (node + 1) * width] = value * factor
     diag[supernodes * width :] = jnp.broadcast_to(level, (LEVEL_ROWS, width))
 
 
@@ -365,7 +364,9 @@
                 functools.partial(diagonal_kernel, orders, head), outs, [product, keep, left], [columns_scratch]
             )
         f16 = jnp.float16
-        term = diag.astype(f16)
+        is_level = lax.broadcasted_iota(jnp.int32, diag.shape, 0) >= count
+        level = diag[count : count + 1]
+        term = jnp.where(is_level, level, diag * power(level, -orders, STEP)).astype(f16)
         sent = swap_core(send)
         last = jnp.concatenate([sent[some:].astype(f16), term[2 * some + LEVEL_ROWS :]])
         last = jnp.where(col_index == 0, last, term)
@@ -375,7 +376,6 @@
         mine, first, second, third = [t * power(v, orders, -STEP) for t, v in zip(wide, levels)]
         total = (mine + first) + (second + third)
         level = functools.reduce(jnp.minimum, levels)
-        is_level = lax.broadcasted_iota(jnp.int32, total.shape, 0) >= count
         size = 8
         while size < rows:
             other = swap(jnp.where(is_level, level, total), rows, cols, 1, size)

time: 33.7 us -> 33.8 us (level)
  no operation moved by 1% of the time
where the time goes in v9:
time: 33.8 us; the launch traced here: 33.6 us
  starting transfers between devices  18.1 us (54%)
  waiting for transfers between devices  9.8 us (29%)
  Pallas kernels  4.45 us (13%)
  between operations  0.8 us (2%)
  other arithmetic  0.45 us (1%)
    ppermute x8, starting transfers between devices, swap(): return lax.ppermute(value, AXES, pairs)  11.9 us
    ppermute x10, starting transfers between devices, swap_core(): return lax.ppermute(value, 'pcol', [(0, 1), (1, 0)])  6.19 us
    ppermute x8, waiting for transfers between devices, swap(): return lax.ppermute(value, AXES, pairs)  5.93 us
    pallas_call x7, Pallas kernels, call(): pl.pallas_call(kernel, out_shape=shapes, in_specs=[space] * len(operands)...  4.45 us
    ppermute x10, waiting for transfers between devices, swap_core(): return lax.ppermute(value, 'pcol', [(0, 1), (1, 0)])  3.88 us
  transfers between devices with their start and end apart: 18, of which 11 were waited for; matrix products, arithmetic and copies ran while one was open for 1% of the time, Pallas kernels for 7%

profile of v9, /device:TPU:0, one launch (start us, length us, event | category | flops | bytes accessed | tf_op | source)
XLA Modules:
  0.0 33.6 jit_solution(3614305112116655265)
XLA Ops:
  0.6 3.0 %collective-permute-start.1 = (bf16[3,2,48,128]{3,2,1,0:T(8,128)(2,1)}, bf16[3,2,48,128]{3,2,1,0:T(8,128)(2,1)S(1)}, u32[]{:S(2)}, u32[]{:S(2)}) collective-permute-start(bf16[3,2,48,128]{3,2,1,0:T(8,128)(2,1)} %panels_in), channel_id=1, source_target_pairs={{0,2},{1,3},{2,0},{3,1},{4,6},{5,7},{6,4},{7,5},{8,10},{9,11},{10,... | collective-permute-start | bytes 221192 | tf_op jit(solution)/shard_map/ppermute | solution.py:33
  3.6 1.5 %shard_map.59 = (bf16[2,96,384]{2,1,0:T(8,128)(2,1)S(1)}, bf16[3,2,48,128]{3,2,1,0:T(8,128)(2,1)S(1)}, bf16[3,2,128,128]{3,2,1,0:T(8,128)(2,1)S(1)}, f32[2,96,12...) custom-call(bf16[2,8,1,48,96]{4,3,2,1,0:T(8,128)(2,1)} %matrix_in.1, ...), custom_call_target="tpu_custom_call" | custom-call | bytes 12582912 | tf_op jit(solution)/shard_map/pallas_call | solution.py:69
  5.1 0.1 collective-permute-start
  5.2 1.0 %collective-permute-done.1.panels_far = bf16[3,2,48,128]{3,2,1,0:T(8,128)(2,1)S(1)} collective-permute-done((bf16[3,2,48,128]{3,2,1,0:T(8,128)(2,1)}, bf16[3,2,48,128]{3,2,1,0:T(8,128)(2,1)S(1)}, u32[]{:S(2)}, u32[]{:S(2)}) %collective-permute-start.1) | collective-permute-done | bytes 73760 | tf_op jit(solution)/shard_map/ppermute | solution.py:33
  6.2 0.1 shard_map.60.block
  6.3 0.1 collective-permute-start.2
  6.4 1.3 %collective-permute-done.2.block_core = bf16[2,48,384]{2,1,0:T(8,128)(2,1)S(1)} collective-permute-done((bf16[2,48,384]{2,1,0:T(8,128)(2,1)S(1)}, bf16[2,48,384]{2,1,0:T(8,128)(2,1)S(1)}, u32[]{:S(2)}, u32[]{:S(2)}) %collective-permute-start.2) | collective-permute-done | bytes 73760 | tf_op jit(solution)/shard_map/ppermute | solution.py:55
  7.6 0.0 collective-permute-done.near_core
  7.7 2.1 %collective-permute-start.3 = (bf16[2,96,384]{2,1,0:T(8,128)(2,1)S(1)}, bf16[2,96,384]{2,1,0:T(8,128)(2,1)S(1)}, u32[]{:S(2)}, u32[]{:S(2)}) collective-permute-start(bf16[2,96,384]{2,1,0:T(8,128)(2,1)S(1)} %get-tuple-element.21), channel_id=1, source_target_pairs={{0,2},{1,9},{2,0},{3,11},{4,6},{5,13},{6,4},{7,15},{8,10},{9,1},{1... | collective-permute-start | bytes 442376 | tf_op jit(solution)/shard_map/ppermute | solution.py:33
  9.8 0.1 collective-permute-start.5
  9.8 1.9 %collective-permute-start.7 = (bf16[2,96,384]{2,1,0:T(8,128)(2,1)S(1)}, bf16[2,96,384]{2,1,0:T(8,128)(2,1)S(1)}, u32[]{:S(2)}, u32[]{:S(2)}) collective-permute-start(bf16[2,96,384]{2,1,0:T(8,128)(2,1)S(1)} %get-tuple-element.23.block_0), channel_id=1, source_target_pairs={{0,2},{1,13},{2,0},{3,15},{4,6},{5,9},{6,4},{7,11},{8,10},{9,5},{1... | collective-permute-start | bytes 442376 | tf_op jit(solution)/shard_map/ppermute | solution.py:33
  11.8 1.1 %collective-permute-done.3.block_1 = bf16[2,96,384]{2,1,0:T(8,128)(2,1)S(1)} collective-permute-done((bf16[2,96,384]{2,1,0:T(8,128)(2,1)S(1)}, bf16[2,96,384]{2,1,0:T(8,128)(2,1)S(1)}, u32[]{:S(2)}, u32[]{:S(2)}) %collective-permute-start.3) | collective-permute-done | bytes 147488 | tf_op jit(solution)/shard_map/ppermute | solution.py:33
  12.9 2.1 %collective-permute-start.4 = (bf16[2,96,384]{2,1,0:T(8,128)(2,1)S(1)}, bf16[2,96,384]{2,1,0:T(8,128)(2,1)S(1)}, u32[]{:S(2)}, u32[]{:S(2)}) collective-permute-start(bf16[2,96,384]{2,1,0:T(8,128)(2,1)S(1)} %collective-permute-done.3.block_1), channel_id=1, source_target_pairs={{0,1},{1,0},{2,3},{3,2},{4,5},{5,4},{6,7},{7,6},{8,9},{9,8},{10,11... | collective-permute-start | bytes 442376 | tf_op jit(solution)/shard_map/ppermute | solution.py:55
  15.0 0.0 collective-permute-done.5.block_2
  15.0 0.5 %collective-permute-start.6 = (bf16[2,96,384]{2,1,0:T(8,128)(2,1)S(1)}, bf16[2,96,384]{2,1,0:T(8,128)(2,1)S(1)}, u32[]{:S(2)}, u32[]{:S(2)}) collective-permute-start(bf16[2,96,384]{2,1,0:T(8,128)(2,1)S(1)} %collective-permute-done.5.block_2), channel_id=1, source_target_pairs={{0,1},{1,0},{2,3},{3,2},{4,5},{5,4},{6,7},{7,6},{8,9},{9,8},{10,11... | collective-permute-start | bytes 442376 | tf_op jit(solution)/shard_map/ppermute | solution.py:55
  15.4 0.0 collective-permute-start.8
  15.5 0.5 %collective-permute-start.9 = (bf16[3,2,48,128]{3,2,1,0:T(8,128)(2,1)S(1)}, bf16[3,2,48,128]{3,2,1,0:T(8,128)(2,1)S(1)}, u32[]{:S(2)}, u32[]{:S(2)}) collective-permute-start(bf16[3,2,48,128]{3,2,1,0:T(8,128)(2,1)S(1)} %collective-permute-done.1.panels_far), channel_id=1, source_target_pairs={{0,1},{1,0},{2,3},{3,2},{4,5},{5,4},{6,7},{7,6},{8,9},{9,8},{10,11... | collective-permute-start | bytes 221192 | tf_op jit(solution)/shard_map/ppermute | solution.py:55
  16.0 0.7 %collective-permute-done.8.panels_core = bf16[3,2,48,128]{3,2,1,0:T(8,128)(2,1)S(1)} collective-permute-done((bf16[3,2,48,128]{3,2,1,0:T(8,128)(2,1)S(1)}, bf16[3,2,48,128]{3,2,1,0:T(8,128)(2,1)S(1)}, u32[]{:S(2)}, u32[]{:S(2)}) %collective-permute-start.8) | collective-permute-done | bytes 73760 | tf_op jit(solution)/shard_map/ppermute | solution.py:55
  16.7 0.2 collective-permute-done.9.panels_far_core
  16.9 0.2 shard_map.62.refs_1_
  17.1 0.0 collective-permute-done.7.block_3
  17.1 0.0 collective-permute-done.4.far_0
  17.1 0.0 collective-permute-done.6.far_1
  17.1 1.0 %shard_map.63 = (bf16[3,48,128]{2,1,0:T(8,128)(2,1)S(1)}, bf16[448,128]{1,0:T(8,128)(2,1)S(1)}, f32[400,128]{1,0:T(8,128)S(1)}) custom-call(bf16[2,96,384]{2,1,0:T(8,128)(2,1)S(1)} %get-tuple-element.18.near, bf16[2,96,384]{2,1,0:T(8,128)(2,1)S(1)} %collective-permute-done.near_core, bf16[2,96,384]{2,1,0:T(8,128)(2,1)S(1)} %collective-permute-done.4.far_0, ...), custom_call_target="tpu_custom_call" | custom-call | bytes 1929216 | tf_op jit(solution)/shard_map/pallas_call | solution.py:69
  18.1 0.9 %collective-permute-start.10 = (bf16[448,128]{1,0:T(8,128)(2,1)S(1)}, bf16[448,128]{1,0:T(8,128)(2,1)S(1)}, u32[]{:S(2)}, u32[]{:S(2)}) collective-permute-start(bf16[448,128]{1,0:T(8,128)(2,1)S(1)} %get-tuple-element.30), channel_id=1, source_target_pairs={{0,1},{1,0},{2,3},{3,2},{4,5},{5,4},{6,7},{7,6},{8,9},{9,8},{10,11... | collective-permute-start | bytes 344072 | tf_op jit(solution)/shard_map/ppermute | solution.py:55
  19.1 0.1 fusion.9
  19.2 1.6 %collective-permute-start.13 = (f16[400,128]{1,0:T(8,128)(2,1)S(1)}, f16[400,128]{1,0:T(8,128)(2,1)S(1)}, u32[]{:S(2)}, u32[]{:S(2)}) collective-permute-start(f16[400,128]{1,0:T(8,128)(2,1)S(1)} %get-tuple-element.39), channel_id=1, source_target_pairs={{0,2},{1,5},{2,0},{3,7},{4,6},{5,1},{6,4},{7,3},{8,10},{9,13},{10,... | collective-permute-start | bytes 307208 | tf_op jit(solution)/shard_map/ppermute | solution.py:33
  20.8 0.5 %collective-permute-start.14 = (f16[400,128]{1,0:T(8,128)(2,1)S(1)}, f16[400,128]{1,0:T(8,128)(2,1)S(1)}, u32[]{:S(2)}, u32[]{:S(2)}) collective-permute-start(f16[400,128]{1,0:T(8,128)(2,1)S(1)} %get-tuple-element.39), channel_id=1, source_target_pairs={{0,2},{1,9},{2,0},{3,11},{4,6},{5,13},{6,4},{7,15},{8,10},{9,1},{1... | collective-permute-start | bytes 307208 | tf_op jit(solution)/shard_map/ppermute | solution.py:33
  21.3 0.0 collective-permute-done.10
  21.4 1.6 %collective-permute-start.11 = (f16[400,128]{1,0:T(8,128)(2,1)S(1)}, f16[400,128]{1,0:T(8,128)(2,1)S(1)}, u32[]{:S(2)}, u32[]{:S(2)}) collective-permute-start(f16[400,128]{1,0:T(8,128)(2,1)S(1)} %maximum_select_fusion), channel_id=1, source_target_pairs={{0,2},{1,13},{2,0},{3,15},{4,6},{5,9},{6,4},{7,11},{8,10},{9,5},{1... | collective-permute-start | bytes 307208 | tf_op jit(solution)/shard_map/ppermute | solution.py:33
  22.9 1.0 %collective-permute-done.13 = f16[400,128]{1,0:T(8,128)(2,1)S(1)} collective-permute-done((f16[400,128]{1,0:T(8,128)(2,1)S(1)}, f16[400,128]{1,0:T(8,128)(2,1)S(1)}, u32[]{:S(2)}, u32[]{:S(2)}) %collective-permute-start.13) | collective-permute-done | bytes 102432 | tf_op jit(solution)/shard_map/ppermute | solution.py:33
  23.9 1.5 %collective-permute-done.14 = f16[400,128]{1,0:T(8,128)(2,1)S(1)} collective-permute-done((f16[400,128]{1,0:T(8,128)(2,1)S(1)}, f16[400,128]{1,0:T(8,128)(2,1)S(1)}, u32[]{:S(2)}, u32[]{:S(2)}) %collective-permute-start.14) | collective-permute-done | bytes 102432 | tf_op jit(solution)/shard_map/ppermute | solution.py:33
  25.4 1.1 %collective-permute-done.11 = f16[400,128]{1,0:T(8,128)(2,1)S(1)} collective-permute-done((f16[400,128]{1,0:T(8,128)(2,1)S(1)}, f16[400,128]{1,0:T(8,128)(2,1)S(1)}, u32[]{:S(2)}, u32[]{:S(2)}) %collective-permute-start.11) | collective-permute-done | bytes 102432 | tf_op jit(solution)/shard_map/ppermute | solution.py:33
  26.6 0.1 fusion.8
  26.7 1.2 %collective-permute-start.15 = (f16[400,128]{1,0:T(8,128)(2,1)S(1)}, f16[400,128]{1,0:T(8,128)(2,1)S(1)}, u32[]{:S(2)}, u32[]{:S(2)}) collective-permute-start(f16[400,128]{1,0:T(8,128)(2,1)S(1)} %get-tuple-element.35), channel_id=1, source_target_pairs={{0,4},{1,3},{2,6},{3,1},{4,0},{5,7},{6,2},{7,5},{8,12},{9,11},{10,... | collective-permute-start | bytes 307208 | tf_op jit(solution)/shard_map/ppermute | solution.py:33
  27.9 1.7 %collective-permute-start.12 = (bf16[144,128]{1,0:T(8,128)(2,1)S(1)}, bf16[144,128]{1,0:T(8,128)(2,1)S(1)}, u32[]{:S(2)}, u32[]{:S(2)}) collective-permute-start(bf16[144,128]{1,0:T(8,128)(2,1)S(1)} %get-tuple-element.47), channel_id=1, source_target_pairs={{0,1},{1,0},{2,3},{3,2},{4,5},{5,4},{6,7},{7,6},{8,9},{9,8},{10,11... | collective-permute-start | bytes 110600 | tf_op jit(solution)/shard_map/ppermute | solution.py:55
  29.5 0.1 collective-permute-start.16
  29.6 0.8 %collective-permute-done.12.other_core = bf16[144,128]{1,0:T(8,128)(2,1)S(1)} collective-permute-done((bf16[144,128]{1,0:T(8,128)(2,1)S(1)}, bf16[144,128]{1,0:T(8,128)(2,1)S(1)}, u32[]{:S(2)}, u32[]{:S(2)}) %collective-permute-start.12) | collective-permute-done | bytes 36896 | tf_op jit(solution)/shard_map/ppermute | solution.py:55
  30.4 0.7 %shard_map.64 = bf16[3,2,48,128]{3,2,1,0:T(8,128)(2,1)} custom-call(bf16[144,128]{1,0:T(8,128)(2,1)S(1)} %bitcast.18, bf16[144,128]{1,0:T(8,128)(2,1)S(1)} %slice.48.own_core, bf16[144,128]{1,0:T(8,128)(2,1)S(1)} %get-tuple-element.48.other, bf16[144,128]{1,0:T(8,128)(2,1)S(1)} %collective-permute-done.12.other_core), custom_call_target="tpu_custom_call" | custom-call | bytes 221184 | tf_op jit(solution)/shard_map/pallas_call | solution.py:69
  31.1 0.3 collective-permute-done.15
  31.4 0.3 collective-permute-start.17
  31.8 0.0 collective-permute-done.16
  31.8 0.9 %collective-permute-done.17 = f16[400,128]{1,0:T(8,128)(2,1)S(1)} collective-permute-done((f16[400,128]{1,0:T(8,128)(2,1)S(1)}, f16[400,128]{1,0:T(8,128)(2,1)S(1)}, u32[]{:S(2)}, u32[]{:S(2)}) %collective-permute-start.17) | collective-permute-done | bytes 102432 | tf_op jit(solution)/shard_map/ppermute | solution.py:55
  32.7 0.9 %shard_map.65 = f32[3,2,128,128]{3,2,1,0:T(8,128)} custom-call(bf16[3,2,128,128]{3,2,1,0:T(8,128)(2,1)S(1)} %get-tuple-element.32.diag_inverse, f32[400,128]{1,0:T(8,128)S(1)} %get-tuple-element.34.mine, f32[400,128]{1,0:T(8,128)S(1)} %convert_element_type.45.far, f32[400,128]{1,0:T(8,128)S(1)} %convert_element_type.46.mine_core, ...), custom_call_target="tpu_custom_call" | custom-call | bytes 1409024 | tf_op jit(solution)/shard_map/pallas_call | solution.py:69
  (16 shorter events, 0.3 us)
Async XLA Ops:
  0.6 5.5 %collective-permute-start.1 = (bf16[3,2,48,128]{3,2,1,0:T(8,128)(2,1)}, bf16[3,2,48,128]{3,2,1,0:T(8,128)(2,1)S(1)}, u32[]{:S(2)}, u32[]{:S(2)}) collective-permute-start(bf16[3,2,48,128]{3,2,1,0:T(8,128)(2,1)} %panels_in), channel_id=1, source_target_pairs={{0,2},{1,3},{2,0},{3,1},{4,6},{5,7},{6,4},{7,5},{8,10},{9,11},{10,... | collective-permute-start | bytes 221192 | tf_op jit(solution)/shard_map/ppermute | solution.py:33
  5.1 2.5 %collective-permute-start = (bf16[2,96,384]{2,1,0:T(8,128)(2,1)S(1)}, bf16[2,96,384]{2,1,0:T(8,128)(2,1)S(1)}, u32[]{:S(2)}, u32[]{:S(2)}) collective-permute-start(bf16[2,96,384]{2,1,0:T(8,128)(2,1)S(1)} %get-tuple-element.18.near), channel_id=1, source_target_pairs={{0,1},{1,0},{2,3},{3,2},{4,5},{5,4},{6,7},{7,6},{8,9},{9,8},{10,11... | collective-permute-start | bytes 442376 | tf_op jit(solution)/shard_map/ppermute | solution.py:55
  6.3 1.3 %collective-permute-start.2 = (bf16[2,48,384]{2,1,0:T(8,128)(2,1)S(1)}, bf16[2,48,384]{2,1,0:T(8,128)(2,1)S(1)}, u32[]{:S(2)}, u32[]{:S(2)}) collective-permute-start(bf16[2,48,384]{2,1,0:T(8,128)(2,1)S(1)} %shard_map.60.block), channel_id=1, source_target_pairs={{0,1},{1,0},{2,3},{3,2},{4,5},{5,4},{6,7},{7,6},{8,9},{9,8},{10,11... | collective-permute-start | bytes 221192 | tf_op jit(solution)/shard_map/ppermute | solution.py:55
  7.7 5.2 %collective-permute-start.3 = (bf16[2,96,384]{2,1,0:T(8,128)(2,1)S(1)}, bf16[2,96,384]{2,1,0:T(8,128)(2,1)S(1)}, u32[]{:S(2)}, u32[]{:S(2)}) collective-permute-start(bf16[2,96,384]{2,1,0:T(8,128)(2,1)S(1)} %get-tuple-element.21), channel_id=1, source_target_pairs={{0,2},{1,9},{2,0},{3,11},{4,6},{5,13},{6,4},{7,15},{8,10},{9,1},{1... | collective-permute-start | bytes 442376 | tf_op jit(solution)/shard_map/ppermute | solution.py:33
  9.8 5.2 %collective-permute-start.5 = (bf16[2,96,384]{2,1,0:T(8,128)(2,1)S(1)}, bf16[2,96,384]{2,1,0:T(8,128)(2,1)S(1)}, u32[]{:S(2)}, u32[]{:S(2)}) collective-permute-start(bf16[2,96,384]{2,1,0:T(8,128)(2,1)S(1)} %get-tuple-element.22), channel_id=1, source_target_pairs={{0,2},{1,5},{2,0},{3,7},{4,6},{5,1},{6,4},{7,3},{8,10},{9,13},{10,... | collective-permute-start | bytes 442376 | tf_op jit(solution)/shard_map/ppermute | solution.py:33
  9.8 7.2 %collective-permute-start.7 = (bf16[2,96,384]{2,1,0:T(8,128)(2,1)S(1)}, bf16[2,96,384]{2,1,0:T(8,128)(2,1)S(1)}, u32[]{:S(2)}, u32[]{:S(2)}) collective-permute-start(bf16[2,96,384]{2,1,0:T(8,128)(2,1)S(1)} %get-tuple-element.23.block_0), channel_id=1, source_target_pairs={{0,2},{1,13},{2,0},{3,15},{4,6},{5,9},{6,4},{7,11},{8,10},{9,5},{1... | collective-permute-start | bytes 442376 | tf_op jit(solution)/shard_map/ppermute | solution.py:33
  12.9 4.2 %collective-permute-start.4 = (bf16[2,96,384]{2,1,0:T(8,128)(2,1)S(1)}, bf16[2,96,384]{2,1,0:T(8,128)(2,1)S(1)}, u32[]{:S(2)}, u32[]{:S(2)}) collective-permute-start(bf16[2,96,384]{2,1,0:T(8,128)(2,1)S(1)} %collective-permute-done.3.block_1), channel_id=1, source_target_pairs={{0,1},{1,0},{2,3},{3,2},{4,5},{5,4},{6,7},{7,6},{8,9},{9,8},{10,11... | collective-permute-start | bytes 442376 | tf_op jit(solution)/shard_map/ppermute | solution.py:55
  15.0 2.1 %collective-permute-start.6 = (bf16[2,96,384]{2,1,0:T(8,128)(2,1)S(1)}, bf16[2,96,384]{2,1,0:T(8,128)(2,1)S(1)}, u32[]{:S(2)}, u32[]{:S(2)}) collective-permute-start(bf16[2,96,384]{2,1,0:T(8,128)(2,1)S(1)} %collective-permute-done.5.block_2), channel_id=1, source_target_pairs={{0,1},{1,0},{2,3},{3,2},{4,5},{5,4},{6,7},{7,6},{8,9},{9,8},{10,11... | collective-permute-start | bytes 442376 | tf_op jit(solution)/shard_map/ppermute | solution.py:55
  15.4 1.3 %collective-permute-start.8 = (bf16[3,2,48,128]{3,2,1,0:T(8,128)(2,1)S(1)}, bf16[3,2,48,128]{3,2,1,0:T(8,128)(2,1)S(1)}, u32[]{:S(2)}, u32[]{:S(2)}) collective-permute-start(bf16[3,2,48,128]{3,2,1,0:T(8,128)(2,1)S(1)} %get-tuple-element.28.panels), channel_id=1, source_target_pairs={{0,1},{1,0},{2,3},{3,2},{4,5},{5,4},{6,7},{7,6},{8,9},{9,8},{10,11... | collective-permute-start | bytes 221192 | tf_op jit(solution)/shard_map/ppermute | solution.py:55
  15.5 1.4 %collective-permute-start.9 = (bf16[3,2,48,128]{3,2,1,0:T(8,128)(2,1)S(1)}, bf16[3,2,48,128]{3,2,1,0:T(8,128)(2,1)S(1)}, u32[]{:S(2)}, u32[]{:S(2)}) collective-permute-start(bf16[3,2,48,128]{3,2,1,0:T(8,128)(2,1)S(1)} %collective-permute-done.1.panels_far), channel_id=1, source_target_pairs={{0,1},{1,0},{2,3},{3,2},{4,5},{5,4},{6,7},{7,6},{8,9},{9,8},{10,11... | collective-permute-start | bytes 221192 | tf_op jit(solution)/shard_map/ppermute | solution.py:55
  18.1 3.2 %collective-permute-start.10 = (bf16[448,128]{1,0:T(8,128)(2,1)S(1)}, bf16[448,128]{1,0:T(8,128)(2,1)S(1)}, u32[]{:S(2)}, u32[]{:S(2)}) collective-permute-start(bf16[448,128]{1,0:T(8,128)(2,1)S(1)} %get-tuple-element.30), channel_id=1, source_target_pairs={{0,1},{1,0},{2,3},{3,2},{4,5},{5,4},{6,7},{7,6},{8,9},{9,8},{10,11... | collective-permute-start | bytes 344072 | tf_op jit(solution)/shard_map/ppermute | solution.py:55
  19.2 4.7 %collective-permute-start.13 = (f16[400,128]{1,0:T(8,128)(2,1)S(1)}, f16[400,128]{1,0:T(8,128)(2,1)S(1)}, u32[]{:S(2)}, u32[]{:S(2)}) collective-permute-start(f16[400,128]{1,0:T(8,128)(2,1)S(1)} %get-tuple-element.39), channel_id=1, source_target_pairs={{0,2},{1,5},{2,0},{3,7},{4,6},{5,1},{6,4},{7,3},{8,10},{9,13},{10,... | collective-permute-start | bytes 307208 | tf_op jit(solution)/shard_map/ppermute | solution.py:33
  20.8 4.7 %collective-permute-start.14 = (f16[400,128]{1,0:T(8,128)(2,1)S(1)}, f16[400,128]{1,0:T(8,128)(2,1)S(1)}, u32[]{:S(2)}, u32[]{:S(2)}) collective-permute-start(f16[400,128]{1,0:T(8,128)(2,1)S(1)} %get-tuple-element.39), channel_id=1, source_target_pairs={{0,2},{1,9},{2,0},{3,11},{4,6},{5,13},{6,4},{7,15},{8,10},{9,1},{1... | collective-permute-start | bytes 307208 | tf_op jit(solution)/shard_map/ppermute | solution.py:33
  21.4 5.1 %collective-permute-start.11 = (f16[400,128]{1,0:T(8,128)(2,1)S(1)}, f16[400,128]{1,0:T(8,128)(2,1)S(1)}, u32[]{:S(2)}, u32[]{:S(2)}) collective-permute-start(f16[400,128]{1,0:T(8,128)(2,1)S(1)} %maximum_select_fusion), channel_id=1, source_target_pairs={{0,2},{1,13},{2,0},{3,15},{4,6},{5,9},{6,4},{7,11},{8,10},{9,5},{1... | collective-permute-start | bytes 307208 | tf_op jit(solution)/shard_map/ppermute | solution.py:33
  26.7 4.7 %collective-permute-start.15 = (f16[400,128]{1,0:T(8,128)(2,1)S(1)}, f16[400,128]{1,0:T(8,128)(2,1)S(1)}, u32[]{:S(2)}, u32[]{:S(2)}) collective-permute-start(f16[400,128]{1,0:T(8,128)(2,1)S(1)} %get-tuple-element.35), channel_id=1, source_target_pairs={{0,4},{1,3},{2,6},{3,1},{4,0},{5,7},{6,2},{7,5},{8,12},{9,11},{10,... | collective-permute-start | bytes 307208 | tf_op jit(solution)/shard_map/ppermute | solution.py:33
  27.9 2.5 %collective-permute-start.12 = (bf16[144,128]{1,0:T(8,128)(2,1)S(1)}, bf16[144,128]{1,0:T(8,128)(2,1)S(1)}, u32[]{:S(2)}, u32[]{:S(2)}) collective-permute-start(bf16[144,128]{1,0:T(8,128)(2,1)S(1)} %get-tuple-element.47), channel_id=1, source_target_pairs={{0,1},{1,0},{2,3},{3,2},{4,5},{5,4},{6,7},{7,6},{8,9},{9,8},{10,11... | collective-permute-start | bytes 110600 | tf_op jit(solution)/shard_map/ppermute | solution.py:55
  29.5 2.2 %collective-permute-start.16 = (f16[400,128]{1,0:T(8,128)(2,1)S(1)}, f16[400,128]{1,0:T(8,128)(2,1)S(1)}, u32[]{:S(2)}, u32[]{:S(2)}) collective-permute-start(f16[400,128]{1,0:T(8,128)(2,1)S(1)} %get-tuple-element.35), channel_id=1, source_target_pairs={{0,1},{1,0},{2,3},{3,2},{4,5},{5,4},{6,7},{7,6},{8,9},{9,8},{10,11... | collective-permute-start | bytes 307208 | tf_op jit(solution)/shard_map/ppermute | solution.py:55
  31.4 1.3 %collective-permute-start.17 = (f16[400,128]{1,0:T(8,128)(2,1)S(1)}, f16[400,128]{1,0:T(8,128)(2,1)S(1)}, u32[]{:S(2)}, u32[]{:S(2)}) collective-permute-start(f16[400,128]{1,0:T(8,128)(2,1)S(1)} %collective-permute-done.15), channel_id=1, source_target_pairs={{0,1},{1,0},{2,3},{3,2},{4,5},{5,4},{6,7},{7,6},{8,9},{9,8},{10,11... | collective-permute-start | bytes 307208 | tf_op jit(solution)/shard_map/ppermute | solution.py:55

commit v10 on v9

--- a/solution.py
+++ b/solution.py
@@ -11,7 +11,7 @@
 
 AXES = ("prow", "pcol")
 MASKS = (4, 2, 6)
-MASKS_SUM = (2, 4, 6)
+MASKS_SUM = (6, 2, 4)
 STEP, LEVELS, LEVEL_ROWS = 16, 5, 16
 VMEM = pl.BlockSpec(memory_space=pltpu.VMEM)
 HBM = pl.BlockSpec(memory_space=pltpu.HBM)

time: 33.8 us -> 33.8 us (level)
  starting transfers between devices: 18.1 us -> 16.7 us
  waiting for transfers between devices: 9.8 us -> 11.2 us
    ppermute x10, starting transfers between devices: 6.19 us -> 4.81 us  [swap_core(): return lax.ppermute(value, 'pcol', [(0, 1), (1, 0)])]
    ppermute x8, waiting for transfers between devices: 5.93 us -> 6.99 us  [swap(): return lax.ppermute(value, AXES, pairs)]
where the time goes in v10:
time: 33.8 us; the launch traced here: 33.6 us
  starting transfers between devices  16.7 us (49%)
  waiting for transfers between devices  11.2 us (33%)
  Pallas kernels  4.45 us (13%)
  between operations  0.8 us (2%)
  other arithmetic  0.45 us (1%)
    ppermute x8, starting transfers between devices, swap(): return lax.ppermute(value, AXES, pairs)  11.9 us
    ppermute x8, waiting for transfers between devices, swap(): return lax.ppermute(value, AXES, pairs)  6.99 us
    ppermute x10, starting transfers between devices, swap_core(): return lax.ppermute(value, 'pcol', [(0, 1), (1, 0)])  4.81 us
    pallas_call x7, Pallas kernels, call(): pl.pallas_call(kernel, out_shape=shapes, in_specs=[space] * len(operands)...  4.45 us
    ppermute x10, waiting for transfers between devices, swap_core(): return lax.ppermute(value, 'pcol', [(0, 1), (1, 0)])  4.2 us
  transfers between devices with their start and end apart: 18, of which 11 were waited for; matrix products, arithmetic and copies ran while one was open for 1% of the time, Pallas kernels for 7%

profile of v10, /device:TPU:0, one launch (start us, length us, event | category | flops | bytes accessed | tf_op | source)
XLA Modules:
  0.0 33.6 jit_solution(1017378803420811796)
XLA Ops:
  0.6 3.0 %collective-permute-start.1 = (bf16[3,2,48,128]{3,2,1,0:T(8,128)(2,1)}, bf16[3,2,48,128]{3,2,1,0:T(8,128)(2,1)S(1)}, u32[]{:S(2)}, u32[]{:S(2)}) collective-permute-start(bf16[3,2,48,128]{3,2,1,0:T(8,128)(2,1)} %panels_in), channel_id=1, source_target_pairs={{0,2},{1,3},{2,0},{3,1},{4,6},{5,7},{6,4},{7,5},{8,10},{9,11},{10,... | collective-permute-start | bytes 221192 | tf_op jit(solution)/shard_map/ppermute | solution.py:33
  3.6 1.5 %shard_map.59 = (bf16[2,96,384]{2,1,0:T(8,128)(2,1)S(1)}, bf16[3,2,48,128]{3,2,1,0:T(8,128)(2,1)S(1)}, bf16[3,2,128,128]{3,2,1,0:T(8,128)(2,1)S(1)}, f32[2,96,12...) custom-call(bf16[2,8,1,48,96]{4,3,2,1,0:T(8,128)(2,1)} %matrix_in.1, ...), custom_call_target="tpu_custom_call" | custom-call | bytes 12582912 | tf_op jit(solution)/shard_map/pallas_call | solution.py:69
  5.1 0.1 collective-permute-start
  5.2 1.0 %collective-permute-done.1.panels_far = bf16[3,2,48,128]{3,2,1,0:T(8,128)(2,1)S(1)} collective-permute-done((bf16[3,2,48,128]{3,2,1,0:T(8,128)(2,1)}, bf16[3,2,48,128]{3,2,1,0:T(8,128)(2,1)S(1)}, u32[]{:S(2)}, u32[]{:S(2)}) %collective-permute-start.1) | collective-permute-done | bytes 73760 | tf_op jit(solution)/shard_map/ppermute | solution.py:33
  6.2 0.1 shard_map.60.block
  6.3 0.1 collective-permute-start.2
  6.4 1.3 %collective-permute-done.2.block_core = bf16[2,48,384]{2,1,0:T(8,128)(2,1)S(1)} collective-permute-done((bf16[2,48,384]{2,1,0:T(8,128)(2,1)S(1)}, bf16[2,48,384]{2,1,0:T(8,128)(2,1)S(1)}, u32[]{:S(2)}, u32[]{:S(2)}) %collective-permute-start.2) | collective-permute-done | bytes 73760 | tf_op jit(solution)/shard_map/ppermute | solution.py:55
  7.6 0.0 collective-permute-done.near_core
  7.7 2.1 %collective-permute-start.3 = (bf16[2,96,384]{2,1,0:T(8,128)(2,1)S(1)}, bf16[2,96,384]{2,1,0:T(8,128)(2,1)S(1)}, u32[]{:S(2)}, u32[]{:S(2)}) collective-permute-start(bf16[2,96,384]{2,1,0:T(8,128)(2,1)S(1)} %get-tuple-element.21), channel_id=1, source_target_pairs={{0,2},{1,9},{2,0},{3,11},{4,6},{5,13},{6,4},{7,15},{8,10},{9,1},{1... | collective-permute-start | bytes 442376 | tf_op jit(solution)/shard_map/ppermute | solution.py:33
  9.8 0.1 collective-permute-start.5
  9.8 1.9 %collective-permute-start.7 = (bf16[2,96,384]{2,1,0:T(8,128)(2,1)S(1)}, bf16[2,96,384]{2,1,0:T(8,128)(2,1)S(1)}, u32[]{:S(2)}, u32[]{:S(2)}) collective-permute-start(bf16[2,96,384]{2,1,0:T(8,128)(2,1)S(1)} %get-tuple-element.23.block_0), channel_id=1, source_target_pairs={{0,2},{1,13},{2,0},{3,15},{4,6},{5,9},{6,4},{7,11},{8,10},{9,5},{1... | collective-permute-start | bytes 442376 | tf_op jit(solution)/shard_map/ppermute | solution.py:33
  11.8 1.1 %collective-permute-done.3.block_1 = bf16[2,96,384]{2,1,0:T(8,128)(2,1)S(1)} collective-permute-done((bf16[2,96,384]{2,1,0:T(8,128)(2,1)S(1)}, bf16[2,96,384]{2,1,0:T(8,128)(2,1)S(1)}, u32[]{:S(2)}, u32[]{:S(2)}) %collective-permute-start.3) | collective-permute-done | bytes 147488 | tf_op jit(solution)/shard_map/ppermute | solution.py:33
  12.9 2.1 %collective-permute-start.4 = (bf16[2,96,384]{2,1,0:T(8,128)(2,1)S(1)}, bf16[2,96,384]{2,1,0:T(8,128)(2,1)S(1)}, u32[]{:S(2)}, u32[]{:S(2)}) collective-permute-start(bf16[2,96,384]{2,1,0:T(8,128)(2,1)S(1)} %collective-permute-done.3.block_1), channel_id=1, source_target_pairs={{0,1},{1,0},{2,3},{3,2},{4,5},{5,4},{6,7},{7,6},{8,9},{9,8},{10,11... | collective-permute-start | bytes 442376 | tf_op jit(solution)/shard_map/ppermute | solution.py:55
  15.0 0.0 collective-permute-done.5.block_2
  15.0 0.5 %collective-permute-start.6 = (bf16[2,96,384]{2,1,0:T(8,128)(2,1)S(1)}, bf16[2,96,384]{2,1,0:T(8,128)(2,1)S(1)}, u32[]{:S(2)}, u32[]{:S(2)}) collective-permute-start(bf16[2,96,384]{2,1,0:T(8,128)(2,1)S(1)} %collective-permute-done.5.block_2), channel_id=1, source_target_pairs={{0,1},{1,0},{2,3},{3,2},{4,5},{5,4},{6,7},{7,6},{8,9},{9,8},{10,11... | collective-permute-start | bytes 442376 | tf_op jit(solution)/shard_map/ppermute | solution.py:55
  15.4 0.0 collective-permute-start.8
  15.5 0.5 %collective-permute-start.9 = (bf16[3,2,48,128]{3,2,1,0:T(8,128)(2,1)S(1)}, bf16[3,2,48,128]{3,2,1,0:T(8,128)(2,1)S(1)}, u32[]{:S(2)}, u32[]{:S(2)}) collective-permute-start(bf16[3,2,48,128]{3,2,1,0:T(8,128)(2,1)S(1)} %collective-permute-done.1.panels_far), channel_id=1, source_target_pairs={{0,1},{1,0},{2,3},{3,2},{4,5},{5,4},{6,7},{7,6},{8,9},{9,8},{10,11... | collective-permute-start | bytes 221192 | tf_op jit(solution)/shard_map/ppermute | solution.py:55
  16.0 0.7 %collective-permute-done.8.panels_core = bf16[3,2,48,128]{3,2,1,0:T(8,128)(2,1)S(1)} collective-permute-done((bf16[3,2,48,128]{3,2,1,0:T(8,128)(2,1)S(1)}, bf16[3,2,48,128]{3,2,1,0:T(8,128)(2,1)S(1)}, u32[]{:S(2)}, u32[]{:S(2)}) %collective-permute-start.8) | collective-permute-done | bytes 73760 | tf_op jit(solution)/shard_map/ppermute | solution.py:55
  16.7 0.2 collective-permute-done.9.panels_far_core
  16.9 0.2 shard_map.62.refs_1_
  17.1 0.0 collective-permute-done.7.block_3
  17.1 0.0 collective-permute-done.4.far_0
  17.1 0.0 collective-permute-done.6.far_1
  17.1 1.0 %shard_map.63 = (bf16[3,48,128]{2,1,0:T(8,128)(2,1)S(1)}, bf16[448,128]{1,0:T(8,128)(2,1)S(1)}, f32[400,128]{1,0:T(8,128)S(1)}) custom-call(bf16[2,96,384]{2,1,0:T(8,128)(2,1)S(1)} %get-tuple-element.18.near, bf16[2,96,384]{2,1,0:T(8,128)(2,1)S(1)} %collective-permute-done.near_core, bf16[2,96,384]{2,1,0:T(8,128)(2,1)S(1)} %collective-permute-done.4.far_0, ...), custom_call_target="tpu_custom_call" | custom-call | bytes 1929216 | tf_op jit(solution)/shard_map/pallas_call | solution.py:69
  18.1 0.9 %collective-permute-start.10 = (bf16[448,128]{1,0:T(8,128)(2,1)S(1)}, bf16[448,128]{1,0:T(8,128)(2,1)S(1)}, u32[]{:S(2)}, u32[]{:S(2)}) collective-permute-start(bf16[448,128]{1,0:T(8,128)(2,1)S(1)} %get-tuple-element.30), channel_id=1, source_target_pairs={{0,1},{1,0},{2,3},{3,2},{4,5},{5,4},{6,7},{7,6},{8,9},{9,8},{10,11... | collective-permute-start | bytes 344072 | tf_op jit(solution)/shard_map/ppermute | solution.py:55
  19.1 0.1 fusion.9
  19.2 1.6 %collective-permute-start.13 = (f16[400,128]{1,0:T(8,128)(2,1)S(1)}, f16[400,128]{1,0:T(8,128)(2,1)S(1)}, u32[]{:S(2)}, u32[]{:S(2)}) collective-permute-start(f16[400,128]{1,0:T(8,128)(2,1)S(1)} %get-tuple-element.39), channel_id=1, source_target_pairs={{0,2},{1,13},{2,0},{3,15},{4,6},{5,9},{6,4},{7,11},{8,10},{9,5},{1... | collective-permute-start | bytes 307208 | tf_op jit(solution)/shard_map/ppermute | solution.py:33
  20.8 0.5 %collective-permute-start.14 = (f16[400,128]{1,0:T(8,128)(2,1)S(1)}, f16[400,128]{1,0:T(8,128)(2,1)S(1)}, u32[]{:S(2)}, u32[]{:S(2)}) collective-permute-start(f16[400,128]{1,0:T(8,128)(2,1)S(1)} %get-tuple-element.39), channel_id=1, source_target_pairs={{0,2},{1,5},{2,0},{3,7},{4,6},{5,1},{6,4},{7,3},{8,10},{9,13},{10,... | collective-permute-start | bytes 307208 | tf_op jit(solution)/shard_map/ppermute | solution.py:33
  21.3 0.0 collective-permute-done.10
  21.4 1.6 %collective-permute-start.11 = (f16[400,128]{1,0:T(8,128)(2,1)S(1)}, f16[400,128]{1,0:T(8,128)(2,1)S(1)}, u32[]{:S(2)}, u32[]{:S(2)}) collective-permute-start(f16[400,128]{1,0:T(8,128)(2,1)S(1)} %maximum_select_fusion), channel_id=1, source_target_pairs={{0,2},{1,9},{2,0},{3,11},{4,6},{5,13},{6,4},{7,15},{8,10},{9,1},{1... | collective-permute-start | bytes 307208 | tf_op jit(solution)/shard_map/ppermute | solution.py:33
  22.9 1.0 %collective-permute-done.13 = f16[400,128]{1,0:T(8,128)(2,1)S(1)} collective-permute-done((f16[400,128]{1,0:T(8,128)(2,1)S(1)}, f16[400,128]{1,0:T(8,128)(2,1)S(1)}, u32[]{:S(2)}, u32[]{:S(2)}) %collective-permute-start.13) | collective-permute-done | bytes 102432 | tf_op jit(solution)/shard_map/ppermute | solution.py:33
  23.9 1.5 %collective-permute-done.14 = f16[400,128]{1,0:T(8,128)(2,1)S(1)} collective-permute-done((f16[400,128]{1,0:T(8,128)(2,1)S(1)}, f16[400,128]{1,0:T(8,128)(2,1)S(1)}, u32[]{:S(2)}, u32[]{:S(2)}) %collective-permute-start.14) | collective-permute-done | bytes 102432 | tf_op jit(solution)/shard_map/ppermute | solution.py:33
  25.4 1.1 %collective-permute-done.11 = f16[400,128]{1,0:T(8,128)(2,1)S(1)} collective-permute-done((f16[400,128]{1,0:T(8,128)(2,1)S(1)}, f16[400,128]{1,0:T(8,128)(2,1)S(1)}, u32[]{:S(2)}, u32[]{:S(2)}) %collective-permute-start.11) | collective-permute-done | bytes 102432 | tf_op jit(solution)/shard_map/ppermute | solution.py:33
  26.6 0.1 fusion.8
  26.7 1.2 %collective-permute-start.15 = (f16[400,128]{1,0:T(8,128)(2,1)S(1)}, f16[400,128]{1,0:T(8,128)(2,1)S(1)}, u32[]{:S(2)}, u32[]{:S(2)}) collective-permute-start(f16[400,128]{1,0:T(8,128)(2,1)S(1)} %get-tuple-element.35), channel_id=1, source_target_pairs={{0,4},{1,3},{2,6},{3,1},{4,0},{5,7},{6,2},{7,5},{8,12},{9,11},{10,... | collective-permute-start | bytes 307208 | tf_op jit(solution)/shard_map/ppermute | solution.py:33
  27.9 0.6 %collective-permute-start.12 = (bf16[144,128]{1,0:T(8,128)(2,1)S(1)}, bf16[144,128]{1,0:T(8,128)(2,1)S(1)}, u32[]{:S(2)}, u32[]{:S(2)}) collective-permute-start(bf16[144,128]{1,0:T(8,128)(2,1)S(1)} %get-tuple-element.47), channel_id=1, source_target_pairs={{0,1},{1,0},{2,3},{3,2},{4,5},{5,4},{6,7},{7,6},{8,9},{9,8},{10,11... | collective-permute-start | bytes 110600 | tf_op jit(solution)/shard_map/ppermute | solution.py:55
  28.5 0.1 collective-permute-start.16
  28.6 0.8 %collective-permute-done.12.other_core = bf16[144,128]{1,0:T(8,128)(2,1)S(1)} collective-permute-done((bf16[144,128]{1,0:T(8,128)(2,1)S(1)}, bf16[144,128]{1,0:T(8,128)(2,1)S(1)}, u32[]{:S(2)}, u32[]{:S(2)}) %collective-permute-start.12) | collective-permute-done | bytes 36896 | tf_op jit(solution)/shard_map/ppermute | solution.py:55
  29.3 0.7 %shard_map.64 = bf16[3,2,48,128]{3,2,1,0:T(8,128)(2,1)} custom-call(bf16[144,128]{1,0:T(8,128)(2,1)S(1)} %bitcast.18, bf16[144,128]{1,0:T(8,128)(2,1)S(1)} %slice.48.own_core, bf16[144,128]{1,0:T(8,128)(2,1)S(1)} %get-tuple-element.48.other, bf16[144,128]{1,0:T(8,128)(2,1)S(1)} %collective-permute-done.12.other_core), custom_call_target="tpu_custom_call" | custom-call | bytes 221184 | tf_op jit(solution)/shard_map/pallas_call | solution.py:69
  30.1 1.3 %collective-permute-done.15 = f16[400,128]{1,0:T(8,128)(2,1)S(1)} collective-permute-done((f16[400,128]{1,0:T(8,128)(2,1)S(1)}, f16[400,128]{1,0:T(8,128)(2,1)S(1)}, u32[]{:S(2)}, u32[]{:S(2)}) %collective-permute-start.15) | collective-permute-done | bytes 102432 | tf_op jit(solution)/shard_map/ppermute | solution.py:33
  31.4 0.0 collective-permute-start.17
  31.4 0.0 collective-permute-done.16
  31.5 1.2 %collective-permute-done.17 = f16[400,128]{1,0:T(8,128)(2,1)S(1)} collective-permute-done((f16[400,128]{1,0:T(8,128)(2,1)S(1)}, f16[400,128]{1,0:T(8,128)(2,1)S(1)}, u32[]{:S(2)}, u32[]{:S(2)}) %collective-permute-start.17) | collective-permute-done | bytes 102432 | tf_op jit(solution)/shard_map/ppermute | solution.py:55
  32.7 0.9 %shard_map.65 = f32[3,2,128,128]{3,2,1,0:T(8,128)} custom-call(bf16[3,2,128,128]{3,2,1,0:T(8,128)(2,1)S(1)} %get-tuple-element.32.diag_inverse, f32[400,128]{1,0:T(8,128)S(1)} %get-tuple-element.34.mine, f32[400,128]{1,0:T(8,128)S(1)} %convert_element_type.45.far, f32[400,128]{1,0:T(8,128)S(1)} %convert_element_type.46.mine_core, ...), custom_call_target="tpu_custom_call" | custom-call | bytes 1409024 | tf_op jit(solution)/shard_map/pallas_call | solution.py:69
  (16 shorter events, 0.3 us)
Async XLA Ops:
  0.6 5.5 %collective-permute-start.1 = (bf16[3,2,48,128]{3,2,1,0:T(8,128)(2,1)}, bf16[3,2,48,128]{3,2,1,0:T(8,128)(2,1)S(1)}, u32[]{:S(2)}, u32[]{:S(2)}) collective-permute-start(bf16[3,2,48,128]{3,2,1,0:T(8,128)(2,1)} %panels_in), channel_id=1, source_target_pairs={{0,2},{1,3},{2,0},{3,1},{4,6},{5,7},{6,4},{7,5},{8,10},{9,11},{10,... | collective-permute-start | bytes 221192 | tf_op jit(solution)/shard_map/ppermute | solution.py:33
  5.1 2.5 %collective-permute-start = (bf16[2,96,384]{2,1,0:T(8,128)(2,1)S(1)}, bf16[2,96,384]{2,1,0:T(8,128)(2,1)S(1)}, u32[]{:S(2)}, u32[]{:S(2)}) collective-permute-start(bf16[2,96,384]{2,1,0:T(8,128)(2,1)S(1)} %get-tuple-element.18.near), channel_id=1, source_target_pairs={{0,1},{1,0},{2,3},{3,2},{4,5},{5,4},{6,7},{7,6},{8,9},{9,8},{10,11... | collective-permute-start | bytes 442376 | tf_op jit(solution)/shard_map/ppermute | solution.py:55
  6.3 1.3 %collective-permute-start.2 = (bf16[2,48,384]{2,1,0:T(8,128)(2,1)S(1)}, bf16[2,48,384]{2,1,0:T(8,128)(2,1)S(1)}, u32[]{:S(2)}, u32[]{:S(2)}) collective-permute-start(bf16[2,48,384]{2,1,0:T(8,128)(2,1)S(1)} %shard_map.60.block), channel_id=1, source_target_pairs={{0,1},{1,0},{2,3},{3,2},{4,5},{5,4},{6,7},{7,6},{8,9},{9,8},{10,11... | collective-permute-start | bytes 221192 | tf_op jit(solution)/shard_map/ppermute | solution.py:55
  7.7 5.2 %collective-permute-start.3 = (bf16[2,96,384]{2,1,0:T(8,128)(2,1)S(1)}, bf16[2,96,384]{2,1,0:T(8,128)(2,1)S(1)}, u32[]{:S(2)}, u32[]{:S(2)}) collective-permute-start(bf16[2,96,384]{2,1,0:T(8,128)(2,1)S(1)} %get-tuple-element.21), channel_id=1, source_target_pairs={{0,2},{1,9},{2,0},{3,11},{4,6},{5,13},{6,4},{7,15},{8,10},{9,1},{1... | collective-permute-start | bytes 442376 | tf_op jit(solution)/shard_map/ppermute | solution.py:33
  9.8 5.2 %collective-permute-start.5 = (bf16[2,96,384]{2,1,0:T(8,128)(2,1)S(1)}, bf16[2,96,384]{2,1,0:T(8,128)(2,1)S(1)}, u32[]{:S(2)}, u32[]{:S(2)}) collective-permute-start(bf16[2,96,384]{2,1,0:T(8,128)(2,1)S(1)} %get-tuple-element.22), channel_id=1, source_target_pairs={{0,2},{1,5},{2,0},{3,7},{4,6},{5,1},{6,4},{7,3},{8,10},{9,13},{10,... | collective-permute-start | bytes 442376 | tf_op jit(solution)/shard_map/ppermute | solution.py:33
  9.8 7.2 %collective-permute-start.7 = (bf16[2,96,384]{2,1,0:T(8,128)(2,1)S(1)}, bf16[2,96,384]{2,1,0:T(8,128)(2,1)S(1)}, u32[]{:S(2)}, u32[]{:S(2)}) collective-permute-start(bf16[2,96,384]{2,1,0:T(8,128)(2,1)S(1)} %get-tuple-element.23.block_0), channel_id=1, source_target_pairs={{0,2},{1,13},{2,0},{3,15},{4,6},{5,9},{6,4},{7,11},{8,10},{9,5},{1... | collective-permute-start | bytes 442376 | tf_op jit(solution)/shard_map/ppermute | solution.py:33
  12.9 4.2 %collective-permute-start.4 = (bf16[2,96,384]{2,1,0:T(8,128)(2,1)S(1)}, bf16[2,96,384]{2,1,0:T(8,128)(2,1)S(1)}, u32[]{:S(2)}, u32[]{:S(2)}) collective-permute-start(bf16[2,96,384]{2,1,0:T(8,128)(2,1)S(1)} %collective-permute-done.3.block_1), channel_id=1, source_target_pairs={{0,1},{1,0},{2,3},{3,2},{4,5},{5,4},{6,7},{7,6},{8,9},{9,8},{10,11... | collective-permute-start | bytes 442376 | tf_op jit(solution)/shard_map/ppermute | solution.py:55
  15.0 2.1 %collective-permute-start.6 = (bf16[2,96,384]{2,1,0:T(8,128)(2,1)S(1)}, bf16[2,96,384]{2,1,0:T(8,128)(2,1)S(1)}, u32[]{:S(2)}, u32[]{:S(2)}) collective-permute-start(bf16[2,96,384]{2,1,0:T(8,128)(2,1)S(1)} %collective-permute-done.5.block_2), channel_id=1, source_target_pairs={{0,1},{1,0},{2,3},{3,2},{4,5},{5,4},{6,7},{7,6},{8,9},{9,8},{10,11... | collective-permute-start | bytes 442376 | tf_op jit(solution)/shard_map/ppermute | solution.py:55
  15.4 1.3 %collective-permute-start.8 = (bf16[3,2,48,128]{3,2,1,0:T(8,128)(2,1)S(1)}, bf16[3,2,48,128]{3,2,1,0:T(8,128)(2,1)S(1)}, u32[]{:S(2)}, u32[]{:S(2)}) collective-permute-start(bf16[3,2,48,128]{3,2,1,0:T(8,128)(2,1)S(1)} %get-tuple-element.28.panels), channel_id=1, source_target_pairs={{0,1},{1,0},{2,3},{3,2},{4,5},{5,4},{6,7},{7,6},{8,9},{9,8},{10,11... | collective-permute-start | bytes 221192 | tf_op jit(solution)/shard_map/ppermute | solution.py:55
  15.5 1.4 %collective-permute-start.9 = (bf16[3,2,48,128]{3,2,1,0:T(8,128)(2,1)S(1)}, bf16[3,2,48,128]{3,2,1,0:T(8,128)(2,1)S(1)}, u32[]{:S(2)}, u32[]{:S(2)}) collective-permute-start(bf16[3,2,48,128]{3,2,1,0:T(8,128)(2,1)S(1)} %collective-permute-done.1.panels_far), channel_id=1, source_target_pairs={{0,1},{1,0},{2,3},{3,2},{4,5},{5,4},{6,7},{7,6},{8,9},{9,8},{10,11... | collective-permute-start | bytes 221192 | tf_op jit(solution)/shard_map/ppermute | solution.py:55
  18.1 3.2 %collective-permute-start.10 = (bf16[448,128]{1,0:T(8,128)(2,1)S(1)}, bf16[448,128]{1,0:T(8,128)(2,1)S(1)}, u32[]{:S(2)}, u32[]{:S(2)}) collective-permute-start(bf16[448,128]{1,0:T(8,128)(2,1)S(1)} %get-tuple-element.30), channel_id=1, source_target_pairs={{0,1},{1,0},{2,3},{3,2},{4,5},{5,4},{6,7},{7,6},{8,9},{9,8},{10,11... | collective-permute-start | bytes 344072 | tf_op jit(solution)/shard_map/ppermute | solution.py:55
  19.2 4.7 %collective-permute-start.13 = (f16[400,128]{1,0:T(8,128)(2,1)S(1)}, f16[400,128]{1,0:T(8,128)(2,1)S(1)}, u32[]{:S(2)}, u32[]{:S(2)}) collective-permute-start(f16[400,128]{1,0:T(8,128)(2,1)S(1)} %get-tuple-element.39), channel_id=1, source_target_pairs={{0,2},{1,13},{2,0},{3,15},{4,6},{5,9},{6,4},{7,11},{8,10},{9,5},{1... | collective-permute-start | bytes 307208 | tf_op jit(solution)/shard_map/ppermute | solution.py:33
  20.8 4.7 %collective-permute-start.14 = (f16[400,128]{1,0:T(8,128)(2,1)S(1)}, f16[400,128]{1,0:T(8,128)(2,1)S(1)}, u32[]{:S(2)}, u32[]{:S(2)}) collective-permute-start(f16[400,128]{1,0:T(8,128)(2,1)S(1)} %get-tuple-element.39), channel_id=1, source_target_pairs={{0,2},{1,5},{2,0},{3,7},{4,6},{5,1},{6,4},{7,3},{8,10},{9,13},{10,... | collective-permute-start | bytes 307208 | tf_op jit(solution)/shard_map/ppermute | solution.py:33
  21.4 5.1 %collective-permute-start.11 = (f16[400,128]{1,0:T(8,128)(2,1)S(1)}, f16[400,128]{1,0:T(8,128)(2,1)S(1)}, u32[]{:S(2)}, u32[]{:S(2)}) collective-permute-start(f16[400,128]{1,0:T(8,128)(2,1)S(1)} %maximum_select_fusion), channel_id=1, source_target_pairs={{0,2},{1,9},{2,0},{3,11},{4,6},{5,13},{6,4},{7,15},{8,10},{9,1},{1... | collective-permute-start | bytes 307208 | tf_op jit(solution)/shard_map/ppermute | solution.py:33
  26.7 4.7 %collective-permute-start.15 = (f16[400,128]{1,0:T(8,128)(2,1)S(1)}, f16[400,128]{1,0:T(8,128)(2,1)S(1)}, u32[]{:S(2)}, u32[]{:S(2)}) collective-permute-start(f16[400,128]{1,0:T(8,128)(2,1)S(1)} %get-tuple-element.35), channel_id=1, source_target_pairs={{0,4},{1,3},{2,6},{3,1},{4,0},{5,7},{6,2},{7,5},{8,12},{9,11},{10,... | collective-permute-start | bytes 307208 | tf_op jit(solution)/shard_map/ppermute | solution.py:33
  27.9 1.5 %collective-permute-start.12 = (bf16[144,128]{1,0:T(8,128)(2,1)S(1)}, bf16[144,128]{1,0:T(8,128)(2,1)S(1)}, u32[]{:S(2)}, u32[]{:S(2)}) collective-permute-start(bf16[144,128]{1,0:T(8,128)(2,1)S(1)} %get-tuple-element.47), channel_id=1, source_target_pairs={{0,1},{1,0},{2,3},{3,2},{4,5},{5,4},{6,7},{7,6},{8,9},{9,8},{10,11... | collective-permute-start | bytes 110600 | tf_op jit(solution)/shard_map/ppermute | solution.py:55
  28.5 3.0 %collective-permute-start.16 = (f16[400,128]{1,0:T(8,128)(2,1)S(1)}, f16[400,128]{1,0:T(8,128)(2,1)S(1)}, u32[]{:S(2)}, u32[]{:S(2)}) collective-permute-start(f16[400,128]{1,0:T(8,128)(2,1)S(1)} %get-tuple-element.35), channel_id=1, source_target_pairs={{0,1},{1,0},{2,3},{3,2},{4,5},{5,4},{6,7},{7,6},{8,9},{9,8},{10,11... | collective-permute-start | bytes 307208 | tf_op jit(solution)/shard_map/ppermute | solution.py:55
  31.4 1.3 %collective-permute-start.17 = (f16[400,128]{1,0:T(8,128)(2,1)S(1)}, f16[400,128]{1,0:T(8,128)(2,1)S(1)}, u32[]{:S(2)}, u32[]{:S(2)}) collective-permute-start(f16[400,128]{1,0:T(8,128)(2,1)S(1)} %collective-permute-done.15), channel_id=1, source_target_pairs={{0,1},{1,0},{2,3},{3,2},{4,5},{5,4},{6,7},{7,6},{8,9},{9,8},{10,11... | collective-permute-start | bytes 307208 | tf_op jit(solution)/shard_map/ppermute | solution.py:55
